TPU v7x, 128 devices: a whole 4x4x4 slice. The times are simulated.
128 devices in a mesh: dp: 16 (over z, y), expert: 8 (over x, core).
Axes of the slice: x: 4, y: 4, z: 4, core: 2. Of those that a mesh axis runs over, the one named last changes fastest.
Arguments:
- tokens: bfloat16 [16384, 1536], P(('dp', 'expert')), may hold values from -6 to 6
- segments: int32 [16384], P(('dp', 'expert')), may hold values from 0 to 2, as said below
- routes: int32 [16384, 8], P(('dp', 'expert')), may hold values from 0 to 15, all different within a row; in each aligned block of 128 rows (0 to 127, 128 to 255, ...) at most 96 rows name the same one
- gain_attn: bfloat16 [1536], P('dp'), may hold values from 0.099609375 to 1.8984375
- w_query: bfloat16 [1536, 1536], P('dp'), may hold values from -0.625 to 0.625
- w_key: bfloat16 [1536, 512], P('dp'), may hold values from -0.625 to 0.625
- w_value: bfloat16 [1536, 512], P('dp'), may hold values from -0.15625 to 0.15625
- w_out: bfloat16 [1536, 1536], P('dp'), may hold values from -6 to 6
- gain_moe: bfloat16 [1536], P('dp'), may hold values from 0.099609375 to 1.8984375
- w_router: bfloat16 [1536, 16], P('dp'), may hold values from -0.078125 to 0.078125
- expert_gate: bfloat16 [16, 1536, 512], P('expert'), may hold values from -0.15625 to 0.15625
- expert_up: bfloat16 [16, 1536, 512], P('expert'), may hold values from -0.15625 to 0.15625
- expert_down: bfloat16 [16, 512, 1536], P('expert'), may hold values from -6 to 6
- out_grad: bfloat16 [16384, 1536], P(('dp', 'expert')), may hold values from -6 to 6
Outputs:
- output: bfloat16 [16384, 1536], P(('dp', 'expert'))
- grad_tokens: float32 [16384, 1536], P(('dp', 'expert'))
- grad_gain_attn: float32 [1536], P('dp')
- grad_query: float32 [1536, 1536], P('dp')
- grad_key: float32 [1536, 512], P('dp')
- grad_value: float32 [1536, 512], P('dp')
- grad_out: float32 [1536, 1536], P('dp')
- grad_gain_moe: float32 [1536], P('dp')
- grad_router: float32 [1536, 16], P('dp')
- grad_gate: float32 [16, 1536, 512], P('expert')
- grad_up: float32 [16, 1536, 512], P('expert')
- grad_down: float32 [16, 512, 1536], P('expert')
Inputs may be any that keep to these rules, and one draw needn't show every extreme that they name: `segments`: within each sequence of 1024 tokens the id starts at 0 and never falls; every id from 0 to 2 occurs in every sequence. `routes`: each row names 8 different experts; among the rows of one device (aligned blocks of 128 rows) no expert is named more than 96 times, and in some block one is named exactly 96 times.
All inputs are finite; a program needn't handle non-finite values.
Results may differ from a plain program's by a relative error of at most 0.025.
Values may be sent and summed in bfloat16 or wider, within the bound.
No kernel may reach another device: no remote copies, remote signals or barrier semaphores. Data moves between devices by JAX's collectives and lax.ppermute only.
A program may use at most 256 MiB of HBM per device.

v0:
```python
import jax
import jax.numpy as jnp
from jax import lax
from jax.experimental import pallas as pl
from jax.experimental.pallas import tpu as pltpu
from jax.sharding import Mesh, PartitionSpec as P

HEADS = 24
KV_HEADS = 8
HEAD_DIM = 64
GROUP = HEADS // KV_HEADS
TOP = 8
EXPERTS = 16

eps = 1e-06
residual_scale = 0.22
score_scale = 0.015625
rope_base = 10000.0
doc_slots = 3
MIB = 1024 * 1024

bf16 = jnp.bfloat16
f32 = jnp.float32


def mm(a, b):
    return lax.dot_general(a, b, (((1,), (0,)), ((), ())), preferred_element_type=f32)


def mm_nt(a, b):
    return lax.dot_general(a, b, (((1,), (1,)), ((), ())), preferred_element_type=f32)


def low_half(value):
    lane = lax.broadcasted_iota(jnp.int32, value.shape, 1)
    return jnp.where(lane < 64, value, jnp.zeros_like(value))


def high_half(value):
    lane = lax.broadcasted_iota(jnp.int32, value.shape, 1)
    return jnp.where(lane >= 64, value, jnp.zeros_like(value))


def quarter(value):
    lane = lax.broadcasted_iota(jnp.int32, value.shape, 1)
    up, down = pltpu.roll(value, 96, 1), pltpu.roll(value, 32, 1)
    return jnp.where(lane % 64 < 32, -up, down)


def visible(chunk, starts):
    keys = 256 * (chunk + 1)
    place = (256 * chunk + lax.broadcasted_iota(jnp.int32, (1, 256), 1)).astype(f32)
    one = jnp.concatenate([starts[0:1], starts[0:1]], axis=1)
    two = jnp.concatenate([starts[1:2], starts[1:2]], axis=1)
    begin = jnp.where(place >= two, two, jnp.where(place >= one, one, jnp.zeros_like(one)))
    at = lax.broadcasted_iota(jnp.int32, (keys, 256), 0).astype(f32)
    return (at <= place) & (at >= begin)


def attend_body(ids, *refs):
    blocks = refs[:8]
    (w, gain, cos_t, sin_t, freq, _, __,
     normed, q01, q2k, val, lse, cos_o, sin_o, starts, mixed, ka, kb, vt) = refs[8:]
    one = jnp.zeros((1, 128), f32)
    two = jnp.zeros((1, 128), f32)
    for b in range(8):
        seg = blocks[b][:, 1536:1664].astype(f32)
        one = one + jnp.sum(jnp.where(seg < 0.5, 1.0, 0.0), axis=0, keepdims=True)
        two = two + jnp.sum(jnp.where(seg < 1.5, 1.0, 0.0), axis=0, keepdims=True)
    starts[...] = jnp.concatenate([one, two, jnp.zeros((6, 128), f32)], axis=0)
    begin_rows = jnp.concatenate([one, two, jnp.zeros((6, 128), f32)], axis=0)
    angles = begin_rows * freq[...]
    cos_b, sin_b = jnp.cos(angles), jnp.sin(angles)
    for b in range(8):
        x = blocks[b][:, 0:1536].astype(f32)
        r = lax.rsqrt(jnp.mean(x * x, axis=1, keepdims=True) + eps)
        at = pl.ds(pl.multiple_of(ids[b] * 128, 128), 128)
        normed[at, :] = (x * r * gain[...]).astype(bf16)
    def project(c, carry):
        at = pl.ds(pl.multiple_of(c * 256, 256), 256)
        u = mm(normed[at, :], w[...])
        place = (lax.broadcasted_iota(jnp.int32, (256, 128), 0) + c * 256).astype(f32)
        in_two, in_one = place >= two, place >= one
        cb = jnp.where(in_two, cos_b[1:2], jnp.where(in_one, cos_b[0:1], 1.0))
        sb = jnp.where(in_two, sin_b[1:2], jnp.where(in_one, sin_b[0:1], 0.0))
        ct, st = cos_t[at, :], sin_t[at, :]
        cc = ct * cb + st * sb
        ss = st * cb - ct * sb
        cos_o[at, :] = cc
        sin_o[at, :] = ss
        a, bq, v = u[:, 0:128], u[:, 128:256], u[:, 256:384]
        a = a * cc + quarter(a) * ss
        bq = bq * cc + quarter(bq) * ss
        v = low_half(v)
        q01[at, :] = a.astype(bf16)
        q2k[at, :] = bq.astype(bf16)
        val[at, :] = v.astype(bf16)
        k = high_half(bq) * score_scale
        kb[at, :] = k.astype(bf16)
        ka[at, :] = pltpu.roll(k, 64, 1).astype(bf16)
        vt[:, at] = v.T.astype(bf16)
        return carry

    lax.fori_loop(0, 4, project, 0)

    for c in range(4):
        at, seen = slice(256 * c, 256 * (c + 1)), slice(0, 256 * (c + 1))
        allowed = visible(c, starts)
        outs = []
        for h in range(3):
            q = q2k[at, :] if h == 2 else q01[at, :]
            kk = kb if h == 1 else ka
            s = mm_nt(kk[seen, :], q)
            s = jnp.where(allowed, s, -1e30)
            top = jnp.max(s, axis=0, keepdims=True)
            p = jnp.exp(s - top)
            total = jnp.sum(p, axis=0, keepdims=True)
            lse[h : h + 1, at] = top + jnp.log(total)
            pb = (p * (1.0 / total)).astype(bf16)
            outs.append(mm(vt[0:64, seen], pb))
        out = jnp.concatenate(outs + [jnp.zeros((64, 256), f32)], axis=0).T.astype(bf16)
        mixed[2 * c] = out[0:128]
        mixed[2 * c + 1] = out[128:256]


def attend_forward(ids, blocks, w, gain, cos_t, sin_t, freq, held):
    vm = pl.BlockSpec(memory_space=pltpu.VMEM)
    shape = jax.ShapeDtypeStruct
    return pl.pallas_call(
        attend_body,
        out_shape=(
            shape((1024, 1536), bf16),
            shape((1024, 128), bf16),
            shape((1024, 128), bf16),
            shape((1024, 128), bf16),
            shape((8, 1024), f32),
            shape((1024, 128), f32),
            shape((1024, 128), f32),
            shape((8, 128), f32),
            shape((8, 128, 256), bf16),
        ),
        in_specs=[pl.BlockSpec(memory_space=pltpu.SMEM)]
        + [vm] * 13
        + [pl.BlockSpec(memory_space=pl.ANY)] * 2,
        out_specs=(vm,) * 9,
        scratch_shapes=[
            pltpu.VMEM((1024, 128), bf16),
            pltpu.VMEM((1024, 128), bf16),
            pltpu.VMEM((128, 1024), bf16),
        ],
        compiler_params=pltpu.CompilerParams(vmem_limit_bytes=56 * MIB),
        cost_estimate=pl.CostEstimate(flops=14_000_000_000, bytes_accessed=12_000_000, transcendentals=3_200_000),
        name="attend_forward",
    )(ids, *blocks, w, gain, cos_t, sin_t, freq, *held)


def attend_back_body(
    here, w, gm, q01, q2k, val, lse, cc, ss, starts, normed, gain,
    dqkv, own, other, grad_gain, ka, kb, vb, kt, do01, do2, dk, dv, d01, dq2,
):
    k = high_half(q2k[...].astype(f32)) * score_scale
    kb[...] = k.astype(bf16)
    k_low = pltpu.roll(k, 64, 1)
    ka[...] = k_low.astype(bf16)
    kt[...] = k_low.T.astype(bf16)
    vb[...] = pltpu.roll(val[...].astype(f32), 64, 1).astype(bf16)
    for b in range(8):
        do01[b * 128 : (b + 1) * 128, :] = gm[b, :, 0:128]
        do2[b * 128 : (b + 1) * 128, :] = gm[b, :, 128:256]
    dk[...] = jnp.zeros_like(dk)
    dv[...] = jnp.zeros_like(dv)

    for c in range(4):
        at, seen = slice(256 * c, 256 * (c + 1)), slice(0, 256 * (c + 1))
        allowed = visible(c, starts)
        qa, qb = q01[at, :], q2k[at, :]
        da, db = do01[at, :], do2[at, :]
        outs = []
        for h in range(3):
            q = qb if h == 2 else qa
            kk = kb if h == 1 else ka
            s = mm_nt(kk[seen, :], q)
            p = jnp.where(allowed, jnp.exp(s - lse[h : h + 1, at]), 0.0)
            d = db if h == 2 else da
            vv = vb if h == 1 else val
            dp = mm_nt(vv[seen, :], d)
            delta = jnp.sum(p * dp, axis=0, keepdims=True)
            ds = (p * (dp - delta)).astype(bf16)
            outs.append(mm(kt[0:64, seen], ds))
            half = high_half if h == 1 else low_half
            dk[seen, :] += mm(ds, half(q))
            dv[seen, :] += mm(p.astype(bf16), half(d))
        out = jnp.concatenate(outs + [jnp.zeros((64, 256), f32)], axis=0).T
        d01[at, :] = out[:, 0:128]
        dq2[at, :] = out[:, 128:256]

    def finish(c, total):
        at = pl.ds(pl.multiple_of(c * 256, 256), 256)
        dkk = dk[at, :]
        dkk = (dkk + pltpu.roll(dkk, 64, 1)) * score_scale
        dvv = dv[at, :]
        dvv = low_half(dvv + pltpu.roll(dvv, 64, 1))
        a = d01[at, :]
        lane = lax.broadcasted_iota(jnp.int32, (256, 128), 1)
        b = jnp.where(lane < 64, dq2[at, :], dkk)
        cos, sin = cc[at, :], ss[at, :]
        a = a * cos - quarter(a) * sin
        b = b * cos - quarter(b) * sin
        row = jnp.concatenate([a, b, dvv], axis=1).astype(bf16)
        dqkv[at, :] = row
        whole = mm_nt(row, w[...])
        total = total + jnp.sum(whole * normed[at, :].astype(f32), axis=0, keepdims=True)
        low = whole.astype(bf16)
        m = lax.rem(c - here[0] + 4, 4)
        own[m] = jnp.where(here[1] == 0, low[0:128], low[128:256])
        other[m] = jnp.where(here[1] == 0, low[128:256], low[0:128])
        return total

    total = lax.fori_loop(0, 4, finish, jnp.zeros((1, 1536), f32))
    grad_gain[...] = total / gain[...]


def attend_backward(here, gm, q01, q2k, val, lse, cc, ss, starts, normed, w, gain):
    vm = pl.BlockSpec(memory_space=pltpu.VMEM)
    shape = jax.ShapeDtypeStruct
    half = pltpu.VMEM((1024, 128), bf16)
    full = pltpu.VMEM((1024, 128), f32)
    return pl.pallas_call(
        attend_back_body,
        out_shape=(
            shape((1024, 384), bf16),
            shape((4, 128, 1536), bf16),
            shape((4, 128, 1536), bf16),
            shape((1, 1536), f32),
        ),
        in_specs=[pl.BlockSpec(memory_space=pltpu.SMEM)] + [vm] * 11,
        out_specs=(vm,) * 4,
        scratch_shapes=[
            half, half, half, pltpu.VMEM((128, 1024), bf16), half, half, full, full, full, full,
        ],
        compiler_params=pltpu.CompilerParams(vmem_limit_bytes=56 * MIB),
        cost_estimate=pl.CostEstimate(flops=1_000_000, bytes_accessed=100_000, transcendentals=0),
        name="attend_backward",
    )(here, w, gm, q01, q2k, val, lse, cc, ss, starts, normed, gain)


def experts_body(
    here, second, grads, back, gate_w, up_w, d_gate, d_up, d_down, aw, gg, gu, routed, st, col
):
    e, c = pl.program_id(0), pl.program_id(1)
    first = (e == 0) & (c == 0)

    @pl.when(first)
    def _():
        for b in range(8):
            at = slice(128 * b, 128 * (b + 1))
            st[:, at] = second[at, 0:1536].T
        routed[...] = jnp.zeros_like(routed)

    @pl.when(c == 0)
    def _():
        lane = lax.broadcasted_iota(jnp.int32, (128, 128), 1)
        name = 4 * here[0] + 2 * here[1] + e
        hit = (lane == name) | (lane == name + 16)
        for b in range(8):
            at = slice(128 * b, 128 * (b + 1))
            table = second[at, 1536:1664].astype(f32)
            w = jnp.sum(jnp.where(hit, table, 0.0), axis=1, keepdims=True)
            col[at, :] = jnp.broadcast_to(w, (128, 128))

    x = second[:, 0:1536]
    gated = mm(x, gate_w[0])
    upper = mm(x, up_w[0])
    h = back[...].astype(f32)
    w = jnp.concatenate([col[...]] * 2, axis=1)
    sig = 1.0 / (1.0 + jnp.exp(-gated))
    silu = gated * sig
    act = silu * upper
    aw[...] = (act * w).astype(bf16)
    dots = residual_scale * jnp.sum(act * h, axis=1, keepdims=True)
    lane = lax.broadcasted_iota(jnp.int32, (1024, 128), 1)
    routed[...] += jnp.where(lane == 4 * here[0] + 2 * here[1] + e, dots, 0.0)
    ga = h * (w * residual_scale)
    gg[...] = (ga * upper * (sig * (1.0 + gated * (1.0 - sig)))).astype(bf16)
    gu[...] = (ga * silu).astype(bf16)

    d_gate[0] = mm(st[...], gg[...]).astype(bf16)
    d_up[0] = mm(st[...], gu[...]).astype(bf16)
    d_down[0] = (mm(aw[...].T, grads[...]) * residual_scale).astype(bf16)


def experts(here, second, grads, back, gate_w, up_w):
    vm = pl.BlockSpec(memory_space=pltpu.VMEM)
    shape = jax.ShapeDtypeStruct
    wide = pl.BlockSpec((1, 1536, 256), lambda e, c: (e, 0, c))
    tall = pl.BlockSpec((1, 256, 1536), lambda e, c: (e, c, 0))
    line = pl.BlockSpec((1024, 256), lambda e, c: (0, 2 * e + c))
    return pl.pallas_call(
        experts_body,
        grid=(2, 2),
        out_shape=(
            shape((2, 1536, 512), bf16),
            shape((2, 1536, 512), bf16),
            shape((2, 512, 1536), bf16),
            shape((1024, 1024), bf16),
            shape((1024, 1024), bf16),
            shape((1024, 1024), bf16),
            shape((1024, 128), f32),
        ),
        in_specs=[pl.BlockSpec(memory_space=pltpu.SMEM)] + [vm] * 2 + [line, wide, wide],
        out_specs=(wide, wide, tall, line, line, line, vm),
        scratch_shapes=[pltpu.VMEM((1536, 1024), bf16), pltpu.VMEM((1024, 128), f32)],
        compiler_params=pltpu.CompilerParams(vmem_limit_bytes=60 * MIB),
        cost_estimate=pl.CostEstimate(flops=16_000_000_000, bytes_accessed=34_000_000, transcendentals=1_000_000),
        name="experts",
    )(here, second, grads, back, gate_w, up_w)


def split_cores(here, value, own, other):
    first = here[1] == 0
    own[0] = jnp.where(first, value[0:128], value[128:256])
    other[0] = jnp.where(first, value[128:256], value[0:128])


def by_chip(here, body, width, name, rows, whole, flops):
    out = pl.BlockSpec((1, 128, width), lambda m, here: (m, 0, 0))
    shape = jax.ShapeDtypeStruct((4, 128, width), bf16)
    lines = [
        pl.BlockSpec((256, a.shape[1]), lambda m, here: (lax.rem(here[0] + m, 4), 0)) for a in rows
    ]
    return pl.pallas_call(
        body,
        grid_spec=pltpu.PrefetchScalarGridSpec(
            num_scalar_prefetch=1,
            grid=(4,),
            in_specs=lines + [pl.BlockSpec(memory_space=pltpu.VMEM)] * len(whole),
            out_specs=(out, out),
        ),
        out_shape=(shape, shape),
        compiler_params=pltpu.CompilerParams(vmem_limit_bytes=56 * MIB),
        cost_estimate=pl.CostEstimate(flops=flops, bytes_accessed=100_000, transcendentals=0),
        name=name,
    )(here, *rows, *whole)


def back_body(here, gg, gu, routed, gate_w, up_w, own, other):
    total = mm_nt(gg[:, 0:512], gate_w[0]) + mm_nt(gg[:, 512:1024], gate_w[1])
    total = total + mm_nt(gu[:, 0:512], up_w[0]) + mm_nt(gu[:, 512:1024], up_w[1])
    table = routed[...]
    high = table.astype(bf16).astype(f32)
    low = pltpu.roll(table - high, 16, 1)
    lane = lax.broadcasted_iota(jnp.int32, table.shape, 1)
    tail = jnp.where(lane < 16, high, low)
    split_cores(here, jnp.concatenate([total, tail], axis=1).astype(bf16), own, other)


def experts_back(here, gg, gu, routed, gate_w, up_w):
    return by_chip(here, back_body, 1664, "experts_back", (gg, gu, routed), (gate_w, up_w), 10**6)


def combine_body(here, aw, down_w, own, other):
    total = mm(aw[:, 0:512], down_w[0]) + mm(aw[:, 512:1024], down_w[1])
    split_cores(here, total.astype(bf16), own, other)


def combine(here, aw, down_w):
    return by_chip(here, combine_body, 1536, "combine", (aw,), (down_w,), 8 * 10**9)


def back_rows_body(ids, *refs):
    blocks, (down_w, grads, back) = refs[:8], refs[8:]

    @pl.when(pl.program_id(0) == 0)
    def _():
        for b in range(8):
            grads[pl.ds(pl.multiple_of(ids[b] * 128, 128), 128), :] = blocks[b][...]

    back[...] = mm_nt(grads[...], down_w[0]).astype(bf16)


def back_rows(ids, blocks, down_w):
    vm = pl.BlockSpec(memory_space=pltpu.VMEM)
    shape = jax.ShapeDtypeStruct
    return pl.pallas_call(
        back_rows_body,
        grid=(2,),
        out_shape=(shape((1024, 1536), bf16), shape((1024, 1024), bf16)),
        in_specs=[pl.BlockSpec(memory_space=pltpu.SMEM)]
        + [vm] * 8
        + [pl.BlockSpec((1, 512, 1536), lambda e: (e, 0, 0))],
        out_specs=(vm, pl.BlockSpec((1024, 512), lambda e: (0, e))),
        compiler_params=pltpu.CompilerParams(vmem_limit_bytes=56 * MIB),
        cost_estimate=pl.CostEstimate(flops=8_000_000_000, bytes_accessed=11_000_000, transcendentals=0),
        name="back_rows",
    )(ids, *blocks, down_w)


def weight_body(normed, grad_qkv, mixed, branch, gain_a, gain_b, router, out):
    first = mm(normed[...].T, grad_qkv[...])
    out[:, 0:256] = first[:, 0:256].astype(bf16)
    lane = lax.broadcasted_iota(jnp.int32, (256, 128), 1)
    rest = jnp.where((lane >= 66) & (lane < 82), pltpu.roll(router[...], 66, 1), first[:, 256:384])
    rest = jnp.where(lane == 64, column(gain_a[...]), rest)
    rest = jnp.where(lane == 65, column(gain_b[...]), rest)
    out[:, 256:384] = rest.astype(bf16)
    cols = jnp.concatenate([branch[b, :, 256:512] for b in range(8)], axis=0)
    out[:, 384:640] = mm(mixed[...].T, cols).astype(bf16)


def weight_grads(normed, grad_qkv, mixed, branch, gain_a, gain_b, router):
    vm = pl.BlockSpec(memory_space=pltpu.VMEM)
    slab = pl.BlockSpec((1024, 256), lambda i: (0, i))
    flat = pl.BlockSpec((1, 256), lambda i: (0, i))
    return pl.pallas_call(
        weight_body,
        grid=(6,),
        out_shape=jax.ShapeDtypeStruct((1536, 640), bf16),
        in_specs=[slab, vm, slab, vm, flat, flat, pl.BlockSpec((256, 128), lambda i: (i, 0))],
        out_specs=pl.BlockSpec((256, 640), lambda i: (i, 0)),
        compiler_params=pltpu.CompilerParams(vmem_limit_bytes=56 * MIB),
        cost_estimate=pl.CostEstimate(flops=1_000_000, bytes_accessed=100_000, transcendentals=0),
        name="weight_grads",
    )(normed, grad_qkv, mixed, branch, gain_a, gain_b, router)


def assemble_body(blocks, query, key, value, out, rest):
    total = jnp.zeros((96, 128), f32)
    for p in range(4):
        a, b = blocks[2 * p].astype(f32), blocks[2 * p + 1].astype(f32)
        total = total + a[:, 256:384] + b[:, 256:384]
        wide, slim = slice(384 * p, 384 * (p + 1)), slice(128 * p, 128 * (p + 1))
        query[:, wide] = jnp.concatenate([a[:, 0:192], b[:, 0:192]], axis=1)
        key[:, slim] = jnp.concatenate([a[:, 192:256], b[:, 192:256]], axis=1)
        value[:, slim] = jnp.concatenate([a[:, 256:320], b[:, 256:320]], axis=1)
        out[:, wide] = jnp.concatenate([a[:, 384:576], b[:, 384:576]], axis=1)
    rest[...] = total


def assemble(blocks):
    vm = pl.BlockSpec(memory_space=pltpu.VMEM)
    shape = jax.ShapeDtypeStruct
    return pl.pallas_call(
        assemble_body,
        out_shape=(
            shape((96, 1536), f32),
            shape((96, 512), f32),
            shape((96, 512), f32),
            shape((96, 1536), f32),
            shape((96, 128), f32),
        ),
        in_specs=[vm],
        out_specs=(vm,) * 5,
        cost_estimate=pl.CostEstimate(flops=1_000_000, bytes_accessed=100_000, transcendentals=0),
        name="assemble",
    )(blocks)


def column(row):
    n = row.shape[1]
    down = lax.broadcasted_iota(jnp.int32, (n, n), 0)
    along = lax.broadcasted_iota(jnp.int32, (n, n), 1)
    return jnp.sum(jnp.where(down == along, row.astype(f32), 0.0), axis=1, keepdims=True)


def pack_body(at, w_query, w_key, w_value, gain_a, gain_b, router, tokens, seg, w_out, share, sent, half):
    first = at[1] == 0
    x = at[0]
    wide = w_query[:, pl.ds(pl.multiple_of(x * 384, 128), 384)].astype(f32)
    slim = pl.ds(pl.multiple_of(x * 128, 128), 128)
    key, value = w_key[:, slim].astype(f32), w_value[:, slim].astype(f32)
    columns = jnp.concatenate(
        [
            jnp.where(first, wide[:, 0:192], wide[:, 192:384]),
            jnp.where(first, key[:, 0:64], key[:, 64:128]),
            jnp.where(first, value[:, 0:64], value[:, 64:128]),
            column(gain_a[...]),
            column(gain_b[...]),
            router[...].astype(f32),
            jnp.zeros((96, 46), f32),
        ],
        axis=1,
    ).astype(bf16)
    for i in range(16):
        share[i] = columns
    sent[:, 0:1536] = tokens[...]
    sent[:, 1536:1664] = jnp.broadcast_to(column(seg[...]), (128, 128)).astype(bf16)
    half[...] = w_out[:, pl.ds(pl.multiple_of(at[1] * 768, 128), 768)]


def pack(at, w_query, w_key, w_value, gain_a, gain_b, router, tokens, seg, w_out):
    vm = pl.BlockSpec(memory_space=pltpu.VMEM)
    shape = jax.ShapeDtypeStruct
    return pl.pallas_call(
        pack_body,
        out_shape=(shape((16, 96, 384), bf16), shape((128, 1664), bf16), shape((96, 768), bf16)),
        in_specs=[pl.BlockSpec(memory_space=pltpu.SMEM)] + [vm] * 9,
        out_specs=(vm,) * 3,
        cost_estimate=pl.CostEstimate(flops=1_000_000, bytes_accessed=2_000_000, transcendentals=0),
        name="pack",
    )(at, w_query, w_key, w_value, gain_a, gain_b, router, tokens, seg, w_out)


def project_out_body(at, mixed, *refs):
    (near, far, tokens, gain, router, named, sent, hidden, gates, mx, hid) = refs
    core = at[1]
    for p in range(4):
        mx[:, 384 * p : 384 * (p + 1)] = jnp.concatenate(
            [mixed[2 * p, :, 0:192], mixed[2 * p + 1, :, 0:192]], axis=1
        )
    own, other = mm(mx[...], near[...]), mm(mx[...], far[...])
    hid[:, pl.ds(pl.multiple_of(core * 768, 128), 768)] = own
    hid[:, pl.ds(pl.multiple_of((1 - core) * 768, 128), 768)] = other
    value = tokens[...].astype(f32) + residual_scale * hid[...]
    hidden[...] = value
    r = lax.rsqrt(jnp.mean(value * value, axis=1, keepdims=True) + eps)
    second = (value * r * gain[...]).astype(bf16)
    sent[:, 0:1536] = second
    logits = mm(second, router[...])
    on = named[...] > 0.5
    logits = jnp.where(on, logits, -1e30)
    top = jnp.max(logits, axis=1, keepdims=True)
    e = jnp.where(on, jnp.exp(logits - top), 0.0)
    g = e / jnp.sum(e, axis=1, keepdims=True)
    gates[...] = g
    high = g.astype(bf16)
    low = pltpu.roll(g - high.astype(f32), 16, 1)
    lane = lax.broadcasted_iota(jnp.int32, g.shape, 1)
    sent[:, 1536:1664] = jnp.where(lane < 16, g, low).astype(bf16)


def project_out(at, mixed, near, far, tokens, gain, router, named):
    vm = pl.BlockSpec(memory_space=pltpu.VMEM)
    shape = jax.ShapeDtypeStruct
    return pl.pallas_call(
        project_out_body,
        out_shape=(
            shape((128, 1664), bf16),
            shape((128, 1536), f32),
            shape((128, 128), f32),
            shape((128, 1536), bf16),
        ),
        in_specs=[pl.BlockSpec(memory_space=pltpu.SMEM)] + [vm] * 7,
        out_specs=(vm,) * 4,
        scratch_shapes=[pltpu.VMEM((128, 1536), f32)],
        compiler_params=pltpu.CompilerParams(vmem_limit_bytes=56 * MIB),
        cost_estimate=pl.CostEstimate(flops=4_000_000_000, bytes_accessed=8_000_000, transcendentals=0),
        name="project_out",
    )(at, mixed, near, far, tokens, gain, router, named)


def middle_body(at, *refs):
    near, far, sums = refs[0], refs[1], refs[2:6]
    (grads, hidden, gates, gain, router, grad_hidden, heads, grad_gain, grad_router, gb, gx) = refs[6:]
    core = at[1]
    total = sums[0][...]
    for other in sums[1:]:
        total = total + other[...].astype(f32)
    value = hidden[...]
    r = lax.rsqrt(jnp.mean(value * value, axis=1, keepdims=True) + eps)
    second = (value * r * gain[...]).astype(bf16)
    g = gates[...]
    table = total[:, 1536:1664]
    lane = lax.broadcasted_iota(jnp.int32, g.shape, 1)
    table = jnp.where(lane < 16, table + pltpu.roll(table, 112, 1), 0.0)
    logits = (g * (table - jnp.sum(g * table, axis=1, keepdims=True))).astype(bf16)
    grad_router[...] = mm(second.T, logits)
    grad_second = total[:, 0:1536] + mm_nt(logits, router[...])
    grad_gain[...] = jnp.sum(grad_second * value * r, axis=0, keepdims=True)
    scaled = grad_second * gain[...]
    gh = (
        grads[...].astype(f32)
        + r * scaled
        - value * (r * r * r) * jnp.mean(value * scaled, axis=1, keepdims=True)
    )
    grad_hidden[...] = gh
    low = (residual_scale * gh).astype(bf16)
    gb[...] = low
    mine = gb[:, pl.ds(pl.multiple_of(core * 768, 128), 768)]
    twin = gb[:, pl.ds(pl.multiple_of((1 - core) * 768, 128), 768)]
    gx[...] = mm_nt(mine, near[...]) + mm_nt(twin, far[...])
    zero = jnp.zeros((128, 64), f32)
    low = low.astype(f32)
    for j in range(8):
        cols = slice(192 * j, 192 * (j + 1))
        heads[j] = jnp.concatenate(
            [gx[:, cols], zero, low[:, cols], zero], axis=1
        ).astype(bf16)


def middle(at, near, far, sums, grads, hidden, gates, gain, router):
    vm = pl.BlockSpec(memory_space=pltpu.VMEM)
    shape = jax.ShapeDtypeStruct
    return pl.pallas_call(
        middle_body,
        out_shape=(
            shape((128, 1536), f32),
            shape((8, 128, 512), bf16),
            shape((1, 1536), f32),
            shape((1536, 128), f32),
        ),
        in_specs=[pl.BlockSpec(memory_space=pltpu.SMEM)] + [vm] * 11,
        out_specs=(vm,) * 4,
        scratch_shapes=[pltpu.VMEM((128, 1536), bf16), pltpu.VMEM((128, 1536), f32)],
        compiler_params=pltpu.CompilerParams(vmem_limit_bytes=56 * MIB),
        cost_estimate=pl.CostEstimate(flops=1_000_000, bytes_accessed=100_000, transcendentals=0),
        name="middle",
    )(at, near, far, *sums, grads, hidden, gates, gain, router)


def shift(value, axis, amount):
    size = lax.axis_size(axis)
    return lax.ppermute(value, axis, [((i + amount) % size, i) for i in range(size)])


def swap(value):
    return lax.ppermute(value, "core", [(0, 1), (1, 0)])


def tied(*values):
    return lax.optimization_barrier(values)


def gather_x(block):
    return [block] + [shift(block, "x", m) for m in (1, 2, 3)]


def both_cores(blocks):
    return [each for block in blocks for each in (block, swap(block))]


def scatter_core(own, other):
    near = own.astype(f32) + swap(other).astype(f32)
    return near[0], [near[m].astype(bf16) for m in range(4)]


def scatter_x(first, low):
    return [first] + [shift(low[m], "x", -m) for m in (2, 1, 3)]


def total_of(terms):
    total = terms[0]
    for term in terms[1:]:
        total = total + term.astype(f32)
    return total


def inverse_rms(values):
    return lax.rsqrt(jnp.mean(values * values, axis=-1, keepdims=True) + eps)


def per_device(
    tokens,
    segments,
    routes,
    gain_attn,
    w_query,
    w_key,
    w_value,
    w_out,
    gain_moe,
    w_router,
    expert_gate,
    expert_up,
    expert_down,
    out_grad,
):
    rows, width = tokens.shape
    parts = 8
    seq = rows * parts
    x, core = lax.axis_index("x"), lax.axis_index("core")
    me = x * 2 + core
    z = lax.axis_index("z")
    at = jnp.stack([x, core, z])

    share, sent, half = pack(
        at,
        w_query,
        w_key,
        w_value,
        gain_attn[None, :],
        gain_moe[None, :],
        w_router,
        tokens,
        segments[None, :],
        w_out,
    )
    out_near = lax.all_gather(half, ("z", "y"), axis=0, tiled=True)
    qkv_w = lax.all_to_all(share, ("z", "y"), 0, 0, tiled=True).reshape(width, 384)
    far = gather_x(sent)
    far[1], grads_sent = tied(far[1], out_grad)
    blocks = both_cores(far)
    grads_far = gather_x(grads_sent)
    extra = qkv_w[:, 256:384]
    gain_one = extra[:, 64].astype(f32)[None, :]
    gain_two = extra[:, 65].astype(f32)[None, :]
    lane = jnp.arange(128, dtype=jnp.int32)
    router_w = jnp.where(lane[None, :] < 16, jnp.roll(extra, -66, axis=1), 0)

    chips = (x + jnp.arange(4, dtype=jnp.int32)) % 4
    cores = jnp.bitwise_xor(core, jnp.arange(2, dtype=jnp.int32))
    ids = (chips[:, None] * 2 + cores[None, :]).reshape(parts)
    place = jnp.arange(seq, dtype=jnp.int32)
    freq = rope_base ** (
        -(jnp.arange(128, dtype=jnp.int32) % 32).astype(f32) * 2.0 / HEAD_DIM
    )[None, :]
    angles = place.astype(f32)[:, None] * freq

    named = jnp.any(routes[:, :, None] == lane[None, None, :], axis=1).astype(f32)

    normed, q01, q2k, val, lse, cos, sin, starts, mixed_head = attend_forward(
        ids, blocks, qkv_w, gain_one, jnp.cos(angles), jnp.sin(angles), freq, (named, router_w)
    )
    lse, out_near, *grads_far = tied(lse, out_near, *grads_far)
    out_far = swap(out_near)
    grad_blocks = both_cores(grads_far)
    mixed = lax.all_to_all(mixed_head, ("x", "core"), 0, 0, tiled=True)
    sent_two, hidden, gates, mixed = project_out(
        at, mixed, out_near, out_far, tokens, gain_two, router_w, named
    )
    second_all = lax.all_gather(sent_two, ("x", "core"), axis=0, tiled=True)
    grad_all, back = back_rows(ids, grad_blocks, expert_down)
    mixed, back = tied(mixed, back)
    mixed_all = lax.all_gather(mixed, ("x", "core"), axis=0, tiled=True)

    grad_w_gate, grad_w_up, grad_w_down, weighted, grad_gate_pre, grad_up_pre, routed = experts(
        at, second_all, grad_all, back, expert_gate, expert_up
    )
    sums = lax.psum((grad_w_gate, grad_w_up, grad_w_down), ("z", "y"))
    own, other = experts_back(at, grad_gate_pre, grad_up_pre, routed, expert_gate, expert_up)
    terms = scatter_x(*scatter_core(own, other))
    grad_hidden, heads, grad_gain_two, grad_router = middle(
        at, out_near, out_far, terms, out_grad, hidden, gates, gain_two, router_w
    )
    grad_router, weighted = tied(grad_router, weighted)
    own_out, other_out = combine(at, weighted, expert_down)
    grad_heads = lax.all_to_all(heads, ("x", "core"), 0, 0, tiled=True)
    first_out, low_out = scatter_core(own_out, other_out)
    output = (hidden + residual_scale * total_of(scatter_x(first_out, low_out))).astype(bf16)
    grad_qkv, own, other, grad_gain_one = attend_backward(
        at, grad_heads, q01, q2k, val, lse, cos, sin, starts, normed, qkv_w, gain_one
    )
    first, low = scatter_core(own, other)
    normed_terms = scatter_x(first, low)
    inputs = tokens.astype(f32)
    normed_mine = total_of(normed_terms)
    scale_one = inverse_rms(inputs)
    scaled_one = normed_mine * gain_one
    grad_inputs = (
        grad_hidden
        + scale_one * scaled_one
        - inputs * scale_one**3 * jnp.mean(inputs * scaled_one, axis=-1, keepdims=True)
    )

    table = weight_grads(
        normed, grad_qkv, mixed_all, grad_heads, grad_gain_one, grad_gain_two, grad_router
    ).reshape(16, width // 16, 640)
    pieces = lax.all_to_all(table, ("z", "y"), 0, 0, tiled=True)
    summed = jnp.sum(pieces.astype(f32), axis=0).astype(bf16)
    lines = jnp.broadcast_to(summed[None], (parts,) + summed.shape)
    lines = lax.all_to_all(lines, ("x", "core"), 0, 0, tiled=True)
    grad_q, grad_k, grad_v, grad_o, rest = assemble(lines)
    return (
        output,
        grad_inputs,
        rest[:, 64],
        grad_q,
        grad_k,
        grad_v,
        grad_o,
        rest[:, 65],
        rest[:, 66:82],
        sums[0].astype(f32),
        sums[1].astype(f32),
        sums[2].astype(f32),
    )


def solution(mesh):
    fine = Mesh(mesh.devices.reshape(4, 4, 4, 2), ("z", "y", "x", "core"))
    dp, expert, both = ("z", "y"), ("x", "core"), ("z", "y", "x", "core")
    placed = (
        P(both, None),
        P(both),
        P(both, None),
        P(dp),
        P(dp, None),
        P(dp, None),
        P(dp, None),
        P(dp, None),
        P(dp),
        P(dp, None),
        P(expert, None, None),
        P(expert, None, None),
        P(expert, None, None),
    )
    return jax.shard_map(
        per_device,
        mesh=fine,
        in_specs=placed + (P(both, None),),
        out_specs=(P(both, None),) * 2 + placed[3:],
        check_vma=False,
    )
```

profile of v0, /device:TPU:1, one launch (start us, length us, event | category | flops | bytes accessed | tf_op | source)
XLA Modules:
  0.0 340.7 jit_solution(6815983784708254512)
XLA Ops:
  17.3 7.8 %all-to-all-start = ((bf16[16,96,384]{2,1,0:T(8,128)(2,1)}), bf16[16,96,384]{2,1,0:T(8,128)(2,1)S(1)}, u32[]{:S(2)}, u32[]{:S(2)}) async-start(bf16[16,96,384]{2,1,0:T(8,128)(2,1)} %get-tuple-element.68), calls=%async_computation | async-start | bytes 2359296 | tf_op jit(solution)/shard_map/all_to_all | solution.py:688
  30.3 4.3 %collective-permute-done.1.refs_2_ = bf16[128,1664]{1,0:T(8,128)(2,1)S(1)} collective-permute-done((bf16[128,1664]{1,0:T(8,128)(2,1)}, bf16[128,1664]{1,0:T(8,128)(2,1)S(1)}, u32[]{:S(2)}, u32[]{:S(2)}) %collective-permute-start.1) | collective-permute-done | bytes 426016 | tf_op jit(solution)/shard_map/ppermute | solution.py:612
  39.4 6.8 %all-to-all-done = bf16[16,96,384]{2,1,0:T(8,128)(2,1)S(1)} async-done(((bf16[16,96,384]{2,1,0:T(8,128)(2,1)}), bf16[16,96,384]{2,1,0:T(8,128)(2,1)S(1)}, u32[]{:S(2)}, u32[]{:S(2)}) %all-to-all-start) | async-done | bytes 1179680 | tf_op jit(solution)/shard_map/all_to_all | solution.py:688
  50.2 15.5 %attend_forward.1 = (bf16[1024,1536]{1,0:T(8,128)(2,1)}, bf16[1024,128]{1,0:T(8,128)(2,1)}, bf16[1024,128]{1,0:T(8,128)(2,1)}, bf16[1024,128]{1,0:T(8,128)(2,1)}...) custom-call(s32[8]{0:T(128)} %add.114.ids, ...), custom_call_target="tpu_custom_call" | custom-call | flops 14000000000 | bytes 12000000 | tf_op jit(solution)/shard_map/attend_forward/pallas_call | solution.py:129
  70.6 4.4 %all-to-all-start.1 = ((bf16[8,128,256]{2,1,0:T(8,128)(2,1)}), bf16[8,128,256]{2,1,0:T(8,128)(2,1)S(1)}, u32[]{:S(2)}, u32[]{:S(2)}) async-start(bf16[8,128,256]{2,1,0:T(8,128)(2,1)} %get-tuple-element.69), calls=%async_computation.1 | async-start | bytes 1048576 | tf_op jit(solution)/shard_map/all_to_all | solution.py:716
  75.6 8.9 %all-to-all-done.1.mixed = bf16[8,128,256]{2,1,0:T(8,128)(2,1)S(1)} async-done(((bf16[8,128,256]{2,1,0:T(8,128)(2,1)}), bf16[8,128,256]{2,1,0:T(8,128)(2,1)S(1)}, u32[]{:S(2)}, u32[]{:S(2)}) %all-to-all-start.1) | async-done | bytes 524320 | tf_op jit(solution)/shard_map/all_to_all | solution.py:716
  86.6 5.0 %project_out.1 = (bf16[128,1664]{1,0:T(8,128)(2,1)}, f32[128,1536]{1,0:T(8,128)}, f32[128,128]{1,0:T(8,128)}, bf16[128,1536]{1,0:T(8,128)(2,1)}) custom-call(s32[3]{0:T(128)} %pad_add_fusion.at.here, bf16[8,128,256]{2,1,0:T(8,128)(2,1)} %copy-done.11, bf16[1536,768]{1,0:T(8,128)(2,1)} %all-gather.4.cloned.1.call-done.refs_0_, bf16[1536,768]{1,0:T(8,128)(2,1)} %copy-done.6, ...), custom_call_target="tpu_custom_call" | custom-call | flops 4000000000 | bytes 8000000 | tf_op jit(solution)/shard_map/project_out/pallas_call | solution.py:534
  96.9 7.9 %back_rows.1 = (bf16[1024,1536]{1,0:T(8,128)(2,1)}, bf16[1024,1024]{1,0:T(8,128)(2,1)}) custom-call(s32[8]{0:T(128)} %add.114.ids, bf16[128,1536]{1,0:T(8,128)(2,1)} %refs_6_.1, bf16[128,1536]{1,0:T(8,128)(2,1)} %copy-done.21, bf16[128,1536]{1,0:T(8,128)(2,1)} %collective-permute-done.7.refs_2_, bf16[128,1536]{1,0:T(8,128)(2,1)} %copy-done.22, ...), custom_call_target="tpu_custom_call" | custom-call | flops 8000000000 | bytes 11000000 | tf_op jit(solution)/shard_map/back_rows/pallas_call | solution.py:384
  105.0 13.6 %all-gather.6.cloned.1.call-done.second = bf16[1024,1664]{1,0:T(8,128)(2,1)} async-done(((bf16[128,1664]{1,0:T(8,128)(2,1)}), bf16[1024,1664]{1,0:T(8,128)(2,1)}) %all-gather.6.cloned.1.call-update) | async-done | bytes 3407888 | tf_op jit(solution)/shard_map/all_gather | solution.py:720
  118.7 25.8 %experts.1 = (bf16[2,1536,512]{2,1,0:T(8,128)(2,1)}, bf16[2,1536,512]{2,1,0:T(8,128)(2,1)}, bf16[2,512,1536]{2,1,0:T(8,128)(2,1)}, bf16[1024,1024]{1,0:T(8,128)(...) custom-call(s32[3]{0:T(128)} %pad_add_fusion.at.here, ...), custom_call_target="tpu_custom_call" | custom-call | flops 16000000000 | bytes 34000000 | tf_op jit(solution)/shard_map/experts/pallas_call | solution.py:298
  144.4 12.5 %experts_back.1 = (bf16[4,128,1664]{2,1,0:T(8,128)(2,1)}, bf16[4,128,1664]{2,1,0:T(8,128)(2,1)}) custom-call(s32[3]{0:T(128)} %pad_add_fusion.at.here, bf16[1024,1024]{1,0:T(8,128)(2,1)} %get-tuple-element.84.gg, bf16[1024,1024]{1,0:T(8,128)(2,1)} %get-tuple-element.85.gu, f32[1024,128]{1,0:T(8,128)} %get-tuple-element.86.routed, ...), custom_call_target="tpu_custom_call" | custom-call | flops 1000000 | bytes 100000 | tf_op jit(solution)/shard_map/experts_back/pallas_call | solution.py:331
  166.3 7.7 %collective-permute-done.16.refs_3_ = bf16[128,1664]{1,0:T(8,128)(2,1)S(1)} collective-permute-done((bf16[128,1664]{1,0:T(8,128)(2,1)S(1)}, bf16[128,1664]{1,0:T(8,128)(2,1)S(1)}, u32[]{:S(2)}, u32[]{:S(2)}) %collective-permute-start.16) | collective-permute-done | bytes 426016 | tf_op jit(solution)/shard_map/ppermute | solution.py:612
  174.0 9.8 %collective-permute-done.17.refs_4_ = bf16[128,1664]{1,0:T(8,128)(2,1)S(1)} collective-permute-done((bf16[128,1664]{1,0:T(8,128)(2,1)S(1)}, bf16[128,1664]{1,0:T(8,128)(2,1)S(1)}, u32[]{:S(2)}, u32[]{:S(2)}) %collective-permute-start.17) | collective-permute-done | bytes 426016 | tf_op jit(solution)/shard_map/ppermute | solution.py:612
  184.7 7.6 %middle.1 = (f32[128,1536]{1,0:T(8,128)}, bf16[8,128,512]{2,1,0:T(8,128)(2,1)}, f32[1,1536]{1,0:T(1,128)}, f32[1536,128]{1,0:T(8,128)}) custom-call(s32[3]{0:T(128)} %pad_add_fusion.at.here, bf16[1536,768]{1,0:T(8,128)(2,1)} %all-gather.4.cloned.1.call-done.refs_0_, bf16[1536,768]{1,0:T(8,128)(2,1)} %copy-done.6, f32[128,1664]{1,0:T(8,128)} %slice_bitcast_fusion.refs_2_, ...), custom_call_target="tpu_custom_call" | custom-call | flops 1000000 | bytes 100000 | tf_op jit(solution)/shard_map/middle/pallas_call | solution.py:593
  192.3 8.2 %combine.1 = (bf16[4,128,1536]{2,1,0:T(8,128)(2,1)}, bf16[4,128,1536]{2,1,0:T(8,128)(2,1)}) custom-call(s32[3]{0:T(128)} %pad_add_fusion.at.here, bf16[1024,1024]{1,0:T(8,128)(2,1)} %get-tuple-element.92.aw, bf16[2,512,1536]{2,1,0:T(8,128)(2,1)} %down_w.1), custom_call_target="tpu_custom_call" | custom-call | flops 8000000000 | bytes 100000 | tf_op jit(solution)/shard_map/combine/pallas_call | solution.py:331
  200.9 18.7 %all_to_all.25.gm.branch = bf16[8,128,512]{2,1,0:T(8,128)(2,1)} all-to-all(bf16[8,128,512]{2,1,0:T(8,128)(2,1)S(1)} %copy-done.9), channel_id=1, replica_groups=mesh['z'=4,'y'=4,'x'=4,'core'=2] {'x','core'}, dimensions={0} | all-to-all | bytes 2097152 | tf_op jit(solution)/shard_map/all_to_all | solution.py:736
  219.6 16.4 %attend_backward.1 = (bf16[1024,384]{1,0:T(8,128)(2,1)}, bf16[4,128,1536]{2,1,0:T(8,128)(2,1)}, bf16[4,128,1536]{2,1,0:T(8,128)(2,1)}, f32[1,1536]{1,0:T(1,128)}) custom-call(s32[3]{0:T(128)} %pad_add_fusion.at.here, bf16[1536,384]{1,0:T(8,128)(2,1)} %bitcast.60, bf16[8,128,512]{2,1,0:T(8,128)(2,1)} %all_to_all.25.gm.branch, ...), custom_call_target="tpu_custom_call" | custom-call | flops 1000000 | bytes 100000 | tf_op jit(solution)/shard_map/attend_backward/pallas_call | solution.py:228
  237.1 8.4 %weight_grads.1 = bf16[1536,640]{1,0:T(8,128)(2,1)} custom-call(bf16[1024,1536]{1,0:T(8,128)(2,1)} %get-tuple-element.104.normed, bf16[1024,384]{1,0:T(8,128)(2,1)} %get-tuple-element.107.grad_qkv, bf16[1024,1536]{1,0:T(8,128)(2,1)} %all-gather.8.cloned.1.call-done.mixed, bf16[8,128,512]{2,1,0:T(8,128)(2,1)} %all_to_all.25.gm.branch, ...), custom_call_target="tpu_custom_call" | custom-call | flops 1000000 | bytes 100000 | tf_op jit(solution)/shard_map/weight_grads/pallas_call | solution.py:414
  245.4 6.8 %all-to-all-start.3 = ((bf16[16,96,640]{2,1,0:T(8,128)(2,1)}), bf16[16,96,640]{2,1,0:T(8,128)(2,1)S(1)}, u32[]{:S(2)}, u32[]{:S(2)}) async-start(bf16[16,96,640]{2,1,0:T(8,128)(2,1)} %bitcast.61), calls=%async_computation.3 | async-start | bytes 3932160 | tf_op jit(solution)/shard_map/all_to_all | solution.py:757
  266.2 8.7 %collective-permute-done.21 = bf16[128,1536]{1,0:T(8,128)(2,1)S(1)} collective-permute-done((bf16[128,1536]{1,0:T(8,128)(2,1)S(1)}, bf16[128,1536]{1,0:T(8,128)(2,1)S(1)}, u32[]{:S(2)}, u32[]{:S(2)}) %collective-permute-start.21) | collective-permute-done | bytes 393248 | tf_op jit(solution)/shard_map/ppermute | solution.py:612
  276.0 11.0 %all-to-all-done.3 = bf16[16,96,640]{2,1,0:T(8,128)(2,1)S(1)} async-done(((bf16[16,96,640]{2,1,0:T(8,128)(2,1)}), bf16[16,96,640]{2,1,0:T(8,128)(2,1)S(1)}, u32[]{:S(2)}, u32[]{:S(2)}) %all-to-all-start.3) | async-done | bytes 1966112 | tf_op jit(solution)/shard_map/all_to_all | solution.py:757
  289.8 6.1 %all-to-all-start.4 = ((bf16[8,96,640]{2,1,0:T(8,128)(2,1)}), bf16[8,96,640]{2,1,0:T(8,128)(2,1)S(1)}, u32[]{:S(2)}, u32[]{:S(2)}) async-start(bf16[8,96,640]{2,1,0:T(8,128)(2,1)} %broadcast_in_dim.25), calls=%async_computation.4 | async-start | bytes 1966080 | tf_op jit(solution)/shard_map/all_to_all | solution.py:760
  299.9 10.4 %all-to-all-done.4.blocks = bf16[8,96,640]{2,1,0:T(8,128)(2,1)S(1)} async-done(((bf16[8,96,640]{2,1,0:T(8,128)(2,1)}), bf16[8,96,640]{2,1,0:T(8,128)(2,1)S(1)}, u32[]{:S(2)}, u32[]{:S(2)}) %all-to-all-start.4) | async-done | bytes 983072 | tf_op jit(solution)/shard_map/all_to_all | solution.py:760
  321.1 5.6 %convert_element_type.183 = f32[2,1536,512]{2,1,0:T(8,128)} convert(bf16[2,1536,512]{2,1,0:T(8,128)(2,1)} %get-tuple-element.162) | non-fusion elementwise | flops 1572864 | bytes 9437184 | tf_op jit(solution)/shard_map/convert_element_type | solution.py:772
  (152 shorter events, 88.8 us)
Async XLA Ops:
  7.2 62.5 %all-gather.4.cloned.1.call-start = ((), (), s32[]{:S(2)}) async-start(), calls=%async_computation.5 | async-start | bytes 2506752 | tf_op jit(solution)/shard_map/all_gather | solution.py:687
  12.1 36.5 %collective-permute-start = (bf16[128,1664]{1,0:T(8,128)(2,1)}, bf16[128,1664]{1,0:T(8,128)(2,1)S(1)}, u32[]{:S(2)}, u32[]{:S(2)}) collective-permute-start(bf16[128,1664]{1,0:T(8,128)(2,1)} %get-tuple-element.66.refs_0_), channel_id=1, source_target_pairs={{0,1},{1,0},{2,3},{3,2},{4,5},{5,4},{6,7},{7,6},{8,9},{9,8},{10,11... | collective-permute-start | bytes 1277960 | tf_op jit(solution)/shard_map/ppermute | solution.py:616
  13.6 21.0 %collective-permute-start.1 = (bf16[128,1664]{1,0:T(8,128)(2,1)}, bf16[128,1664]{1,0:T(8,128)(2,1)S(1)}, u32[]{:S(2)}, u32[]{:S(2)}) collective-permute-start(bf16[128,1664]{1,0:T(8,128)(2,1)} %get-tuple-element.66.refs_0_), channel_id=1, source_target_pairs={{2,0},{4,2},{6,4},{0,6},{3,1},{5,3},{7,5},{1,7},{10,8},{12,10},{14... | collective-permute-start | bytes 1277960 | tf_op jit(solution)/shard_map/ppermute | solution.py:612
  16.1 22.8 %collective-permute-start.3 = (bf16[128,1664]{1,0:T(8,128)(2,1)}, bf16[128,1664]{1,0:T(8,128)(2,1)S(1)}, u32[]{:S(2)}, u32[]{:S(2)}) collective-permute-start(bf16[128,1664]{1,0:T(8,128)(2,1)} %get-tuple-element.66.refs_0_), channel_id=1, source_target_pairs={{4,0},{6,2},{0,4},{2,6},{5,1},{7,3},{1,5},{3,7},{12,8},{14,10},{8,... | collective-permute-start | bytes 1277960 | tf_op jit(solution)/shard_map/ppermute | solution.py:612
  16.7 22.6 %collective-permute-start.5 = (bf16[128,1664]{1,0:T(8,128)(2,1)}, bf16[128,1664]{1,0:T(8,128)(2,1)}, u32[]{:S(2)}, u32[]{:S(2)}) collective-permute-start(bf16[128,1664]{1,0:T(8,128)(2,1)} %get-tuple-element.66.refs_0_), channel_id=1, source_target_pairs={{6,0},{0,2},{2,4},{4,6},{7,1},{1,3},{3,5},{5,7},{14,8},{8,10},{10,... | collective-permute-start | bytes 1277960 | tf_op jit(solution)/shard_map/ppermute | solution.py:612
  17.3 29.0 %all-to-all-start = ((bf16[16,96,384]{2,1,0:T(8,128)(2,1)}), bf16[16,96,384]{2,1,0:T(8,128)(2,1)S(1)}, u32[]{:S(2)}, u32[]{:S(2)}) async-start(bf16[16,96,384]{2,1,0:T(8,128)(2,1)} %get-tuple-element.68), calls=%async_computation | async-start | bytes 2359296 | tf_op jit(solution)/shard_map/all_to_all | solution.py:688
  35.6 30.1 %collective-permute-start.7 = (bf16[128,1536]{1,0:T(8,128)(2,1)S(1)}, bf16[128,1536]{1,0:T(8,128)(2,1)}, u32[]{:S(2)}, u32[]{:S(2)}) collective-permute-start(bf16[128,1536]{1,0:T(8,128)(2,1)S(1)} %copy-done.15), channel_id=1, source_target_pairs={{2,0},{4,2},{6,4},{0,6},{3,1},{5,3},{7,5},{1,7},{10,8},{12,10},{14... | collective-permute-start | bytes 1179656 | tf_op jit(solution)/shard_map/ppermute | solution.py:612
  48.6 17.1 %collective-permute-start.8 = (bf16[128,1536]{1,0:T(8,128)(2,1)S(1)}, bf16[128,1536]{1,0:T(8,128)(2,1)S(1)}, u32[]{:S(2)}, u32[]{:S(2)}) collective-permute-start(bf16[128,1536]{1,0:T(8,128)(2,1)S(1)} %copy-done.15), channel_id=1, source_target_pairs={{4,0},{6,2},{0,4},{2,6},{5,1},{7,3},{1,5},{3,7},{12,8},{14,10},{8,... | collective-permute-start | bytes 1179656 | tf_op jit(solution)/shard_map/ppermute | solution.py:612
  48.8 20.8 %collective-permute-start.9 = (bf16[128,1536]{1,0:T(8,128)(2,1)S(1)}, bf16[128,1536]{1,0:T(8,128)(2,1)}, u32[]{:S(2)}, u32[]{:S(2)}) collective-permute-start(bf16[128,1536]{1,0:T(8,128)(2,1)S(1)} %copy-done.15), channel_id=1, source_target_pairs={{6,0},{0,2},{2,4},{4,6},{7,1},{1,3},{3,5},{5,7},{14,8},{8,10},{10,... | collective-permute-start | bytes 1179656 | tf_op jit(solution)/shard_map/ppermute | solution.py:612
  69.7 14.8 %collective-permute-start.10 = (bf16[1536,768]{1,0:T(8,128)(2,1)}, bf16[1536,768]{1,0:T(8,128)(2,1)S(1)}, u32[]{:S(2)}, u32[]{:S(2)}) collective-permute-start(bf16[1536,768]{1,0:T(8,128)(2,1)} %all-gather.4.cloned.1.call-done.refs_0_), channel_id=1, source_target_pairs={{0,1},{1,0},{2,3},{3,2},{4,5},{5,4},{6,7},{7,6},{8,9},{9,8},{10,11... | collective-permute-start | bytes 7077896 | tf_op jit(solution)/shard_map/ppermute | solution.py:616
  75.0 43.7 %all-gather.6.cloned.1.call-start = ((), (), s32[]{:S(2)}) async-start(), calls=%async_computation.6 | async-start | bytes 3833856 | tf_op jit(solution)/shard_map/all_gather | solution.py:720
  91.7 145.4 %all-gather.8.cloned.1.call-start = ((), (), s32[]{:S(2)}) async-start(), calls=%async_computation.7 | async-start | bytes 3538944 | tf_op jit(solution)/shard_map/all_gather | solution.py:723
  104.8 216.4 %all-reduce.3.cloned.1.call-start = ((), (), s32[]{:S(2)}) async-start(), calls=%async_computation.8 | async-start | bytes 18874368 | tf_op jit(solution)/shard_map/psum | solution.py:728
  162.6 21.2 %collective-permute-start.17 = (bf16[128,1664]{1,0:T(8,128)(2,1)S(1)}, bf16[128,1664]{1,0:T(8,128)(2,1)S(1)}, u32[]{:S(2)}, u32[]{:S(2)}) collective-permute-start(bf16[128,1664]{1,0:T(8,128)(2,1)S(1)} %get-tuple-element.172), channel_id=1, source_target_pairs={{6,0},{0,2},{2,4},{4,6},{7,1},{1,3},{3,5},{5,7},{14,8},{8,10},{10,... | collective-permute-start | bytes 1277960 | tf_op jit(solution)/shard_map/ppermute | solution.py:612
  162.9 20.9 %collective-permute-start.18 = (bf16[128,1664]{1,0:T(8,128)(2,1)S(1)}, bf16[128,1664]{1,0:T(8,128)(2,1)S(1)}, u32[]{:S(2)}, u32[]{:S(2)}) collective-permute-start(bf16[128,1664]{1,0:T(8,128)(2,1)S(1)} %get-tuple-element.171), channel_id=1, source_target_pairs={{2,0},{4,2},{6,4},{0,6},{3,1},{5,3},{7,5},{1,7},{10,8},{12,10},{14... | collective-permute-start | bytes 1277960 | tf_op jit(solution)/shard_map/ppermute | solution.py:612
  200.5 51.7 %collective-permute-start.19 = (bf16[4,128,1536]{2,1,0:T(8,128)(2,1)}, bf16[4,128,1536]{2,1,0:T(8,128)(2,1)}, u32[]{:S(2)}, u32[]{:S(2)}) collective-permute-start(bf16[4,128,1536]{2,1,0:T(8,128)(2,1)} %get-tuple-element.94), channel_id=1, source_target_pairs={{0,1},{1,0},{2,3},{3,2},{4,5},{5,4},{6,7},{7,6},{8,9},{9,8},{10,11... | collective-permute-start | bytes 4718600 | tf_op jit(solution)/shard_map/ppermute | solution.py:616
  236.0 21.0 %collective-permute-start.23 = (bf16[4,128,1536]{2,1,0:T(8,128)(2,1)}, bf16[4,128,1536]{2,1,0:T(8,128)(2,1)S(1)}, u32[]{:S(2)}, u32[]{:S(2)}) collective-permute-start(bf16[4,128,1536]{2,1,0:T(8,128)(2,1)} %get-tuple-element.106), channel_id=1, source_target_pairs={{0,1},{1,0},{2,3},{3,2},{4,5},{5,4},{6,7},{7,6},{8,9},{9,8},{10,11... | collective-permute-start | bytes 4718600 | tf_op jit(solution)/shard_map/ppermute | solution.py:616
  245.4 41.5 %all-to-all-start.3 = ((bf16[16,96,640]{2,1,0:T(8,128)(2,1)}), bf16[16,96,640]{2,1,0:T(8,128)(2,1)S(1)}, u32[]{:S(2)}, u32[]{:S(2)}) async-start(bf16[16,96,640]{2,1,0:T(8,128)(2,1)} %bitcast.61), calls=%async_computation.3 | async-start | bytes 3932160 | tf_op jit(solution)/shard_map/all_to_all | solution.py:757
  255.7 19.2 %collective-permute-start.21 = (bf16[128,1536]{1,0:T(8,128)(2,1)S(1)}, bf16[128,1536]{1,0:T(8,128)(2,1)S(1)}, u32[]{:S(2)}, u32[]{:S(2)}) collective-permute-start(bf16[128,1536]{1,0:T(8,128)(2,1)S(1)} %get-tuple-element.179), channel_id=1, source_target_pairs={{6,0},{0,2},{2,4},{4,6},{7,1},{1,3},{3,5},{5,7},{14,8},{8,10},{10,... | collective-permute-start | bytes 1179656 | tf_op jit(solution)/shard_map/ppermute | solution.py:612
  256.3 18.7 %collective-permute-start.20 = (bf16[128,1536]{1,0:T(8,128)(2,1)S(1)}, bf16[128,1536]{1,0:T(8,128)(2,1)S(1)}, u32[]{:S(2)}, u32[]{:S(2)}) collective-permute-start(bf16[128,1536]{1,0:T(8,128)(2,1)S(1)} %get-tuple-element.177), channel_id=1, source_target_pairs={{4,0},{6,2},{0,4},{2,6},{5,1},{7,3},{1,5},{3,7},{12,8},{14,10},{8,... | collective-permute-start | bytes 1179656 | tf_op jit(solution)/shard_map/ppermute | solution.py:612
  260.3 35.6 %collective-permute-start.26 = (bf16[128,1536]{1,0:T(8,128)(2,1)}, bf16[128,1536]{1,0:T(8,128)(2,1)S(1)}, u32[]{:S(2)}, u32[]{:S(2)}) collective-permute-start(bf16[128,1536]{1,0:T(8,128)(2,1)} %get-tuple-element.175), channel_id=1, source_target_pairs={{2,0},{4,2},{6,4},{0,6},{3,1},{5,3},{7,5},{1,7},{10,8},{12,10},{14... | collective-permute-start | bytes 1179656 | tf_op jit(solution)/shard_map/ppermute | solution.py:612
  262.3 33.6 %collective-permute-start.25 = (bf16[128,1536]{1,0:T(8,128)(2,1)}, bf16[128,1536]{1,0:T(8,128)(2,1)S(1)}, u32[]{:S(2)}, u32[]{:S(2)}) collective-permute-start(bf16[128,1536]{1,0:T(8,128)(2,1)} %get-tuple-element.176), channel_id=1, source_target_pairs={{6,0},{0,2},{2,4},{4,6},{7,1},{1,3},{3,5},{5,7},{14,8},{8,10},{10,... | collective-permute-start | bytes 1179656 | tf_op jit(solution)/shard_map/ppermute | solution.py:612
  265.2 30.6 %collective-permute-start.24 = (bf16[128,1536]{1,0:T(8,128)(2,1)}, bf16[128,1536]{1,0:T(8,128)(2,1)S(1)}, u32[]{:S(2)}, u32[]{:S(2)}) collective-permute-start(bf16[128,1536]{1,0:T(8,128)(2,1)} %get-tuple-element.174), channel_id=1, source_target_pairs={{4,0},{6,2},{0,4},{2,6},{5,1},{7,3},{1,5},{3,7},{12,8},{14,10},{8,... | collective-permute-start | bytes 1179656 | tf_op jit(solution)/shard_map/ppermute | solution.py:612
  289.8 20.5 %all-to-all-start.4 = ((bf16[8,96,640]{2,1,0:T(8,128)(2,1)}), bf16[8,96,640]{2,1,0:T(8,128)(2,1)S(1)}, u32[]{:S(2)}, u32[]{:S(2)}) async-start(bf16[8,96,640]{2,1,0:T(8,128)(2,1)} %broadcast_in_dim.25), calls=%async_computation.4 | async-start | bytes 1966080 | tf_op jit(solution)/shard_map/all_to_all | solution.py:760
  (36 other events, 251.4 us)
Sparse Core Ops, SparseCore 0:
  12.2 56.7 all-gather.3
  91.8 26.8 all-gather.5
  120.4 27.6 all-gather.7
  157.3 163.7 all-reduce.2
where the time goes:
time: 346 us; the launch traced here: 341 us
  Pallas kernels  113 us (33%)
  waiting for transfers between devices  97.7 us (28%)
  starting transfers between devices  50.5 us (15%)
  other arithmetic  30.5 us (9%)
  blocking collectives  18.7 us (5%)
  local copies, waits for them, and re-layouts  16.5 us (5%)
  between operations  14.2 us (4%)
    ppermute x15, waiting for transfers between devices, shift(): lax.ppermute(value, axis, [((i + amount) % size, i) for i in range(size)])  36.5 us
    pallas_call x1, Pallas kernels, experts(): pl.pallas_call(experts_body, grid=(2, 2), out_shape=(shape((2, 1536, 512)...  25.8 us
    pallas_call x2, Pallas kernels, by_chip(): pl.pallas_call(body, grid_spec=pltpu.PrefetchScalarGridSpec(num_scalar_pr...  20.7 us
    all_to_all x1, blocking collectives, per_device(): grad_heads = lax.all_to_all(heads, ('x', 'core'), 0, 0, tiled=True)  18.7 us
    ppermute x15, starting transfers between devices, shift(): lax.ppermute(value, axis, [((i + amount) % size, i) for i in range(size)])  18 us
    pallas_call x1, Pallas kernels, attend_backward(): pl.pallas_call(attend_back_body, out_shape=(shape((1024, 384), bf16), sha...  16.4 us
    pallas_call x1, Pallas kernels, attend_forward(): pl.pallas_call(attend_body, out_shape=(shape((1024, 1536), bf16), shape((...  15.5 us
    all_gather x1, waiting for transfers between devices, per_device(): second_all = lax.all_gather(sent_two, ('x', 'core'), axis=0, tiled=True)  13.6 us
  transfers between devices with their start and end apart: 35, of which 17 were waited for; matrix products, arithmetic and copies ran while one was open for 8% of the time, Pallas kernels for 31%

commit v1 on v0

--- a/solution.py
+++ b/solution.py
@@ -59,8 +59,7 @@
 
 def attend_body(ids, *refs):
     blocks = refs[:8]
-    (w, gain, cos_t, sin_t, freq, _, __,
-     normed, q01, q2k, val, lse, cos_o, sin_o, starts, mixed, ka, kb, vt) = refs[8:]
+    (w, cos_t, sin_t, freq, _, normed, narrow, q01, q2k, val, lse, cos_o, sin_o, starts, mixed, ka, kb, vt) = refs[8:]
     one = jnp.zeros((1, 128), f32)
     two = jnp.zeros((1, 128), f32)
     for b in range(8):
@@ -71,11 +70,13 @@
     begin_rows = jnp.concatenate([one, two, jnp.zeros((6, 128), f32)], axis=0)
     angles = begin_rows * freq[...]
     cos_b, sin_b = jnp.cos(angles), jnp.sin(angles)
+    narrow[...] = w[:, 256:384].astype(f32).T
+    gain = narrow[64:65, :]
     for b in range(8):
         x = blocks[b][:, 0:1536].astype(f32)
         r = lax.rsqrt(jnp.mean(x * x, axis=1, keepdims=True) + eps)
         at = pl.ds(pl.multiple_of(ids[b] * 128, 128), 128)
-        normed[at, :] = (x * r * gain[...]).astype(bf16)
+        normed[at, :] = (x * r * gain).astype(bf16)
     def project(c, carry):
         at = pl.ds(pl.multiple_of(c * 256, 256), 256)
         u = mm(normed[at, :], w[...])
@@ -123,13 +124,14 @@
         mixed[2 * c + 1] = out[128:256]
 
 
-def attend_forward(ids, blocks, w, gain, cos_t, sin_t, freq, held):
+def attend_forward(ids, blocks, w, cos_t, sin_t, freq, held):
     vm = pl.BlockSpec(memory_space=pltpu.VMEM)
     shape = jax.ShapeDtypeStruct
     return pl.pallas_call(
         attend_body,
         out_shape=(
             shape((1024, 1536), bf16),
+            shape((128, 1536), f32),
             shape((1024, 128), bf16),
             shape((1024, 128), bf16),
             shape((1024, 128), bf16),
@@ -140,9 +142,9 @@
             shape((8, 128, 256), bf16),
         ),
         in_specs=[pl.BlockSpec(memory_space=pltpu.SMEM)]
-        + [vm] * 13
-        + [pl.BlockSpec(memory_space=pl.ANY)] * 2,
-        out_specs=(vm,) * 9,
+        + [vm] * 12
+        + [pl.BlockSpec(memory_space=pl.ANY)],
+        out_specs=(vm,) * 10,
         scratch_shapes=[
             pltpu.VMEM((1024, 128), bf16),
             pltpu.VMEM((1024, 128), bf16),
@@ -151,11 +153,11 @@
         compiler_params=pltpu.CompilerParams(vmem_limit_bytes=56 * MIB),
         cost_estimate=pl.CostEstimate(flops=14_000_000_000, bytes_accessed=12_000_000, transcendentals=3_200_000),
         name="attend_forward",
-    )(ids, *blocks, w, gain, cos_t, sin_t, freq, *held)
+    )(ids, *blocks, w, cos_t, sin_t, freq, held)
 
 
 def attend_back_body(
-    here, w, gm, q01, q2k, val, lse, cc, ss, starts, normed, gain,
+    here, w, gm, q01, q2k, val, lse, cc, ss, starts, normed, narrow,
     dqkv, own, other, grad_gain, ka, kb, vb, kt, do01, do2, dk, dv, d01, dq2,
 ):
     k = high_half(q2k[...].astype(f32)) * score_scale
@@ -211,16 +213,15 @@
         whole = mm_nt(row, w[...])
         total = total + jnp.sum(whole * normed[at, :].astype(f32), axis=0, keepdims=True)
         low = whole.astype(bf16)
-        m = lax.rem(c - here[0] + 4, 4)
-        own[m] = jnp.where(here[1] == 0, low[0:128], low[128:256])
-        other[m] = jnp.where(here[1] == 0, low[128:256], low[0:128])
+        own[c] = jnp.where(here[1] == 0, low[0:128], low[128:256])
+        other[c] = jnp.where(here[1] == 0, low[128:256], low[0:128])
         return total
 
     total = lax.fori_loop(0, 4, finish, jnp.zeros((1, 1536), f32))
-    grad_gain[...] = total / gain[...]
-
-
-def attend_backward(here, gm, q01, q2k, val, lse, cc, ss, starts, normed, w, gain):
+    grad_gain[...] = total / narrow[64:65, :]
+
+
+def attend_backward(here, gm, q01, q2k, val, lse, cc, ss, starts, normed, w, narrow):
     vm = pl.BlockSpec(memory_space=pltpu.VMEM)
     shape = jax.ShapeDtypeStruct
     half = pltpu.VMEM((1024, 128), bf16)
@@ -241,17 +242,19 @@
         compiler_params=pltpu.CompilerParams(vmem_limit_bytes=56 * MIB),
         cost_estimate=pl.CostEstimate(flops=1_000_000, bytes_accessed=100_000, transcendentals=0),
         name="attend_backward",
-    )(here, w, gm, q01, q2k, val, lse, cc, ss, starts, normed, gain)
-
-
-def experts_body(
-    here, second, grads, back, gate_w, up_w, d_gate, d_up, d_down, aw, gg, gu, routed, st, col
-):
+    )(here, w, gm, q01, q2k, val, lse, cc, ss, starts, normed, narrow)
+
+
+def experts_body(ids, *refs):
+    blocks = refs[:8]
+    (grads, back, gate_w, up_w, d_gate, d_up, d_down, aw, gg, gu, routed, second, st, col) = refs[8:]
     e, c = pl.program_id(0), pl.program_id(1)
     first = (e == 0) & (c == 0)
 
     @pl.when(first)
     def _():
+        for b in range(8):
+            second[pl.ds(pl.multiple_of(ids[b] * 128, 128), 128), :] = blocks[b][...]
         for b in range(8):
             at = slice(128 * b, 128 * (b + 1))
             st[:, at] = second[at, 0:1536].T
@@ -260,7 +263,7 @@
     @pl.when(c == 0)
     def _():
         lane = lax.broadcasted_iota(jnp.int32, (128, 128), 1)
-        name = 4 * here[0] + 2 * here[1] + e
+        name = 2 * ids[0] + e
         hit = (lane == name) | (lane == name + 16)
         for b in range(8):
             at = slice(128 * b, 128 * (b + 1))
@@ -279,7 +282,7 @@
     aw[...] = (act * w).astype(bf16)
     dots = residual_scale * jnp.sum(act * h, axis=1, keepdims=True)
     lane = lax.broadcasted_iota(jnp.int32, (1024, 128), 1)
-    routed[...] += jnp.where(lane == 4 * here[0] + 2 * here[1] + e, dots, 0.0)
+    routed[...] += jnp.where(lane == 2 * ids[0] + e, dots, 0.0)
     ga = h * (w * residual_scale)
     gg[...] = (ga * upper * (sig * (1.0 + gated * (1.0 - sig)))).astype(bf16)
     gu[...] = (ga * silu).astype(bf16)
@@ -289,7 +292,7 @@
     d_down[0] = (mm(aw[...].T, grads[...]) * residual_scale).astype(bf16)
 
 
-def experts(here, second, grads, back, gate_w, up_w):
+def experts(ids, blocks, grads, back, gate_w, up_w):
     vm = pl.BlockSpec(memory_space=pltpu.VMEM)
     shape = jax.ShapeDtypeStruct
     wide = pl.BlockSpec((1, 1536, 256), lambda e, c: (e, 0, c))
@@ -307,13 +310,17 @@
             shape((1024, 1024), bf16),
             shape((1024, 128), f32),
         ),
-        in_specs=[pl.BlockSpec(memory_space=pltpu.SMEM)] + [vm] * 2 + [line, wide, wide],
+        in_specs=[pl.BlockSpec(memory_space=pltpu.SMEM)] + [vm] * 9 + [line, wide, wide],
         out_specs=(wide, wide, tall, line, line, line, vm),
-        scratch_shapes=[pltpu.VMEM((1536, 1024), bf16), pltpu.VMEM((1024, 128), f32)],
+        scratch_shapes=[
+            pltpu.VMEM((1024, 1664), bf16),
+            pltpu.VMEM((1536, 1024), bf16),
+            pltpu.VMEM((1024, 128), f32),
+        ],
         compiler_params=pltpu.CompilerParams(vmem_limit_bytes=60 * MIB),
         cost_estimate=pl.CostEstimate(flops=16_000_000_000, bytes_accessed=34_000_000, transcendentals=1_000_000),
         name="experts",
-    )(here, second, grads, back, gate_w, up_w)
+    )(ids, *blocks, grads, back, gate_w, up_w)
 
 
 def split_cores(here, value, own, other):
@@ -322,28 +329,31 @@
     other[0] = jnp.where(first, value[128:256], value[0:128])
 
 
-def by_chip(here, body, width, name, rows, whole, flops):
+def by_chip(here, body, width, name, rows, whole, held, flops):
     out = pl.BlockSpec((1, 128, width), lambda m, here: (m, 0, 0))
     shape = jax.ShapeDtypeStruct((4, 128, width), bf16)
     lines = [
-        pl.BlockSpec((256, a.shape[1]), lambda m, here: (lax.rem(here[0] + m, 4), 0)) for a in rows
+        pl.BlockSpec((256, a.shape[1]), lambda m, here: (m, 0)) for a in rows
     ]
     return pl.pallas_call(
         body,
         grid_spec=pltpu.PrefetchScalarGridSpec(
             num_scalar_prefetch=1,
             grid=(4,),
-            in_specs=lines + [pl.BlockSpec(memory_space=pltpu.VMEM)] * len(whole),
+            in_specs=lines
+            + [pl.BlockSpec(memory_space=pltpu.VMEM)] * len(whole)
+            + [pl.BlockSpec(memory_space=pl.ANY)] * len(held),
             out_specs=(out, out),
         ),
         out_shape=(shape, shape),
         compiler_params=pltpu.CompilerParams(vmem_limit_bytes=56 * MIB),
         cost_estimate=pl.CostEstimate(flops=flops, bytes_accessed=100_000, transcendentals=0),
         name=name,
-    )(here, *rows, *whole)
-
-
-def back_body(here, gg, gu, routed, gate_w, up_w, own, other):
+    )(here, *rows, *whole, *held)
+
+
+def back_body(here, gg, gu, routed, gate_w, up_w, *refs):
+    own, other = refs[-2:]
     total = mm_nt(gg[:, 0:512], gate_w[0]) + mm_nt(gg[:, 512:1024], gate_w[1])
     total = total + mm_nt(gu[:, 0:512], up_w[0]) + mm_nt(gu[:, 512:1024], up_w[1])
     table = routed[...]
@@ -354,8 +364,9 @@
     split_cores(here, jnp.concatenate([total, tail], axis=1).astype(bf16), own, other)
 
 
-def experts_back(here, gg, gu, routed, gate_w, up_w):
-    return by_chip(here, back_body, 1664, "experts_back", (gg, gu, routed), (gate_w, up_w), 10**6)
+def experts_back(here, gg, gu, routed, gate_w, up_w, held):
+    rows, whole = (gg, gu, routed), (gate_w, up_w)
+    return by_chip(here, back_body, 1664, "experts_back", rows, whole, held, 10**6)
 
 
 def combine_body(here, aw, down_w, own, other):
@@ -364,7 +375,28 @@
 
 
 def combine(here, aw, down_w):
-    return by_chip(here, combine_body, 1536, "combine", (aw,), (down_w,), 8 * 10**9)
+    return by_chip(here, combine_body, 1536, "combine", (aw,), (down_w,), (), 8 * 10**9)
+
+
+def widen_body(a, b, c, x, y, z):
+    x[...] = a[...].astype(f32)
+    y[...] = b[...].astype(f32)
+    z[...] = c[...].astype(f32)
+
+
+def widen(a, b, c):
+    wide = pl.BlockSpec((1, 384, 512), lambda e, i: (e, i, 0))
+    tall = pl.BlockSpec((1, 128, 1536), lambda e, i: (e, i, 0))
+    return pl.pallas_call(
+        widen_body,
+        grid=(2, 4),
+        out_shape=tuple(jax.ShapeDtypeStruct(v.shape, f32) for v in (a, b, c)),
+        in_specs=[wide, wide, tall],
+        out_specs=(wide, wide, tall),
+        compiler_params=pltpu.CompilerParams(vmem_limit_bytes=56 * MIB),
+        cost_estimate=pl.CostEstimate(flops=1_000_000, bytes_accessed=28_000_000, transcendentals=0),
+        name="widen",
+    )(a, b, c)
 
 
 def back_rows_body(ids, *refs):
@@ -397,46 +429,80 @@
 
 def weight_body(normed, grad_qkv, mixed, branch, gain_a, gain_b, router, out):
     first = mm(normed[...].T, grad_qkv[...])
-    out[:, 0:256] = first[:, 0:256].astype(bf16)
-    lane = lax.broadcasted_iota(jnp.int32, (256, 128), 1)
-    rest = jnp.where((lane >= 66) & (lane < 82), pltpu.roll(router[...], 66, 1), first[:, 256:384])
-    rest = jnp.where(lane == 64, column(gain_a[...]), rest)
-    rest = jnp.where(lane == 65, column(gain_b[...]), rest)
-    out[:, 256:384] = rest.astype(bf16)
     cols = jnp.concatenate([branch[b, :, 256:512] for b in range(8)], axis=0)
-    out[:, 384:640] = mm(mixed[...].T, cols).astype(bf16)
+    second = mm(mixed[...].T, cols)
+    last = jnp.concatenate([first[:, 256:320], second[:, 0:192]], axis=1)
+    zero = jnp.zeros((1, 32), f32)
+    for y in range(4):
+        rows, lanes = slice(96 * y, 96 * (y + 1)), slice(96 * y, 96 * (y + 1))
+        gains = jnp.concatenate(
+            [gain_a[:, lanes], zero, gain_b[:, lanes], zero], axis=1
+        )
+        small = jnp.concatenate([router[:, lanes], jnp.zeros((16, 160), f32)], axis=1)
+        row = lax.broadcasted_iota(jnp.int32, (16, 256), 0)
+        extra = jnp.where(row == 0, jnp.broadcast_to(gains, (16, 256)), 0.0)
+        out[y, 0:96, 0:256] = first[rows, 0:256].astype(bf16)
+        out[y, 96:112, 0:256] = small.astype(bf16)
+        out[y, 0:96, 256:512] = last[rows].astype(bf16)
+        out[y, 96:112, 256:512] = extra.astype(bf16)
 
 
 def weight_grads(normed, grad_qkv, mixed, branch, gain_a, gain_b, router):
     vm = pl.BlockSpec(memory_space=pltpu.VMEM)
-    slab = pl.BlockSpec((1024, 256), lambda i: (0, i))
-    flat = pl.BlockSpec((1, 256), lambda i: (0, i))
+    slab = pl.BlockSpec((1024, 384), lambda i: (0, i))
+    flat = pl.BlockSpec((1, 384), lambda i: (0, i))
     return pl.pallas_call(
         weight_body,
-        grid=(6,),
-        out_shape=jax.ShapeDtypeStruct((1536, 640), bf16),
-        in_specs=[slab, vm, slab, vm, flat, flat, pl.BlockSpec((256, 128), lambda i: (i, 0))],
-        out_specs=pl.BlockSpec((256, 640), lambda i: (i, 0)),
+        grid=(4,),
+        out_shape=jax.ShapeDtypeStruct((16, 112, 512), bf16),
+        in_specs=[slab, vm, slab, vm, flat, flat, pl.BlockSpec((16, 384), lambda i: (0, i))],
+        out_specs=pl.BlockSpec((4, 112, 512), lambda i: (i, 0, 0)),
         compiler_params=pltpu.CompilerParams(vmem_limit_bytes=56 * MIB),
         cost_estimate=pl.CostEstimate(flops=1_000_000, bytes_accessed=100_000, transcendentals=0),
         name="weight_grads",
     )(normed, grad_qkv, mixed, branch, gain_a, gain_b, router)
 
 
-def assemble_body(blocks, query, key, value, out, rest):
-    total = jnp.zeros((96, 128), f32)
-    for p in range(4):
-        a, b = blocks[2 * p].astype(f32), blocks[2 * p + 1].astype(f32)
-        total = total + a[:, 256:384] + b[:, 256:384]
-        wide, slim = slice(384 * p, 384 * (p + 1)), slice(128 * p, 128 * (p + 1))
+def sum_body(pieces, out):
+    total = pieces[0].astype(f32)
+    for i in range(1, pieces.shape[0]):
+        total = total + pieces[i].astype(f32)
+    out[...] = total.astype(bf16)
+
+
+def sum_pieces(pieces):
+    vm = pl.BlockSpec(memory_space=pltpu.VMEM)
+    return pl.pallas_call(
+        sum_body,
+        out_shape=jax.ShapeDtypeStruct(pieces.shape[1:], bf16),
+        in_specs=[vm],
+        out_specs=vm,
+        cost_estimate=pl.CostEstimate(flops=1_000_000, bytes_accessed=100_000, transcendentals=0),
+        name="sum_pieces",
+    )(pieces)
+
+
+def assemble_body(ids, *refs):
+    blocks, (query, key, value, out, gain_a, gain_b, router) = refs[:8], refs[8:]
+    total = jnp.zeros((16, 512), f32)
+    for m in range(4):
+        here, there = blocks[2 * m][...].astype(f32), blocks[2 * m + 1][...].astype(f32)
+        total = total + here[96:112] + there[96:112]
+        first = ids[2 * m] < ids[2 * m + 1]
+        a, b = jnp.where(first, here, there)[0:96], jnp.where(first, there, here)[0:96]
+        chip = ids[2 * m] // 2
+        wide = pl.ds(pl.multiple_of(chip * 384, 128), 384)
+        slim = pl.ds(pl.multiple_of(chip * 128, 128), 128)
         query[:, wide] = jnp.concatenate([a[:, 0:192], b[:, 0:192]], axis=1)
         key[:, slim] = jnp.concatenate([a[:, 192:256], b[:, 192:256]], axis=1)
         value[:, slim] = jnp.concatenate([a[:, 256:320], b[:, 256:320]], axis=1)
-        out[:, wide] = jnp.concatenate([a[:, 384:576], b[:, 384:576]], axis=1)
-    rest[...] = total
-
-
-def assemble(blocks):
+        out[:, wide] = jnp.concatenate([a[:, 320:512], b[:, 320:512]], axis=1)
+    router[...] = total[:, 0:96]
+    gain_a[...] = total[0:1, 256:352]
+    gain_b[...] = total[0:1, 384:480]
+
+
+def assemble(ids, blocks):
     vm = pl.BlockSpec(memory_space=pltpu.VMEM)
     shape = jax.ShapeDtypeStruct
     return pl.pallas_call(
@@ -446,13 +512,15 @@
             shape((96, 512), f32),
             shape((96, 512), f32),
             shape((96, 1536), f32),
-            shape((96, 128), f32),
+            shape((1, 96), f32),
+            shape((1, 96), f32),
+            shape((16, 96), f32),
         ),
-        in_specs=[vm],
-        out_specs=(vm,) * 5,
+        in_specs=[pl.BlockSpec(memory_space=pltpu.SMEM)] + [vm] * 8,
+        out_specs=(vm,) * 7,
         cost_estimate=pl.CostEstimate(flops=1_000_000, bytes_accessed=100_000, transcendentals=0),
         name="assemble",
-    )(blocks)
+    )(ids, *blocks)
 
 
 def column(row):
@@ -462,7 +530,9 @@
     return jnp.sum(jnp.where(down == along, row.astype(f32), 0.0), axis=1, keepdims=True)
 
 
-def pack_body(at, w_query, w_key, w_value, gain_a, gain_b, router, tokens, seg, w_out, share, sent, half):
+def pack_body(
+    at, w_query, w_key, w_value, gain_a, gain_b, router, tokens, seg, share, sent
+):
     first = at[1] == 0
     x = at[0]
     wide = w_query[:, pl.ds(pl.multiple_of(x * 384, 128), 384)].astype(f32)
@@ -475,7 +545,7 @@
             jnp.where(first, value[:, 0:64], value[:, 64:128]),
             column(gain_a[...]),
             column(gain_b[...]),
-            router[...].astype(f32),
+            router[...].astype(f32).T,
             jnp.zeros((96, 46), f32),
         ],
         axis=1,
@@ -484,38 +554,32 @@
         share[i] = columns
     sent[:, 0:1536] = tokens[...]
     sent[:, 1536:1664] = jnp.broadcast_to(column(seg[...]), (128, 128)).astype(bf16)
-    half[...] = w_out[:, pl.ds(pl.multiple_of(at[1] * 768, 128), 768)]
-
-
-def pack(at, w_query, w_key, w_value, gain_a, gain_b, router, tokens, seg, w_out):
+
+
+def pack(at, w_query, w_key, w_value, gain_a, gain_b, router, tokens, seg):
     vm = pl.BlockSpec(memory_space=pltpu.VMEM)
     shape = jax.ShapeDtypeStruct
     return pl.pallas_call(
         pack_body,
-        out_shape=(shape((16, 96, 384), bf16), shape((128, 1664), bf16), shape((96, 768), bf16)),
-        in_specs=[pl.BlockSpec(memory_space=pltpu.SMEM)] + [vm] * 9,
-        out_specs=(vm,) * 3,
+        out_shape=(shape((16, 96, 384), bf16), shape((128, 1664), bf16)),
+        in_specs=[pl.BlockSpec(memory_space=pltpu.SMEM)] + [vm] * 8,
+        out_specs=(vm,) * 2,
         cost_estimate=pl.CostEstimate(flops=1_000_000, bytes_accessed=2_000_000, transcendentals=0),
         name="pack",
-    )(at, w_query, w_key, w_value, gain_a, gain_b, router, tokens, seg, w_out)
-
-
-def project_out_body(at, mixed, *refs):
-    (near, far, tokens, gain, router, named, sent, hidden, gates, mx, hid) = refs
-    core = at[1]
+    )(at, w_query, w_key, w_value, gain_a, gain_b, router, tokens, seg)
+
+
+def project_out_body(mixed, w_out, tokens, narrow, named, sent, hidden, gates, mx):
     for p in range(4):
         mx[:, 384 * p : 384 * (p + 1)] = jnp.concatenate(
             [mixed[2 * p, :, 0:192], mixed[2 * p + 1, :, 0:192]], axis=1
         )
-    own, other = mm(mx[...], near[...]), mm(mx[...], far[...])
-    hid[:, pl.ds(pl.multiple_of(core * 768, 128), 768)] = own
-    hid[:, pl.ds(pl.multiple_of((1 - core) * 768, 128), 768)] = other
-    value = tokens[...].astype(f32) + residual_scale * hid[...]
+    value = tokens[...].astype(f32) + residual_scale * mm(mx[...], w_out[...])
     hidden[...] = value
     r = lax.rsqrt(jnp.mean(value * value, axis=1, keepdims=True) + eps)
-    second = (value * r * gain[...]).astype(bf16)
+    second = (value * r * narrow[65:66, :]).astype(bf16)
     sent[:, 0:1536] = second
-    logits = mm(second, router[...])
+    logits = pltpu.roll(mm_nt(second, narrow[...].astype(bf16)), 62, 1)
     on = named[...] > 0.5
     logits = jnp.where(on, logits, -1e30)
     top = jnp.max(logits, axis=1, keepdims=True)
@@ -528,7 +592,7 @@
     sent[:, 1536:1664] = jnp.where(lane < 16, g, low).astype(bf16)
 
 
-def project_out(at, mixed, near, far, tokens, gain, router, named):
+def project_out(mixed, w_out, tokens, narrow, named):
     vm = pl.BlockSpec(memory_space=pltpu.VMEM)
     shape = jax.ShapeDtypeStruct
     return pl.pallas_call(
@@ -539,34 +603,34 @@
             shape((128, 128), f32),
             shape((128, 1536), bf16),
         ),
-        in_specs=[pl.BlockSpec(memory_space=pltpu.SMEM)] + [vm] * 7,
+        in_specs=[vm] * 5,
         out_specs=(vm,) * 4,
-        scratch_shapes=[pltpu.VMEM((128, 1536), f32)],
         compiler_params=pltpu.CompilerParams(vmem_limit_bytes=56 * MIB),
         cost_estimate=pl.CostEstimate(flops=4_000_000_000, bytes_accessed=8_000_000, transcendentals=0),
         name="project_out",
-    )(at, mixed, near, far, tokens, gain, router, named)
-
-
-def middle_body(at, *refs):
-    near, far, sums = refs[0], refs[1], refs[2:6]
-    (grads, hidden, gates, gain, router, grad_hidden, heads, grad_gain, grad_router, gb, gx) = refs[6:]
-    core = at[1]
-    total = sums[0][...]
-    for other in sums[1:]:
-        total = total + other[...].astype(f32)
+    )(mixed, w_out, tokens, narrow, named)
+
+
+def middle_body(
+    w_out, sums, grads, hidden, gates, narrow, _, grad_hidden, heads, grad_gain, grad_router, gx
+):
+    gain = narrow[65:66, :]
+    total = sums[0].astype(f32)
+    for i in range(1, 4):
+        total = total + sums[i].astype(f32)
     value = hidden[...]
     r = lax.rsqrt(jnp.mean(value * value, axis=1, keepdims=True) + eps)
-    second = (value * r * gain[...]).astype(bf16)
+    second = (value * r * gain).astype(bf16)
     g = gates[...]
     table = total[:, 1536:1664]
     lane = lax.broadcasted_iota(jnp.int32, g.shape, 1)
     table = jnp.where(lane < 16, table + pltpu.roll(table, 112, 1), 0.0)
     logits = (g * (table - jnp.sum(g * table, axis=1, keepdims=True))).astype(bf16)
-    grad_router[...] = mm(second.T, logits)
-    grad_second = total[:, 0:1536] + mm_nt(logits, router[...])
+    grad_router[...] = mm(logits.astype(f32).T.astype(bf16), second)[0:16]
+    router = pltpu.roll(logits.astype(f32), 66, 1).astype(bf16)
+    grad_second = total[:, 0:1536] + mm(router, narrow[...].astype(bf16))
     grad_gain[...] = jnp.sum(grad_second * value * r, axis=0, keepdims=True)
-    scaled = grad_second * gain[...]
+    scaled = grad_second * gain
     gh = (
         grads[...].astype(f32)
         + r * scaled
@@ -574,20 +638,15 @@
     )
     grad_hidden[...] = gh
     low = (residual_scale * gh).astype(bf16)
-    gb[...] = low
-    mine = gb[:, pl.ds(pl.multiple_of(core * 768, 128), 768)]
-    twin = gb[:, pl.ds(pl.multiple_of((1 - core) * 768, 128), 768)]
-    gx[...] = mm_nt(mine, near[...]) + mm_nt(twin, far[...])
+    gx[...] = mm_nt(low, w_out[...])
     zero = jnp.zeros((128, 64), f32)
     low = low.astype(f32)
     for j in range(8):
         cols = slice(192 * j, 192 * (j + 1))
-        heads[j] = jnp.concatenate(
-            [gx[:, cols], zero, low[:, cols], zero], axis=1
-        ).astype(bf16)
-
-
-def middle(at, near, far, sums, grads, hidden, gates, gain, router):
+        heads[j] = jnp.concatenate([gx[:, cols], zero, low[:, cols], zero], axis=1).astype(bf16)
+
+
+def middle(w_out, sums, grads, hidden, gates, narrow, held):
     vm = pl.BlockSpec(memory_space=pltpu.VMEM)
     shape = jax.ShapeDtypeStruct
     return pl.pallas_call(
@@ -596,15 +655,15 @@
             shape((128, 1536), f32),
             shape((8, 128, 512), bf16),
             shape((1, 1536), f32),
-            shape((1536, 128), f32),
+            shape((16, 1536), f32),
         ),
-        in_specs=[pl.BlockSpec(memory_space=pltpu.SMEM)] + [vm] * 11,
+        in_specs=[vm] * 6 + [pl.BlockSpec(memory_space=pl.ANY)],
         out_specs=(vm,) * 4,
-        scratch_shapes=[pltpu.VMEM((128, 1536), bf16), pltpu.VMEM((128, 1536), f32)],
+        scratch_shapes=[pltpu.VMEM((128, 1536), f32)],
         compiler_params=pltpu.CompilerParams(vmem_limit_bytes=56 * MIB),
         cost_estimate=pl.CostEstimate(flops=1_000_000, bytes_accessed=100_000, transcendentals=0),
         name="middle",
-    )(at, near, far, *sums, grads, hidden, gates, gain, router)
+    )(w_out, sums, grads, hidden, gates, narrow, held)
 
 
 def shift(value, axis, amount):
@@ -628,17 +687,22 @@
     return [each for block in blocks for each in (block, swap(block))]
 
 
-def scatter_core(own, other):
-    near = own.astype(f32) + swap(other).astype(f32)
-    return near[0], [near[m].astype(bf16) for m in range(4)]
-
-
-def scatter_x(first, low):
-    return [first] + [shift(low[m], "x", -m) for m in (2, 1, 3)]
+def near_sum(own, other):
+    return (own.astype(f32) + swap(other).astype(f32)).astype(bf16)
+
+
+def exchange(near):
+    return lax.all_to_all(near, "x", 0, 0, tiled=True)
+
+
+def exchange_apart(near):
+    x = lax.axis_index("x")
+    pieces = [lax.dynamic_index_in_dim(near, (x + m) % 4, 0, False) for m in range(4)]
+    return [pieces[0]] + [shift(pieces[m], "x", -m) for m in (2, 1, 3)]
 
 
 def total_of(terms):
-    total = terms[0]
+    total = terms[0].astype(f32)
     for term in terms[1:]:
         total = total + term.astype(f32)
     return total
@@ -672,29 +736,24 @@
     z = lax.axis_index("z")
     at = jnp.stack([x, core, z])
 
-    share, sent, half = pack(
+    share, sent = pack(
         at,
         w_query,
         w_key,
         w_value,
         gain_attn[None, :],
         gain_moe[None, :],
-        w_router,
+        w_router.T,
         tokens,
         segments[None, :],
-        w_out,
-    )
-    out_near = lax.all_gather(half, ("z", "y"), axis=0, tiled=True)
+    )
+    out_all = lax.all_gather(w_out, ("z", "y"), axis=0, tiled=True)
     qkv_w = lax.all_to_all(share, ("z", "y"), 0, 0, tiled=True).reshape(width, 384)
     far = gather_x(sent)
     far[1], grads_sent = tied(far[1], out_grad)
     blocks = both_cores(far)
     grads_far = gather_x(grads_sent)
-    extra = qkv_w[:, 256:384]
-    gain_one = extra[:, 64].astype(f32)[None, :]
-    gain_two = extra[:, 65].astype(f32)[None, :]
     lane = jnp.arange(128, dtype=jnp.int32)
-    router_w = jnp.where(lane[None, :] < 16, jnp.roll(extra, -66, axis=1), 0)
 
     chips = (x + jnp.arange(4, dtype=jnp.int32)) % 4
     cores = jnp.bitwise_xor(core, jnp.arange(2, dtype=jnp.int32))
@@ -707,71 +766,76 @@
 
     named = jnp.any(routes[:, :, None] == lane[None, None, :], axis=1).astype(f32)
 
-    normed, q01, q2k, val, lse, cos, sin, starts, mixed_head = attend_forward(
-        ids, blocks, qkv_w, gain_one, jnp.cos(angles), jnp.sin(angles), freq, (named, router_w)
-    )
-    lse, out_near, *grads_far = tied(lse, out_near, *grads_far)
-    out_far = swap(out_near)
+    normed, narrow, q01, q2k, val, lse, cos, sin, starts, mixed_head = attend_forward(
+        ids, blocks, qkv_w, jnp.cos(angles), jnp.sin(angles), freq, named
+    )
+    mixed_head, *grads_far = tied(mixed_head, *grads_far)
     grad_blocks = both_cores(grads_far)
     mixed = lax.all_to_all(mixed_head, ("x", "core"), 0, 0, tiled=True)
     sent_two, hidden, gates, mixed = project_out(
-        at, mixed, out_near, out_far, tokens, gain_two, router_w, named
-    )
-    second_all = lax.all_gather(sent_two, ("x", "core"), axis=0, tiled=True)
+        mixed, out_all, tokens, narrow, named
+    )
+    far_two = gather_x(sent_two)
     grad_all, back = back_rows(ids, grad_blocks, expert_down)
-    mixed, back = tied(mixed, back)
+    far_two[2], back = tied(far_two[2], back)
+    mixed, *far_two = tied(mixed, *far_two)
+    second_blocks = both_cores(far_two)
     mixed_all = lax.all_gather(mixed, ("x", "core"), axis=0, tiled=True)
 
     grad_w_gate, grad_w_up, grad_w_down, weighted, grad_gate_pre, grad_up_pre, routed = experts(
-        at, second_all, grad_all, back, expert_gate, expert_up
+        ids, second_blocks, grad_all, back, expert_gate, expert_up
     )
     sums = lax.psum((grad_w_gate, grad_w_up, grad_w_down), ("z", "y"))
-    own, other = experts_back(at, grad_gate_pre, grad_up_pre, routed, expert_gate, expert_up)
-    terms = scatter_x(*scatter_core(own, other))
+    own, other = experts_back(
+        at, grad_gate_pre, grad_up_pre, routed, expert_gate, expert_up, ()
+    )
+    near = near_sum(own, other)
+    near, weighted = tied(near, weighted)
+    terms = exchange(near)
+    own_out, other_out = combine(at, weighted, expert_down)
+
     grad_hidden, heads, grad_gain_two, grad_router = middle(
-        at, out_near, out_far, terms, out_grad, hidden, gates, gain_two, router_w
-    )
-    grad_router, weighted = tied(grad_router, weighted)
-    own_out, other_out = combine(at, weighted, expert_down)
+        out_all, terms, out_grad, hidden, gates, narrow, own_out
+    )
     grad_heads = lax.all_to_all(heads, ("x", "core"), 0, 0, tiled=True)
-    first_out, low_out = scatter_core(own_out, other_out)
-    output = (hidden + residual_scale * total_of(scatter_x(first_out, low_out))).astype(bf16)
+    near_out = near_sum(own_out, other_out)
     grad_qkv, own, other, grad_gain_one = attend_backward(
-        at, grad_heads, q01, q2k, val, lse, cos, sin, starts, normed, qkv_w, gain_one
-    )
-    first, low = scatter_core(own, other)
-    normed_terms = scatter_x(first, low)
+        at, grad_heads, q01, q2k, val, lse, cos, sin, starts, normed, qkv_w, narrow
+    )
+    table = weight_grads(
+        normed, grad_qkv, mixed_all, grad_heads, grad_gain_one, grad_gain_two, grad_router
+    )
+    near_out, table = tied(near_out, table)
+    output = (hidden + residual_scale * total_of(exchange_apart(near_out))).astype(bf16)
+    normed_mine = total_of(exchange_apart(near_sum(own, other)))
     inputs = tokens.astype(f32)
-    normed_mine = total_of(normed_terms)
     scale_one = inverse_rms(inputs)
-    scaled_one = normed_mine * gain_one
+    scaled_one = normed_mine * narrow[64:65, :]
     grad_inputs = (
         grad_hidden
         + scale_one * scaled_one
         - inputs * scale_one**3 * jnp.mean(inputs * scaled_one, axis=-1, keepdims=True)
     )
 
-    table = weight_grads(
-        normed, grad_qkv, mixed_all, grad_heads, grad_gain_one, grad_gain_two, grad_router
-    ).reshape(16, width // 16, 640)
     pieces = lax.all_to_all(table, ("z", "y"), 0, 0, tiled=True)
-    summed = jnp.sum(pieces.astype(f32), axis=0).astype(bf16)
-    lines = jnp.broadcast_to(summed[None], (parts,) + summed.shape)
-    lines = lax.all_to_all(lines, ("x", "core"), 0, 0, tiled=True)
-    grad_q, grad_k, grad_v, grad_o, rest = assemble(lines)
+    pieces, output, grad_inputs = tied(pieces, output, grad_inputs)
+    lines = both_cores(gather_x(sum_pieces(pieces)))
+    grad_gate, grad_up, grad_down = widen(*sums)
+    lines[0], grad_down = tied(lines[0], grad_down)
+    grad_q, grad_k, grad_v, grad_o, gain_a, gain_b, router = assemble(ids, lines)
     return (
         output,
         grad_inputs,
-        rest[:, 64],
+        gain_a.reshape(-1),
         grad_q,
         grad_k,
         grad_v,
         grad_o,
-        rest[:, 65],
-        rest[:, 66:82],
-        sums[0].astype(f32),
-        sums[1].astype(f32),
-        sums[2].astype(f32),
+        gain_b.reshape(-1),
+        router.T,
+        grad_gate,
+        grad_up,
+        grad_down,
     )
 
 

time: 346 us -> 337 us (0.974)
  blocking collectives: 18.7 us -> 0 us
  other arithmetic: 30.5 us -> 16 us
  Pallas kernels: 113 us -> 125 us
  waiting for transfers between devices: 97.7 us -> 107 us
  starting transfers between devices: 50.5 us -> 58 us
  local copies, waits for them, and re-layouts: 16.5 us -> 10.7 us
    all_to_all x1 -> x0, blocking collectives: 18.7 us -> none  [per_device(): grad_heads = lax.all_to_all(heads, ('x', 'core'), 0, 0, tiled=True)]
    all_to_all x1 -> x2, waiting for transfers between devices: 10.4 us -> 28.6 us  [the longest x1 14.9 us: per_device(): grad_heads = lax.all_to_all(heads, ('x', 'core'), 0, 0, tiled=True)]
    ppermute x15 -> x18, waiting for transfers between devices: 36.5 us -> 53.3 us  [shift(): lax.ppermute(value, axis, [((i + amount) % size, i) for i in range(size)])]
    all_gather x2 -> x1, waiting for transfers between devices: 13.6 us -> 0.01 us  [per_device(): out_all = lax.all_gather(w_out, ('z', 'y'), axis=0, tiled=True)]
    pallas_call x1 -> x3, Pallas kernels: 8.36 us -> 21.2 us  [the longest x1 11.1 us: widen(): pl.pallas_call(widen_body, grid=(2, 4), out_shape=tuple((jax.ShapeDtypeSt...]
    all_to_all x1, waiting for transfers between devices: 11 us -> 2.45 us  [per_device(): pieces = lax.all_to_all(table, ('z', 'y'), 0, 0, tiled=True)]
    ppermute x12 -> x19, starting transfers between devices: 7.13 us -> 14.2 us  [swap(): return lax.ppermute(value, 'core', [(0, 1), (1, 0)])]
    convert_element_type x5 -> x4, other arithmetic: 14.4 us -> 9.03 us  [the longest x3 7.99 us: near_sum(): return (own.astype(f32) + swap(other).astype(f32)).astype(bf16)]
  transfers between devices with their start and end apart: 35 -> 45, of which waited for: 17 -> 20; matrix products, arithmetic and copies ran while one was open for 8% -> 5% of each run, Pallas kernels for 31% -> 37%
where the time goes in v1:
time: 337 us; the launch traced here: 332 us
  Pallas kernels  125 us (37%)
  waiting for transfers between devices  107 us (32%)
  starting transfers between devices  58 us (17%)
  other arithmetic  16 us (5%)
  between operations  14.3 us (4%)
  local copies, waits for them, and re-layouts  10.7 us (3%)
    ppermute x18, waiting for transfers between devices, shift(): lax.ppermute(value, axis, [((i + amount) % size, i) for i in range(size)])  53.3 us
    pallas_call x1, Pallas kernels, experts(): pl.pallas_call(experts_body, grid=(2, 2), out_shape=(shape((2, 1536, 512)...  26.2 us
    pallas_call x2, Pallas kernels, by_chip(): pl.pallas_call(body, grid_spec=pltpu.PrefetchScalarGridSpec(num_scalar_pr...  20.5 us
    ppermute x18, starting transfers between devices, shift(): lax.ppermute(value, axis, [((i + amount) % size, i) for i in range(size)])  16.9 us
    pallas_call x1, Pallas kernels, attend_backward(): pl.pallas_call(attend_back_body, out_shape=(shape((1024, 384), bf16), sha...  16.6 us
    pallas_call x1, Pallas kernels, attend_forward(): pl.pallas_call(attend_body, out_shape=(shape((1024, 1536), bf16), shape((...  15.5 us
    all_to_all x1, waiting for transfers between devices, per_device(): grad_heads = lax.all_to_all(heads, ('x', 'core'), 0, 0, tiled=True)  14.9 us
    ppermute x19, starting transfers between devices, swap(): return lax.ppermute(value, 'core', [(0, 1), (1, 0)])  14.2 us
  transfers between devices with their start and end apart: 45, of which 20 were waited for; matrix products, arithmetic and copies ran while one was open for 5% of the time, Pallas kernels for 37%

profile of v1, /device:TPU:1, one launch (start us, length us, event | category | flops | bytes accessed | tf_op | source)
XLA Modules:
  0.0 331.7 jit_solution(2527691719415777082)
XLA Ops:
  16.4 7.8 %all-to-all-start = ((bf16[16,96,384]{2,1,0:T(8,128)(2,1)}), bf16[16,96,384]{2,1,0:T(8,128)(2,1)S(1)}, u32[]{:S(2)}, u32[]{:S(2)}) async-start(bf16[16,96,384]{2,1,0:T(8,128)(2,1)} %get-tuple-element.84), calls=%async_computation | async-start | bytes 2359296 | tf_op jit(solution)/shard_map/all_to_all | solution.py:751
  25.9 7.8 %collective-permute-done.1.refs_2_ = bf16[128,1664]{1,0:T(8,128)(2,1)S(1)} collective-permute-done((bf16[128,1664]{1,0:T(8,128)(2,1)}, bf16[128,1664]{1,0:T(8,128)(2,1)S(1)}, u32[]{:S(2)}, u32[]{:S(2)}) %collective-permute-start.1) | collective-permute-done | bytes 426016 | tf_op jit(solution)/shard_map/ppermute | solution.py:671
  48.5 15.5 %attend_forward.1 = (bf16[1024,1536]{1,0:T(8,128)(2,1)}, f32[128,1536]{1,0:T(8,128)}, bf16[1024,128]{1,0:T(8,128)(2,1)}, bf16[1024,128]{1,0:T(8,128)(2,1)}, bf16...) custom-call(s32[8]{0:T(128)} %add.160.ids, ...), custom_call_target="tpu_custom_call" | custom-call | flops 14000000000 | bytes 12000000 | tf_op jit(solution)/shard_map/attend_forward/pallas_call | solution.py:130
  64.0 5.1 %all-to-all-start.1 = ((bf16[8,128,256]{2,1,0:T(8,128)(2,1)}), bf16[8,128,256]{2,1,0:T(8,128)(2,1)S(1)}, u32[]{:S(2)}, u32[]{:S(2)}) async-start(bf16[8,128,256]{2,1,0:T(8,128)(2,1)} %get-tuple-element.87), calls=%async_computation.1 | async-start | bytes 1048576 | tf_op jit(solution)/shard_map/all_to_all | solution.py:774
  70.1 8.5 %all-to-all-done.1.mixed = bf16[8,128,256]{2,1,0:T(8,128)(2,1)S(1)} async-done(((bf16[8,128,256]{2,1,0:T(8,128)(2,1)}), bf16[8,128,256]{2,1,0:T(8,128)(2,1)S(1)}, u32[]{:S(2)}, u32[]{:S(2)}) %all-to-all-start.1) | async-done | bytes 524320 | tf_op jit(solution)/shard_map/all_to_all | solution.py:774
  79.3 5.2 %project_out.1 = (bf16[128,1664]{1,0:T(8,128)(2,1)}, f32[128,1536]{1,0:T(8,128)}, f32[128,128]{1,0:T(8,128)}, bf16[128,1536]{1,0:T(8,128)(2,1)}) custom-call(bf16[8,128,256]{2,1,0:T(8,128)(2,1)} %copy-done.10, bf16[1536,1536]{1,0:T(8,128)(2,1)} %all-gather.3.cloned.1.call-done.w_out, bf16[128,1536]{1,0:T(8,128)(2,1)} %tokens.3, ...), custom_call_target="tpu_custom_call" | custom-call | flops 4000000000 | bytes 8000000 | tf_op jit(solution)/shard_map/project_out/pallas_call | solution.py:598
  88.1 7.7 %back_rows.1 = (bf16[1024,1536]{1,0:T(8,128)(2,1)}, bf16[1024,1024]{1,0:T(8,128)(2,1)}) custom-call(s32[8]{0:T(128)} %add.160.ids, bf16[128,1536]{1,0:T(8,128)(2,1)} %grads.1, bf16[128,1536]{1,0:T(8,128)(2,1)} %copy-done.34, bf16[128,1536]{1,0:T(8,128)(2,1)} %collective-permute-done.7.refs_2_, bf16[128,1536]{1,0:T(8,128)(2,1)} %copy-done.35, ...), custom_call_target="tpu_custom_call" | custom-call | flops 8000000000 | bytes 11000000 | tf_op jit(solution)/shard_map/back_rows/pallas_call | solution.py:416
  97.8 10.4 %collective-permute-done.16.refs_6_ = bf16[128,1664]{1,0:T(8,128)(2,1)S(1)} collective-permute-done((bf16[128,1664]{1,0:T(8,128)(2,1)}, bf16[128,1664]{1,0:T(8,128)(2,1)S(1)}, u32[]{:S(2)}, u32[]{:S(2)}) %collective-permute-start.16) | collective-permute-done | bytes 426016 | tf_op jit(solution)/shard_map/ppermute | solution.py:671
  112.9 26.2 %experts.1 = (bf16[2,1536,512]{2,1,0:T(8,128)(2,1)}, bf16[2,1536,512]{2,1,0:T(8,128)(2,1)}, bf16[2,512,1536]{2,1,0:T(8,128)(2,1)}, bf16[1024,1024]{1,0:T(8,128)(...) custom-call(s32[8]{0:T(128)} %add.160.ids, ...), custom_call_target="tpu_custom_call" | custom-call | flops 16000000000 | bytes 34000000 | tf_op jit(solution)/shard_map/experts/pallas_call | solution.py:301
  139.1 12.4 %experts_back.1 = (bf16[4,128,1664]{2,1,0:T(8,128)(2,1)}, bf16[4,128,1664]{2,1,0:T(8,128)(2,1)}) custom-call(s32[3]{0:T(128)} %pad_add_fusion.at.here, bf16[1024,1024]{1,0:T(8,128)(2,1)} %get-tuple-element.103.gg, bf16[1024,1024]{1,0:T(8,128)(2,1)} %get-tuple-element.104.gu, f32[1024,128]{1,0:T(8,128)} %get-tuple-element.105.routed, ...), custom_call_target="tpu_custom_call" | custom-call | flops 1000000 | bytes 100000 | tf_op jit(solution)/shard_map/experts_back/pallas_call | solution.py:338
  162.2 8.1 %combine.1 = (bf16[4,128,1536]{2,1,0:T(8,128)(2,1)}, bf16[4,128,1536]{2,1,0:T(8,128)(2,1)}) custom-call(s32[3]{0:T(128)} %pad_add_fusion.at.here, bf16[1024,1024]{1,0:T(8,128)(2,1)} %get-tuple-element.109.aw, bf16[2,512,1536]{2,1,0:T(8,128)(2,1)} %down_w.1), custom_call_target="tpu_custom_call" | custom-call | flops 8000000000 | bytes 100000 | tf_op jit(solution)/shard_map/combine/pallas_call | solution.py:338
  170.3 13.7 %all-to-all-done.2.sums = bf16[4,128,1664]{2,1,0:T(8,128)(2,1)S(1)} async-done(((bf16[4,128,1664]{2,1,0:T(8,128)(2,1)}), bf16[4,128,1664]{2,1,0:T(8,128)(2,1)S(1)}, u32[]{:S(2)}, u32[]{:S(2)}) %all-to-all-start.2) | async-done | bytes 1703968 | tf_op jit(solution)/shard_map/all_to_all | solution.py:695
  185.2 7.1 %middle.1 = (f32[128,1536]{1,0:T(8,128)}, bf16[8,128,512]{2,1,0:T(8,128)(2,1)}, f32[1,1536]{1,0:T(1,128)}, f32[16,1536]{1,0:T(8,128)}) custom-call(bf16[1536,1536]{1,0:T(8,128)(2,1)} %all-gather.3.cloned.1.call-done.w_out, bf16[4,128,1664]{2,1,0:T(8,128)(2,1)} %copy-done.2, bf16[128,1536]{1,0:T(8,128)(2,1)} %grads.1, f32[128,1536]{1,0:T(8,128)} %get-tuple-element.114.hidden, ...), custom_call_target="tpu_custom_call" | custom-call | flops 1000000 | bytes 100000 | tf_op jit(solution)/shard_map/middle/pallas_call | solution.py:652
  192.3 4.7 %all-to-all-start.3 = ((bf16[8,128,512]{2,1,0:T(8,128)(2,1)}), bf16[8,128,512]{2,1,0:T(8,128)(2,1)S(1)}, u32[]{:S(2)}, u32[]{:S(2)}) async-start(bf16[8,128,512]{2,1,0:T(8,128)(2,1)} %get-tuple-element.116), calls=%async_computation.3 | async-start | bytes 2097152 | tf_op jit(solution)/shard_map/all_to_all | solution.py:800
  197.2 14.9 %all-to-all-done.3.gm.branch = bf16[8,128,512]{2,1,0:T(8,128)(2,1)S(1)} async-done(((bf16[8,128,512]{2,1,0:T(8,128)(2,1)}), bf16[8,128,512]{2,1,0:T(8,128)(2,1)S(1)}, u32[]{:S(2)}, u32[]{:S(2)}) %all-to-all-start.3) | async-done | bytes 1048608 | tf_op jit(solution)/shard_map/all_to_all | solution.py:800
  213.1 16.6 %attend_backward.1 = (bf16[1024,384]{1,0:T(8,128)(2,1)}, bf16[4,128,1536]{2,1,0:T(8,128)(2,1)}, bf16[4,128,1536]{2,1,0:T(8,128)(2,1)}, f32[1,1536]{1,0:T(1,128)}) custom-call(s32[3]{0:T(128)} %pad_add_fusion.at.here, bf16[1536,384]{1,0:T(8,128)(2,1)} %bitcast.34, bf16[8,128,512]{2,1,0:T(8,128)(2,1)} %copy-done, bf16[1024,128]{1,0:T(8,128)(2,1)} %get-tuple-element.117.q01, ...), custom_call_target="tpu_custom_call" | custom-call | flops 1000000 | bytes 100000 | tf_op jit(solution)/shard_map/attend_backward/pallas_call | solution.py:229
  234.7 7.6 %weight_grads.1 = bf16[16,112,512]{2,1,0:T(8,128)(2,1)} custom-call(bf16[1024,1536]{1,0:T(8,128)(2,1)} %get-tuple-element.112.normed, bf16[1024,384]{1,0:T(8,128)(2,1)} %get-tuple-element.124.grad_qkv, bf16[1024,1536]{1,0:T(8,128)(2,1)} %all-gather.5.cloned.1.call-done.mixed, bf16[8,128,512]{2,1,0:T(8,128)(2,1)} %copy-done, ...), custom_call_target="tpu_custom_call" | custom-call | flops 1000000 | bytes 100000 | tf_op jit(solution)/shard_map/weight_grads/pallas_call | solution.py:454
  242.3 5.6 %all-to-all-start.4 = ((bf16[16,112,512]{2,1,0:T(8,128)(2,1)}), bf16[16,112,512]{2,1,0:T(8,128)(2,1)S(1)}, u32[]{:S(2)}, u32[]{:S(2)}) async-start(bf16[16,112,512]{2,1,0:T(8,128)(2,1)} %weight_grads.1), calls=%async_computation.4 | async-start | bytes 3670016 | tf_op jit(solution)/shard_map/all_to_all | solution.py:820
  254.4 4.0 %collective-permute-done.25 = bf16[128,1536]{1,0:T(8,128)(2,1)S(1)} collective-permute-done((bf16[128,1536]{1,0:T(8,128)(2,1)S(1)}, bf16[128,1536]{1,0:T(8,128)(2,1)S(1)}, u32[]{:S(2)}, u32[]{:S(2)}) %collective-permute-start.25) | collective-permute-done | bytes 393248 | tf_op jit(solution)/shard_map/ppermute | solution.py:671
  259.5 8.6 %collective-permute-done.24 = bf16[128,1536]{1,0:T(8,128)(2,1)S(1)} collective-permute-done((bf16[128,1536]{1,0:T(8,128)(2,1)S(1)}, bf16[128,1536]{1,0:T(8,128)(2,1)S(1)}, u32[]{:S(2)}, u32[]{:S(2)}) %collective-permute-start.24) | collective-permute-done | bytes 393248 | tf_op jit(solution)/shard_map/ppermute | solution.py:671
  269.1 6.2 %collective-permute-done.29 = bf16[128,1536]{1,0:T(8,128)(2,1)S(1)} collective-permute-done((bf16[128,1536]{1,0:T(8,128)(2,1)S(1)}, bf16[128,1536]{1,0:T(8,128)(2,1)S(1)}, u32[]{:S(2)}, u32[]{:S(2)}) %collective-permute-start.29) | collective-permute-done | bytes 393248 | tf_op jit(solution)/shard_map/ppermute | solution.py:671
  275.4 10.3 %collective-permute-done.28 = bf16[128,1536]{1,0:T(8,128)(2,1)S(1)} collective-permute-done((bf16[128,1536]{1,0:T(8,128)(2,1)S(1)}, bf16[128,1536]{1,0:T(8,128)(2,1)S(1)}, u32[]{:S(2)}, u32[]{:S(2)}) %collective-permute-start.28) | collective-permute-done | bytes 393248 | tf_op jit(solution)/shard_map/ppermute | solution.py:671
  304.9 4.9 %all-reduce.3.cloned.1.call-done = (bf16[2,1536,512]{2,1,0:T(8,128)(2,1)}, bf16[2,1536,512]{2,1,0:T(8,128)(2,1)}, bf16[2,512,1536]{2,1,0:T(8,128)(2,1)}) async-done(((bf16[2,1536,512]{2,1,0:T(8,128)(2,1)}, bf16[2,1536,512]{2,1,0:T(8,128)(2,1)}, bf16[2,512,1536]{2,1,0:T(8,128)(2,1)}), (bf16[2,1536,512]{2,1,0:T(8,128)(2,1)}, bf16[2,1536,512]{2,1,0:T(8,128)(2,1)}, ...) | async-done | bytes 9437200 | tf_op jit(solution)/shard_map/psum | solution.py:788
  309.8 11.1 %widen.1 = (f32[2,1536,512]{2,1,0:T(8,128)}, f32[2,1536,512]{2,1,0:T(8,128)}, f32[2,512,1536]{2,1,0:T(8,128)}) custom-call(bf16[2,1536,512]{2,1,0:T(8,128)(2,1)} %get-tuple-element.154.a, bf16[2,1536,512]{2,1,0:T(8,128)(2,1)} %get-tuple-element.155.b, bf16[2,512,1536]{2,1,0:T(8,128)(2,1)} %get-tuple-element.156.c), custom_call_target="tpu_custom_call" | custom-call | flops 1000000 | bytes 28000000 | tf_op jit(solution)/shard_map/widen/pallas_call | solution.py:390
  (179 shorter events, 87.4 us)
Async XLA Ops:
  7.2 71.3 %all-gather.3.cloned.1.call-start = ((), (), s32[]{:S(2)}) async-start(), calls=%async_computation.5 | async-start | bytes 5013504 | tf_op jit(solution)/shard_map/all_gather | solution.py:750
  11.3 31.0 %collective-permute-start = (bf16[128,1664]{1,0:T(8,128)(2,1)}, bf16[128,1664]{1,0:T(8,128)(2,1)S(1)}, u32[]{:S(2)}, u32[]{:S(2)}) collective-permute-start(bf16[128,1664]{1,0:T(8,128)(2,1)} %get-tuple-element.82.refs_0_), channel_id=1, source_target_pairs={{0,1},{1,0},{2,3},{3,2},{4,5},{5,4},{6,7},{7,6},{8,9},{9,8},{10,11... | collective-permute-start | bytes 1277960 | tf_op jit(solution)/shard_map/ppermute | solution.py:675
  12.7 21.1 %collective-permute-start.1 = (bf16[128,1664]{1,0:T(8,128)(2,1)}, bf16[128,1664]{1,0:T(8,128)(2,1)S(1)}, u32[]{:S(2)}, u32[]{:S(2)}) collective-permute-start(bf16[128,1664]{1,0:T(8,128)(2,1)} %get-tuple-element.82.refs_0_), channel_id=1, source_target_pairs={{2,0},{4,2},{6,4},{0,6},{3,1},{5,3},{7,5},{1,7},{10,8},{12,10},{14... | collective-permute-start | bytes 1277960 | tf_op jit(solution)/shard_map/ppermute | solution.py:671
  15.3 19.5 %collective-permute-start.3 = (bf16[128,1664]{1,0:T(8,128)(2,1)}, bf16[128,1664]{1,0:T(8,128)(2,1)S(1)}, u32[]{:S(2)}, u32[]{:S(2)}) collective-permute-start(bf16[128,1664]{1,0:T(8,128)(2,1)} %get-tuple-element.82.refs_0_), channel_id=1, source_target_pairs={{4,0},{6,2},{0,4},{2,6},{5,1},{7,3},{1,5},{3,7},{12,8},{14,10},{8,... | collective-permute-start | bytes 1277960 | tf_op jit(solution)/shard_map/ppermute | solution.py:671
  15.8 22.2 %collective-permute-start.5 = (bf16[128,1664]{1,0:T(8,128)(2,1)}, bf16[128,1664]{1,0:T(8,128)(2,1)S(1)}, u32[]{:S(2)}, u32[]{:S(2)}) collective-permute-start(bf16[128,1664]{1,0:T(8,128)(2,1)} %get-tuple-element.82.refs_0_), channel_id=1, source_target_pairs={{6,0},{0,2},{2,4},{4,6},{7,1},{1,3},{3,5},{5,7},{14,8},{8,10},{10,... | collective-permute-start | bytes 1277960 | tf_op jit(solution)/shard_map/ppermute | solution.py:671
  16.4 31.0 %all-to-all-start = ((bf16[16,96,384]{2,1,0:T(8,128)(2,1)}), bf16[16,96,384]{2,1,0:T(8,128)(2,1)S(1)}, u32[]{:S(2)}, u32[]{:S(2)}) async-start(bf16[16,96,384]{2,1,0:T(8,128)(2,1)} %get-tuple-element.84), calls=%async_computation | async-start | bytes 2359296 | tf_op jit(solution)/shard_map/all_to_all | solution.py:751
  41.9 22.0 %collective-permute-start.7 = (bf16[128,1536]{1,0:T(8,128)(2,1)S(1)}, bf16[128,1536]{1,0:T(8,128)(2,1)}, u32[]{:S(2)}, u32[]{:S(2)}) collective-permute-start(bf16[128,1536]{1,0:T(8,128)(2,1)S(1)} %copy-done.11), channel_id=1, source_target_pairs={{2,0},{4,2},{6,4},{0,6},{3,1},{5,3},{7,5},{1,7},{10,8},{12,10},{14... | collective-permute-start | bytes 1179656 | tf_op jit(solution)/shard_map/ppermute | solution.py:671
  42.2 21.7 %collective-permute-start.8 = (bf16[128,1536]{1,0:T(8,128)(2,1)S(1)}, bf16[128,1536]{1,0:T(8,128)(2,1)}, u32[]{:S(2)}, u32[]{:S(2)}) collective-permute-start(bf16[128,1536]{1,0:T(8,128)(2,1)S(1)} %copy-done.11), channel_id=1, source_target_pairs={{4,0},{6,2},{0,4},{2,6},{5,1},{7,3},{1,5},{3,7},{12,8},{14,10},{8,... | collective-permute-start | bytes 1179656 | tf_op jit(solution)/shard_map/ppermute | solution.py:671
  42.8 21.2 %collective-permute-start.9 = (bf16[128,1536]{1,0:T(8,128)(2,1)S(1)}, bf16[128,1536]{1,0:T(8,128)(2,1)}, u32[]{:S(2)}, u32[]{:S(2)}) collective-permute-start(bf16[128,1536]{1,0:T(8,128)(2,1)S(1)} %copy-done.11), channel_id=1, source_target_pairs={{6,0},{0,2},{2,4},{4,6},{7,1},{1,3},{3,5},{5,7},{14,8},{8,10},{10,... | collective-permute-start | bytes 1179656 | tf_op jit(solution)/shard_map/ppermute | solution.py:671
  69.1 165.6 %all-gather.5.cloned.1.call-start = ((), (), s32[]{:S(2)}) async-start(), calls=%async_computation.6 | async-start | bytes 3538944 | tf_op jit(solution)/shard_map/all_gather | solution.py:783
  86.7 21.5 %collective-permute-start.16 = (bf16[128,1664]{1,0:T(8,128)(2,1)}, bf16[128,1664]{1,0:T(8,128)(2,1)S(1)}, u32[]{:S(2)}, u32[]{:S(2)}) collective-permute-start(bf16[128,1664]{1,0:T(8,128)(2,1)} %get-tuple-element.97.refs_0_), channel_id=1, source_target_pairs={{6,0},{0,2},{2,4},{4,6},{7,1},{1,3},{3,5},{5,7},{14,8},{8,10},{10,... | collective-permute-start | bytes 1277960 | tf_op jit(solution)/shard_map/ppermute | solution.py:671
  108.3 201.6 %all-reduce.3.cloned.1.call-start = ((), (), s32[]{:S(2)}) async-start(), calls=%async_computation.7 | async-start | bytes 18874368 | tf_op jit(solution)/shard_map/psum | solution.py:788
  158.4 25.6 %all-to-all-start.2 = ((bf16[4,128,1664]{2,1,0:T(8,128)(2,1)}), bf16[4,128,1664]{2,1,0:T(8,128)(2,1)S(1)}, u32[]{:S(2)}, u32[]{:S(2)}) async-start(bf16[4,128,1664]{2,1,0:T(8,128)(2,1)} %add_convert_fusion), calls=%async_computation.2 | async-start | bytes 3407872 | tf_op jit(solution)/shard_map/all_to_all | solution.py:695
  192.3 19.8 %all-to-all-start.3 = ((bf16[8,128,512]{2,1,0:T(8,128)(2,1)}), bf16[8,128,512]{2,1,0:T(8,128)(2,1)S(1)}, u32[]{:S(2)}, u32[]{:S(2)}) async-start(bf16[8,128,512]{2,1,0:T(8,128)(2,1)} %get-tuple-element.116), calls=%async_computation.3 | async-start | bytes 2097152 | tf_op jit(solution)/shard_map/all_to_all | solution.py:800
  197.0 34.7 %collective-permute-start.22 = (bf16[4,128,1536]{2,1,0:T(8,128)(2,1)}, bf16[4,128,1536]{2,1,0:T(8,128)(2,1)}, u32[]{:S(2)}, u32[]{:S(2)}) collective-permute-start(bf16[4,128,1536]{2,1,0:T(8,128)(2,1)} %get-tuple-element.111), channel_id=1, source_target_pairs={{0,1},{1,0},{2,3},{3,2},{4,5},{5,4},{6,7},{7,6},{8,9},{9,8},{10,11... | collective-permute-start | bytes 4718600 | tf_op jit(solution)/shard_map/ppermute | solution.py:675
  229.7 20.7 %collective-permute-start.26 = (bf16[4,128,1536]{2,1,0:T(8,128)(2,1)}, bf16[4,128,1536]{2,1,0:T(8,128)(2,1)}, u32[]{:S(2)}, u32[]{:S(2)}) collective-permute-start(bf16[4,128,1536]{2,1,0:T(8,128)(2,1)} %get-tuple-element.133), channel_id=1, source_target_pairs={{0,1},{1,0},{2,3},{3,2},{4,5},{5,4},{6,7},{7,6},{8,9},{9,8},{10,11... | collective-permute-start | bytes 4718600 | tf_op jit(solution)/shard_map/ppermute | solution.py:675
  242.3 47.6 %all-to-all-start.4 = ((bf16[16,112,512]{2,1,0:T(8,128)(2,1)}), bf16[16,112,512]{2,1,0:T(8,128)(2,1)S(1)}, u32[]{:S(2)}, u32[]{:S(2)}) async-start(bf16[16,112,512]{2,1,0:T(8,128)(2,1)} %weight_grads.1), calls=%async_computation.4 | async-start | bytes 3670016 | tf_op jit(solution)/shard_map/all_to_all | solution.py:820
  249.1 19.0 %collective-permute-start.24 = (bf16[128,1536]{1,0:T(8,128)(2,1)S(1)}, bf16[128,1536]{1,0:T(8,128)(2,1)S(1)}, u32[]{:S(2)}, u32[]{:S(2)}) collective-permute-start(bf16[128,1536]{1,0:T(8,128)(2,1)S(1)} %get-tuple-element.162), channel_id=1, source_target_pairs={{6,0},{0,2},{2,4},{4,6},{7,1},{1,3},{3,5},{5,7},{14,8},{8,10},{10,... | collective-permute-start | bytes 1179656 | tf_op jit(solution)/shard_map/ppermute | solution.py:671
  252.4 23.0 %collective-permute-start.29 = (bf16[128,1536]{1,0:T(8,128)(2,1)S(1)}, bf16[128,1536]{1,0:T(8,128)(2,1)S(1)}, u32[]{:S(2)}, u32[]{:S(2)}) collective-permute-start(bf16[128,1536]{1,0:T(8,128)(2,1)S(1)} %get-tuple-element.158), channel_id=1, source_target_pairs={{2,0},{4,2},{6,4},{0,6},{3,1},{5,3},{7,5},{1,7},{10,8},{12,10},{14... | collective-permute-start | bytes 1179656 | tf_op jit(solution)/shard_map/ppermute | solution.py:671
  254.4 31.2 %collective-permute-start.28 = (bf16[128,1536]{1,0:T(8,128)(2,1)S(1)}, bf16[128,1536]{1,0:T(8,128)(2,1)S(1)}, u32[]{:S(2)}, u32[]{:S(2)}) collective-permute-start(bf16[128,1536]{1,0:T(8,128)(2,1)S(1)} %get-tuple-element.159), channel_id=1, source_target_pairs={{6,0},{0,2},{2,4},{4,6},{7,1},{1,3},{3,5},{5,7},{14,8},{8,10},{10,... | collective-permute-start | bytes 1179656 | tf_op jit(solution)/shard_map/ppermute | solution.py:671
  258.5 27.2 %collective-permute-start.27 = (bf16[128,1536]{1,0:T(8,128)(2,1)S(1)}, bf16[128,1536]{1,0:T(8,128)(2,1)S(1)}, u32[]{:S(2)}, u32[]{:S(2)}) collective-permute-start(bf16[128,1536]{1,0:T(8,128)(2,1)S(1)} %get-tuple-element.157), channel_id=1, source_target_pairs={{4,0},{6,2},{0,4},{2,6},{5,1},{7,3},{1,5},{3,7},{12,8},{14,10},{8,... | collective-permute-start | bytes 1179656 | tf_op jit(solution)/shard_map/ppermute | solution.py:671
  296.7 24.3 %collective-permute-start.30 = (bf16[112,512]{1,0:T(8,128)(2,1)}, bf16[112,512]{1,0:T(8,128)(2,1)S(1)}, u32[]{:S(2)}, u32[]{:S(2)}) collective-permute-start(bf16[112,512]{1,0:T(8,128)(2,1)} %sum_pieces.1.refs_0_), channel_id=1, source_target_pairs={{0,1},{1,0},{2,3},{3,2},{4,5},{5,4},{6,7},{7,6},{8,9},{9,8},{10,11... | collective-permute-start | bytes 344072 | tf_op jit(solution)/shard_map/ppermute | solution.py:675
  298.1 22.9 %collective-permute-start.32 = (bf16[112,512]{1,0:T(8,128)(2,1)S(1)}, bf16[112,512]{1,0:T(8,128)(2,1)S(1)}, u32[]{:S(2)}, u32[]{:S(2)}) collective-permute-start(bf16[112,512]{1,0:T(8,128)(2,1)S(1)} %collective-permute-done.31.refs_2_), channel_id=1, source_target_pairs={{0,1},{1,0},{2,3},{3,2},{4,5},{5,4},{6,7},{7,6},{8,9},{9,8},{10,11... | collective-permute-start | bytes 344072 | tf_op jit(solution)/shard_map/ppermute | solution.py:675
  300.5 20.4 %collective-permute-start.34 = (bf16[112,512]{1,0:T(8,128)(2,1)S(1)}, bf16[112,512]{1,0:T(8,128)(2,1)S(1)}, u32[]{:S(2)}, u32[]{:S(2)}) collective-permute-start(bf16[112,512]{1,0:T(8,128)(2,1)S(1)} %collective-permute-done.33.refs_4_), channel_id=1, source_target_pairs={{0,1},{1,0},{2,3},{3,2},{4,5},{5,4},{6,7},{7,6},{8,9},{9,8},{10,11... | collective-permute-start | bytes 344072 | tf_op jit(solution)/shard_map/ppermute | solution.py:675
  (58 other events, 538.7 us)
Sparse Core Ops, SparseCore 0:
  10.2 67.8 all-gather.2
  108.4 26.7 all-gather.4
  139.9 169.8 all-reduce.2

commit v2 on v1

--- a/solution.py
+++ b/solution.py
@@ -378,21 +378,42 @@
     return by_chip(here, combine_body, 1536, "combine", (aw,), (down_w,), (), 8 * 10**9)
 
 
-def widen_body(a, b, c, x, y, z):
-    x[...] = a[...].astype(f32)
-    y[...] = b[...].astype(f32)
-    z[...] = c[...].astype(f32)
+def widen_body(a, b, c, x, y, z, *refs):
+    held, grown, got, sent = refs[0:3], refs[3:6], refs[6], refs[7]
+    work = []
+    for k, (source, target) in enumerate(((a, x), (b, y), (c, z))):
+        half = source.shape[1] // 2
+        for e in range(2):
+            for i in range(2):
+                j = 2 * e + i
+                at = pl.ds(half * i, half)
+                load = pltpu.make_async_copy(
+                    source.at[e, at], held[k].at[j], got.at[4 * k + j]
+                )
+                store = pltpu.make_async_copy(
+                    grown[k].at[j], target.at[e, at], sent.at[4 * k + j]
+                )
+                load.start()
+                work.append((k, j, load, store))
+    for k, j, load, store in work:
+        load.wait()
+        grown[k][j] = held[k][j].astype(f32)
+        store.start()
+    for _, _, _, store in work:
+        store.wait()
 
 
 def widen(a, b, c):
-    wide = pl.BlockSpec((1, 384, 512), lambda e, i: (e, i, 0))
-    tall = pl.BlockSpec((1, 128, 1536), lambda e, i: (e, i, 0))
+    hbm = pl.BlockSpec(memory_space=pl.ANY)
+    shapes = [(4, v.shape[1] // 2, v.shape[2]) for v in (a, b, c)]
     return pl.pallas_call(
         widen_body,
-        grid=(2, 4),
         out_shape=tuple(jax.ShapeDtypeStruct(v.shape, f32) for v in (a, b, c)),
-        in_specs=[wide, wide, tall],
-        out_specs=(wide, wide, tall),
+        in_specs=[hbm] * 3,
+        out_specs=(hbm,) * 3,
+        scratch_shapes=[pltpu.VMEM(s, bf16) for s in shapes]
+        + [pltpu.VMEM(s, f32) for s in shapes]
+        + [pltpu.SemaphoreType.DMA((12,)), pltpu.SemaphoreType.DMA((12,))],
         compiler_params=pltpu.CompilerParams(vmem_limit_bytes=56 * MIB),
         cost_estimate=pl.CostEstimate(flops=1_000_000, bytes_accessed=28_000_000, transcendentals=0),
         name="widen",
@@ -821,7 +842,6 @@
     pieces, output, grad_inputs = tied(pieces, output, grad_inputs)
     lines = both_cores(gather_x(sum_pieces(pieces)))
     grad_gate, grad_up, grad_down = widen(*sums)
-    lines[0], grad_down = tied(lines[0], grad_down)
     grad_q, grad_k, grad_v, grad_o, gain_a, gain_b, router = assemble(ids, lines)
     return (
         output,

time: 337 us -> 330 us (0.979)
    psum x1, waiting for transfers between devices: 4.94 us -> 0.55 us  [per_device(): sums = lax.psum((grad_w_gate, grad_w_up, grad_w_down), ('z', 'y'))]
  transfers between devices with their start and end apart: 45 -> 45, of which waited for: 20 -> 21; matrix products, arithmetic and copies ran while one was open for 5% -> 5% of each run, Pallas kernels for 37% -> 35%
where the time goes in v2:
time: 330 us; the launch traced here: 326 us
  Pallas kernels  123 us (37%)
  waiting for transfers between devices  104 us (32%)
  starting transfers between devices  58 us (18%)
  other arithmetic  16 us (5%)
  between operations  14.3 us (4%)
  local copies, waits for them, and re-layouts  10 us (3%)
    ppermute x18, waiting for transfers between devices, shift(): lax.ppermute(value, axis, [((i + amount) % size, i) for i in range(size)])  53.3 us
    pallas_call x1, Pallas kernels, experts(): pl.pallas_call(experts_body, grid=(2, 2), out_shape=(shape((2, 1536, 512)...  26.2 us
    pallas_call x2, Pallas kernels, by_chip(): pl.pallas_call(body, grid_spec=pltpu.PrefetchScalarGridSpec(num_scalar_pr...  20.5 us
    ppermute x18, starting transfers between devices, shift(): lax.ppermute(value, axis, [((i + amount) % size, i) for i in range(size)])  16.9 us
    pallas_call x1, Pallas kernels, attend_backward(): pl.pallas_call(attend_back_body, out_shape=(shape((1024, 384), bf16), sha...  16.6 us
    pallas_call x1, Pallas kernels, attend_forward(): pl.pallas_call(attend_body, out_shape=(shape((1024, 1536), bf16), shape((...  15.5 us
    all_to_all x1, waiting for transfers between devices, per_device(): grad_heads = lax.all_to_all(heads, ('x', 'core'), 0, 0, tiled=True)  14.9 us
    ppermute x19, starting transfers between devices, swap(): return lax.ppermute(value, 'core', [(0, 1), (1, 0)])  14.1 us
  transfers between devices with their start and end apart: 45, of which 21 were waited for; matrix products, arithmetic and copies ran while one was open for 5% of the time, Pallas kernels for 35%

profile of v2, /device:TPU:1, one launch (start us, length us, event | category | flops | bytes accessed | tf_op | source)
XLA Modules:
  0.0 325.7 jit_solution(3133723307807786871)
XLA Ops:
  16.4 7.8 %all-to-all-start = ((bf16[16,96,384]{2,1,0:T(8,128)(2,1)}), bf16[16,96,384]{2,1,0:T(8,128)(2,1)S(1)}, u32[]{:S(2)}, u32[]{:S(2)}) async-start(bf16[16,96,384]{2,1,0:T(8,128)(2,1)} %get-tuple-element.82), calls=%async_computation | async-start | bytes 2359296 | tf_op jit(solution)/shard_map/all_to_all | solution.py:772
  25.9 7.8 %collective-permute-done.1.refs_2_ = bf16[128,1664]{1,0:T(8,128)(2,1)S(1)} collective-permute-done((bf16[128,1664]{1,0:T(8,128)(2,1)}, bf16[128,1664]{1,0:T(8,128)(2,1)S(1)}, u32[]{:S(2)}, u32[]{:S(2)}) %collective-permute-start.1) | collective-permute-done | bytes 426016 | tf_op jit(solution)/shard_map/ppermute | solution.py:692
  48.5 15.5 %attend_forward.1 = (bf16[1024,1536]{1,0:T(8,128)(2,1)}, f32[128,1536]{1,0:T(8,128)}, bf16[1024,128]{1,0:T(8,128)(2,1)}, bf16[1024,128]{1,0:T(8,128)(2,1)}, bf16...) custom-call(s32[8]{0:T(128)} %add.160.ids, ...), custom_call_target="tpu_custom_call" | custom-call | flops 14000000000 | bytes 12000000 | tf_op jit(solution)/shard_map/attend_forward/pallas_call | solution.py:130
  64.0 5.1 %all-to-all-start.1 = ((bf16[8,128,256]{2,1,0:T(8,128)(2,1)}), bf16[8,128,256]{2,1,0:T(8,128)(2,1)S(1)}, u32[]{:S(2)}, u32[]{:S(2)}) async-start(bf16[8,128,256]{2,1,0:T(8,128)(2,1)} %get-tuple-element.85), calls=%async_computation.1 | async-start | bytes 1048576 | tf_op jit(solution)/shard_map/all_to_all | solution.py:795
  70.1 8.5 %all-to-all-done.1.mixed = bf16[8,128,256]{2,1,0:T(8,128)(2,1)S(1)} async-done(((bf16[8,128,256]{2,1,0:T(8,128)(2,1)}), bf16[8,128,256]{2,1,0:T(8,128)(2,1)S(1)}, u32[]{:S(2)}, u32[]{:S(2)}) %all-to-all-start.1) | async-done | bytes 524320 | tf_op jit(solution)/shard_map/all_to_all | solution.py:795
  79.3 5.2 %project_out.1 = (bf16[128,1664]{1,0:T(8,128)(2,1)}, f32[128,1536]{1,0:T(8,128)}, f32[128,128]{1,0:T(8,128)}, bf16[128,1536]{1,0:T(8,128)(2,1)}) custom-call(bf16[8,128,256]{2,1,0:T(8,128)(2,1)} %copy-done.10, bf16[1536,1536]{1,0:T(8,128)(2,1)} %all-gather.3.cloned.1.call-done.w_out, bf16[128,1536]{1,0:T(8,128)(2,1)} %tokens.3, ...), custom_call_target="tpu_custom_call" | custom-call | flops 4000000000 | bytes 8000000 | tf_op jit(solution)/shard_map/project_out/pallas_call | solution.py:619
  88.1 7.7 %back_rows.1 = (bf16[1024,1536]{1,0:T(8,128)(2,1)}, bf16[1024,1024]{1,0:T(8,128)(2,1)}) custom-call(s32[8]{0:T(128)} %add.160.ids, bf16[128,1536]{1,0:T(8,128)(2,1)} %grads.1, bf16[128,1536]{1,0:T(8,128)(2,1)} %copy-done.34, bf16[128,1536]{1,0:T(8,128)(2,1)} %collective-permute-done.7.refs_2_, bf16[128,1536]{1,0:T(8,128)(2,1)} %copy-done.35, ...), custom_call_target="tpu_custom_call" | custom-call | flops 8000000000 | bytes 11000000 | tf_op jit(solution)/shard_map/back_rows/pallas_call | solution.py:437
  97.8 10.4 %collective-permute-done.16.refs_6_ = bf16[128,1664]{1,0:T(8,128)(2,1)S(1)} collective-permute-done((bf16[128,1664]{1,0:T(8,128)(2,1)}, bf16[128,1664]{1,0:T(8,128)(2,1)S(1)}, u32[]{:S(2)}, u32[]{:S(2)}) %collective-permute-start.16) | collective-permute-done | bytes 426016 | tf_op jit(solution)/shard_map/ppermute | solution.py:692
  112.9 26.2 %experts.1 = (bf16[2,1536,512]{2,1,0:T(8,128)(2,1)}, bf16[2,1536,512]{2,1,0:T(8,128)(2,1)}, bf16[2,512,1536]{2,1,0:T(8,128)(2,1)}, bf16[1024,1024]{1,0:T(8,128)(...) custom-call(s32[8]{0:T(128)} %add.160.ids, ...), custom_call_target="tpu_custom_call" | custom-call | flops 16000000000 | bytes 34000000 | tf_op jit(solution)/shard_map/experts/pallas_call | solution.py:301
  139.1 12.4 %experts_back.1 = (bf16[4,128,1664]{2,1,0:T(8,128)(2,1)}, bf16[4,128,1664]{2,1,0:T(8,128)(2,1)}) custom-call(s32[3]{0:T(128)} %pad_add_fusion.at.here, bf16[1024,1024]{1,0:T(8,128)(2,1)} %get-tuple-element.101.gg, bf16[1024,1024]{1,0:T(8,128)(2,1)} %get-tuple-element.102.gu, f32[1024,128]{1,0:T(8,128)} %get-tuple-element.103.routed, ...), custom_call_target="tpu_custom_call" | custom-call | flops 1000000 | bytes 100000 | tf_op jit(solution)/shard_map/experts_back/pallas_call | solution.py:338
  158.4 3.8 %all-to-all-start.2 = ((bf16[4,128,1664]{2,1,0:T(8,128)(2,1)}), bf16[4,128,1664]{2,1,0:T(8,128)(2,1)S(1)}, u32[]{:S(2)}, u32[]{:S(2)}) async-start(bf16[4,128,1664]{2,1,0:T(8,128)(2,1)} %add_convert_fusion), calls=%async_computation.2 | async-start | bytes 3407872 | tf_op jit(solution)/shard_map/all_to_all | solution.py:716
  162.2 8.1 %combine.1 = (bf16[4,128,1536]{2,1,0:T(8,128)(2,1)}, bf16[4,128,1536]{2,1,0:T(8,128)(2,1)}) custom-call(s32[3]{0:T(128)} %pad_add_fusion.at.here, bf16[1024,1024]{1,0:T(8,128)(2,1)} %get-tuple-element.107.aw, bf16[2,512,1536]{2,1,0:T(8,128)(2,1)} %down_w.1), custom_call_target="tpu_custom_call" | custom-call | flops 8000000000 | bytes 100000 | tf_op jit(solution)/shard_map/combine/pallas_call | solution.py:338
  170.3 13.7 %all-to-all-done.2.sums = bf16[4,128,1664]{2,1,0:T(8,128)(2,1)S(1)} async-done(((bf16[4,128,1664]{2,1,0:T(8,128)(2,1)}), bf16[4,128,1664]{2,1,0:T(8,128)(2,1)S(1)}, u32[]{:S(2)}, u32[]{:S(2)}) %all-to-all-start.2) | async-done | bytes 1703968 | tf_op jit(solution)/shard_map/all_to_all | solution.py:716
  185.2 7.1 %middle.1 = (f32[128,1536]{1,0:T(8,128)}, bf16[8,128,512]{2,1,0:T(8,128)(2,1)}, f32[1,1536]{1,0:T(1,128)}, f32[16,1536]{1,0:T(8,128)}) custom-call(bf16[1536,1536]{1,0:T(8,128)(2,1)} %all-gather.3.cloned.1.call-done.w_out, bf16[4,128,1664]{2,1,0:T(8,128)(2,1)} %copy-done.2, bf16[128,1536]{1,0:T(8,128)(2,1)} %grads.1, f32[128,1536]{1,0:T(8,128)} %get-tuple-element.112.hidden, ...), custom_call_target="tpu_custom_call" | custom-call | flops 1000000 | bytes 100000 | tf_op jit(solution)/shard_map/middle/pallas_call | solution.py:673
  192.4 4.6 %all-to-all-start.3 = ((bf16[8,128,512]{2,1,0:T(8,128)(2,1)}), bf16[8,128,512]{2,1,0:T(8,128)(2,1)S(1)}, u32[]{:S(2)}, u32[]{:S(2)}) async-start(bf16[8,128,512]{2,1,0:T(8,128)(2,1)} %get-tuple-element.114), calls=%async_computation.3 | async-start | bytes 2097152 | tf_op jit(solution)/shard_map/all_to_all | solution.py:821
  197.2 14.9 %all-to-all-done.3.gm.branch = bf16[8,128,512]{2,1,0:T(8,128)(2,1)S(1)} async-done(((bf16[8,128,512]{2,1,0:T(8,128)(2,1)}), bf16[8,128,512]{2,1,0:T(8,128)(2,1)S(1)}, u32[]{:S(2)}, u32[]{:S(2)}) %all-to-all-start.3) | async-done | bytes 1048608 | tf_op jit(solution)/shard_map/all_to_all | solution.py:821
  213.1 16.6 %attend_backward.1 = (bf16[1024,384]{1,0:T(8,128)(2,1)}, bf16[4,128,1536]{2,1,0:T(8,128)(2,1)}, bf16[4,128,1536]{2,1,0:T(8,128)(2,1)}, f32[1,1536]{1,0:T(1,128)}) custom-call(s32[3]{0:T(128)} %pad_add_fusion.at.here, bf16[1536,384]{1,0:T(8,128)(2,1)} %bitcast.34, bf16[8,128,512]{2,1,0:T(8,128)(2,1)} %copy-done, bf16[1024,128]{1,0:T(8,128)(2,1)} %get-tuple-element.115.q01, ...), custom_call_target="tpu_custom_call" | custom-call | flops 1000000 | bytes 100000 | tf_op jit(solution)/shard_map/attend_backward/pallas_call | solution.py:229
  234.7 7.6 %weight_grads.1 = bf16[16,112,512]{2,1,0:T(8,128)(2,1)} custom-call(bf16[1024,1536]{1,0:T(8,128)(2,1)} %get-tuple-element.110.normed, bf16[1024,384]{1,0:T(8,128)(2,1)} %get-tuple-element.122.grad_qkv, bf16[1024,1536]{1,0:T(8,128)(2,1)} %all-gather.5.cloned.1.call-done.mixed, bf16[8,128,512]{2,1,0:T(8,128)(2,1)} %copy-done, ...), custom_call_target="tpu_custom_call" | custom-call | flops 1000000 | bytes 100000 | tf_op jit(solution)/shard_map/weight_grads/pallas_call | solution.py:475
  242.3 5.6 %all-to-all-start.4 = ((bf16[16,112,512]{2,1,0:T(8,128)(2,1)}), bf16[16,112,512]{2,1,0:T(8,128)(2,1)S(1)}, u32[]{:S(2)}, u32[]{:S(2)}) async-start(bf16[16,112,512]{2,1,0:T(8,128)(2,1)} %weight_grads.1), calls=%async_computation.4 | async-start | bytes 3670016 | tf_op jit(solution)/shard_map/all_to_all | solution.py:841
  254.5 4.0 %collective-permute-done.25 = bf16[128,1536]{1,0:T(8,128)(2,1)S(1)} collective-permute-done((bf16[128,1536]{1,0:T(8,128)(2,1)S(1)}, bf16[128,1536]{1,0:T(8,128)(2,1)S(1)}, u32[]{:S(2)}, u32[]{:S(2)}) %collective-permute-start.25) | collective-permute-done | bytes 393248 | tf_op jit(solution)/shard_map/ppermute | solution.py:692
  259.5 8.6 %collective-permute-done.24 = bf16[128,1536]{1,0:T(8,128)(2,1)S(1)} collective-permute-done((bf16[128,1536]{1,0:T(8,128)(2,1)S(1)}, bf16[128,1536]{1,0:T(8,128)(2,1)S(1)}, u32[]{:S(2)}, u32[]{:S(2)}) %collective-permute-start.24) | collective-permute-done | bytes 393248 | tf_op jit(solution)/shard_map/ppermute | solution.py:692
  269.1 6.2 %collective-permute-done.29 = bf16[128,1536]{1,0:T(8,128)(2,1)S(1)} collective-permute-done((bf16[128,1536]{1,0:T(8,128)(2,1)S(1)}, bf16[128,1536]{1,0:T(8,128)(2,1)S(1)}, u32[]{:S(2)}, u32[]{:S(2)}) %collective-permute-start.29) | collective-permute-done | bytes 393248 | tf_op jit(solution)/shard_map/ppermute | solution.py:692
  275.4 10.3 %collective-permute-done.28 = bf16[128,1536]{1,0:T(8,128)(2,1)S(1)} collective-permute-done((bf16[128,1536]{1,0:T(8,128)(2,1)S(1)}, bf16[128,1536]{1,0:T(8,128)(2,1)S(1)}, u32[]{:S(2)}, u32[]{:S(2)}) %collective-permute-start.28) | collective-permute-done | bytes 393248 | tf_op jit(solution)/shard_map/ppermute | solution.py:692
  309.8 9.1 %widen.1 = (f32[2,1536,512]{2,1,0:T(8,128)}, f32[2,1536,512]{2,1,0:T(8,128)}, f32[2,512,1536]{2,1,0:T(8,128)}) custom-call(bf16[2,1536,512]{2,1,0:T(8,128)(2,1)} %get-tuple-element.150.a, bf16[2,1536,512]{2,1,0:T(8,128)(2,1)} %get-tuple-element.151.b, bf16[2,512,1536]{2,1,0:T(8,128)(2,1)} %get-tuple-element.152.c), custom_call_target="tpu_custom_call" | custom-call | flops 1000000 | bytes 28000000 | tf_op jit(solution)/shard_map/widen/pallas_call | solution.py:409
  (179 shorter events, 84.5 us)
Async XLA Ops:
  7.2 71.3 %all-gather.3.cloned.1.call-start = ((), (), s32[]{:S(2)}) async-start(), calls=%async_computation.5 | async-start | bytes 5013504 | tf_op jit(solution)/shard_map/all_gather | solution.py:771
  11.3 31.0 %collective-permute-start = (bf16[128,1664]{1,0:T(8,128)(2,1)}, bf16[128,1664]{1,0:T(8,128)(2,1)S(1)}, u32[]{:S(2)}, u32[]{:S(2)}) collective-permute-start(bf16[128,1664]{1,0:T(8,128)(2,1)} %get-tuple-element.80.refs_0_), channel_id=1, source_target_pairs={{0,1},{1,0},{2,3},{3,2},{4,5},{5,4},{6,7},{7,6},{8,9},{9,8},{10,11... | collective-permute-start | bytes 1277960 | tf_op jit(solution)/shard_map/ppermute | solution.py:696
  12.7 21.1 %collective-permute-start.1 = (bf16[128,1664]{1,0:T(8,128)(2,1)}, bf16[128,1664]{1,0:T(8,128)(2,1)S(1)}, u32[]{:S(2)}, u32[]{:S(2)}) collective-permute-start(bf16[128,1664]{1,0:T(8,128)(2,1)} %get-tuple-element.80.refs_0_), channel_id=1, source_target_pairs={{2,0},{4,2},{6,4},{0,6},{3,1},{5,3},{7,5},{1,7},{10,8},{12,10},{14... | collective-permute-start | bytes 1277960 | tf_op jit(solution)/shard_map/ppermute | solution.py:692
  15.3 19.5 %collective-permute-start.3 = (bf16[128,1664]{1,0:T(8,128)(2,1)}, bf16[128,1664]{1,0:T(8,128)(2,1)S(1)}, u32[]{:S(2)}, u32[]{:S(2)}) collective-permute-start(bf16[128,1664]{1,0:T(8,128)(2,1)} %get-tuple-element.80.refs_0_), channel_id=1, source_target_pairs={{4,0},{6,2},{0,4},{2,6},{5,1},{7,3},{1,5},{3,7},{12,8},{14,10},{8,... | collective-permute-start | bytes 1277960 | tf_op jit(solution)/shard_map/ppermute | solution.py:692
  15.8 22.2 %collective-permute-start.5 = (bf16[128,1664]{1,0:T(8,128)(2,1)}, bf16[128,1664]{1,0:T(8,128)(2,1)S(1)}, u32[]{:S(2)}, u32[]{:S(2)}) collective-permute-start(bf16[128,1664]{1,0:T(8,128)(2,1)} %get-tuple-element.80.refs_0_), channel_id=1, source_target_pairs={{6,0},{0,2},{2,4},{4,6},{7,1},{1,3},{3,5},{5,7},{14,8},{8,10},{10,... | collective-permute-start | bytes 1277960 | tf_op jit(solution)/shard_map/ppermute | solution.py:692
  16.4 31.0 %all-to-all-start = ((bf16[16,96,384]{2,1,0:T(8,128)(2,1)}), bf16[16,96,384]{2,1,0:T(8,128)(2,1)S(1)}, u32[]{:S(2)}, u32[]{:S(2)}) async-start(bf16[16,96,384]{2,1,0:T(8,128)(2,1)} %get-tuple-element.82), calls=%async_computation | async-start | bytes 2359296 | tf_op jit(solution)/shard_map/all_to_all | solution.py:772
  41.9 22.0 %collective-permute-start.7 = (bf16[128,1536]{1,0:T(8,128)(2,1)S(1)}, bf16[128,1536]{1,0:T(8,128)(2,1)}, u32[]{:S(2)}, u32[]{:S(2)}) collective-permute-start(bf16[128,1536]{1,0:T(8,128)(2,1)S(1)} %copy-done.11), channel_id=1, source_target_pairs={{2,0},{4,2},{6,4},{0,6},{3,1},{5,3},{7,5},{1,7},{10,8},{12,10},{14... | collective-permute-start | bytes 1179656 | tf_op jit(solution)/shard_map/ppermute | solution.py:692
  42.2 21.7 %collective-permute-start.8 = (bf16[128,1536]{1,0:T(8,128)(2,1)S(1)}, bf16[128,1536]{1,0:T(8,128)(2,1)}, u32[]{:S(2)}, u32[]{:S(2)}) collective-permute-start(bf16[128,1536]{1,0:T(8,128)(2,1)S(1)} %copy-done.11), channel_id=1, source_target_pairs={{4,0},{6,2},{0,4},{2,6},{5,1},{7,3},{1,5},{3,7},{12,8},{14,10},{8,... | collective-permute-start | bytes 1179656 | tf_op jit(solution)/shard_map/ppermute | solution.py:692
  42.8 21.2 %collective-permute-start.9 = (bf16[128,1536]{1,0:T(8,128)(2,1)S(1)}, bf16[128,1536]{1,0:T(8,128)(2,1)}, u32[]{:S(2)}, u32[]{:S(2)}) collective-permute-start(bf16[128,1536]{1,0:T(8,128)(2,1)S(1)} %copy-done.11), channel_id=1, source_target_pairs={{6,0},{0,2},{2,4},{4,6},{7,1},{1,3},{3,5},{5,7},{14,8},{8,10},{10,... | collective-permute-start | bytes 1179656 | tf_op jit(solution)/shard_map/ppermute | solution.py:692
  69.1 165.6 %all-gather.5.cloned.1.call-start = ((), (), s32[]{:S(2)}) async-start(), calls=%async_computation.6 | async-start | bytes 3538944 | tf_op jit(solution)/shard_map/all_gather | solution.py:804
  69.6 17.8 %collective-permute-start.14 = (bf16[128,1536]{1,0:T(8,128)(2,1)}, bf16[128,1536]{1,0:T(8,128)(2,1)S(1)}, u32[]{:S(2)}, u32[]{:S(2)}) collective-permute-start(bf16[128,1536]{1,0:T(8,128)(2,1)} %collective-permute-done.8.refs_4_), channel_id=1, source_target_pairs={{0,1},{1,0},{2,3},{3,2},{4,5},{5,4},{6,7},{7,6},{8,9},{9,8},{10,11... | collective-permute-start | bytes 1179656 | tf_op jit(solution)/shard_map/ppermute | solution.py:696
  69.7 17.6 %collective-permute-start.15 = (bf16[128,1536]{1,0:T(8,128)(2,1)}, bf16[128,1536]{1,0:T(8,128)(2,1)}, u32[]{:S(2)}, u32[]{:S(2)}) collective-permute-start(bf16[128,1536]{1,0:T(8,128)(2,1)} %collective-permute-done.9.refs_6_), channel_id=1, source_target_pairs={{0,1},{1,0},{2,3},{3,2},{4,5},{5,4},{6,7},{7,6},{8,9},{9,8},{10,11... | collective-permute-start | bytes 1179656 | tf_op jit(solution)/shard_map/ppermute | solution.py:696
  86.7 21.5 %collective-permute-start.16 = (bf16[128,1664]{1,0:T(8,128)(2,1)}, bf16[128,1664]{1,0:T(8,128)(2,1)S(1)}, u32[]{:S(2)}, u32[]{:S(2)}) collective-permute-start(bf16[128,1664]{1,0:T(8,128)(2,1)} %get-tuple-element.95.refs_0_), channel_id=1, source_target_pairs={{6,0},{0,2},{2,4},{4,6},{7,1},{1,3},{3,5},{5,7},{14,8},{8,10},{10,... | collective-permute-start | bytes 1277960 | tf_op jit(solution)/shard_map/ppermute | solution.py:692
  108.3 201.6 %all-reduce.3.cloned.1.call-start = ((), (), s32[]{:S(2)}) async-start(), calls=%async_computation.7 | async-start | bytes 18874368 | tf_op jit(solution)/shard_map/psum | solution.py:809
  158.4 25.6 %all-to-all-start.2 = ((bf16[4,128,1664]{2,1,0:T(8,128)(2,1)}), bf16[4,128,1664]{2,1,0:T(8,128)(2,1)S(1)}, u32[]{:S(2)}, u32[]{:S(2)}) async-start(bf16[4,128,1664]{2,1,0:T(8,128)(2,1)} %add_convert_fusion), calls=%async_computation.2 | async-start | bytes 3407872 | tf_op jit(solution)/shard_map/all_to_all | solution.py:716
  192.4 19.8 %all-to-all-start.3 = ((bf16[8,128,512]{2,1,0:T(8,128)(2,1)}), bf16[8,128,512]{2,1,0:T(8,128)(2,1)S(1)}, u32[]{:S(2)}, u32[]{:S(2)}) async-start(bf16[8,128,512]{2,1,0:T(8,128)(2,1)} %get-tuple-element.114), calls=%async_computation.3 | async-start | bytes 2097152 | tf_op jit(solution)/shard_map/all_to_all | solution.py:821
  197.0 34.7 %collective-permute-start.22 = (bf16[4,128,1536]{2,1,0:T(8,128)(2,1)}, bf16[4,128,1536]{2,1,0:T(8,128)(2,1)}, u32[]{:S(2)}, u32[]{:S(2)}) collective-permute-start(bf16[4,128,1536]{2,1,0:T(8,128)(2,1)} %get-tuple-element.109), channel_id=1, source_target_pairs={{0,1},{1,0},{2,3},{3,2},{4,5},{5,4},{6,7},{7,6},{8,9},{9,8},{10,11... | collective-permute-start | bytes 4718600 | tf_op jit(solution)/shard_map/ppermute | solution.py:696
  229.7 20.7 %collective-permute-start.26 = (bf16[4,128,1536]{2,1,0:T(8,128)(2,1)}, bf16[4,128,1536]{2,1,0:T(8,128)(2,1)}, u32[]{:S(2)}, u32[]{:S(2)}) collective-permute-start(bf16[4,128,1536]{2,1,0:T(8,128)(2,1)} %get-tuple-element.131), channel_id=1, source_target_pairs={{0,1},{1,0},{2,3},{3,2},{4,5},{5,4},{6,7},{7,6},{8,9},{9,8},{10,11... | collective-permute-start | bytes 4718600 | tf_op jit(solution)/shard_map/ppermute | solution.py:696
  242.3 47.7 %all-to-all-start.4 = ((bf16[16,112,512]{2,1,0:T(8,128)(2,1)}), bf16[16,112,512]{2,1,0:T(8,128)(2,1)S(1)}, u32[]{:S(2)}, u32[]{:S(2)}) async-start(bf16[16,112,512]{2,1,0:T(8,128)(2,1)} %weight_grads.1), calls=%async_computation.4 | async-start | bytes 3670016 | tf_op jit(solution)/shard_map/all_to_all | solution.py:841
  249.1 19.0 %collective-permute-start.24 = (bf16[128,1536]{1,0:T(8,128)(2,1)S(1)}, bf16[128,1536]{1,0:T(8,128)(2,1)S(1)}, u32[]{:S(2)}, u32[]{:S(2)}) collective-permute-start(bf16[128,1536]{1,0:T(8,128)(2,1)S(1)} %get-tuple-element.158), channel_id=1, source_target_pairs={{6,0},{0,2},{2,4},{4,6},{7,1},{1,3},{3,5},{5,7},{14,8},{8,10},{10,... | collective-permute-start | bytes 1179656 | tf_op jit(solution)/shard_map/ppermute | solution.py:692
  249.6 18.5 %collective-permute-start.23 = (bf16[128,1536]{1,0:T(8,128)(2,1)S(1)}, bf16[128,1536]{1,0:T(8,128)(2,1)S(1)}, u32[]{:S(2)}, u32[]{:S(2)}) collective-permute-start(bf16[128,1536]{1,0:T(8,128)(2,1)S(1)} %get-tuple-element.156), channel_id=1, source_target_pairs={{4,0},{6,2},{0,4},{2,6},{5,1},{7,3},{1,5},{3,7},{12,8},{14,10},{8,... | collective-permute-start | bytes 1179656 | tf_op jit(solution)/shard_map/ppermute | solution.py:692
  252.4 23.0 %collective-permute-start.29 = (bf16[128,1536]{1,0:T(8,128)(2,1)S(1)}, bf16[128,1536]{1,0:T(8,128)(2,1)S(1)}, u32[]{:S(2)}, u32[]{:S(2)}) collective-permute-start(bf16[128,1536]{1,0:T(8,128)(2,1)S(1)} %get-tuple-element.154), channel_id=1, source_target_pairs={{2,0},{4,2},{6,4},{0,6},{3,1},{5,3},{7,5},{1,7},{10,8},{12,10},{14... | collective-permute-start | bytes 1179656 | tf_op jit(solution)/shard_map/ppermute | solution.py:692
  254.4 31.2 %collective-permute-start.28 = (bf16[128,1536]{1,0:T(8,128)(2,1)S(1)}, bf16[128,1536]{1,0:T(8,128)(2,1)S(1)}, u32[]{:S(2)}, u32[]{:S(2)}) collective-permute-start(bf16[128,1536]{1,0:T(8,128)(2,1)S(1)} %get-tuple-element.155), channel_id=1, source_target_pairs={{6,0},{0,2},{2,4},{4,6},{7,1},{1,3},{3,5},{5,7},{14,8},{8,10},{10,... | collective-permute-start | bytes 1179656 | tf_op jit(solution)/shard_map/ppermute | solution.py:692
  258.5 27.2 %collective-permute-start.27 = (bf16[128,1536]{1,0:T(8,128)(2,1)S(1)}, bf16[128,1536]{1,0:T(8,128)(2,1)S(1)}, u32[]{:S(2)}, u32[]{:S(2)}) collective-permute-start(bf16[128,1536]{1,0:T(8,128)(2,1)S(1)} %get-tuple-element.153), channel_id=1, source_target_pairs={{4,0},{6,2},{0,4},{2,6},{5,1},{7,3},{1,5},{3,7},{12,8},{14,10},{8,... | collective-permute-start | bytes 1179656 | tf_op jit(solution)/shard_map/ppermute | solution.py:692
  (58 other events, 444.7 us)
Sparse Core Ops, SparseCore 0:
  10.2 67.8 all-gather.2
  108.4 26.7 all-gather.4
  139.9 169.8 all-reduce.2

commit v3 on v2

--- a/solution.py
+++ b/solution.py
@@ -157,9 +157,12 @@
 
 
 def attend_back_body(
-    here, w, gm, q01, q2k, val, lse, cc, ss, starts, normed, narrow,
-    dqkv, own, other, grad_gain, ka, kb, vb, kt, do01, do2, dk, dv, d01, dq2,
+    here, w, gm, q01, q2k, val, lse, cc, ss, starts, normed_hbm, narrow,
+    dqkv, own_hbm, other_hbm, grad_gain, ka, kb, vb, kt, do01, do2, dk, dv, d01, dq2,
+    normed, own, other, got, sent,
 ):
+    load = pltpu.make_async_copy(normed_hbm, normed, got)
+    load.start()
     k = high_half(q2k[...].astype(f32)) * score_scale
     kb[...] = k.astype(bf16)
     k_low = pltpu.roll(k, 64, 1)
@@ -168,7 +171,7 @@
     vb[...] = pltpu.roll(val[...].astype(f32), 64, 1).astype(bf16)
     for b in range(8):
         do01[b * 128 : (b + 1) * 128, :] = gm[b, :, 0:128]
-        do2[b * 128 : (b + 1) * 128, :] = gm[b, :, 128:256]
+        do2[b * 128 : (b + 1) * 128, :] = low_half(gm[b, :, 128:256])
     dk[...] = jnp.zeros_like(dk)
     dv[...] = jnp.zeros_like(dv)
 
@@ -196,6 +199,14 @@
         d01[at, :] = out[:, 0:128]
         dq2[at, :] = out[:, 128:256]
 
+    load.wait()
+
+    def store(c):
+        return (
+            pltpu.make_async_copy(own.at[c], own_hbm.at[c], sent.at[0, c]),
+            pltpu.make_async_copy(other.at[c], other_hbm.at[c], sent.at[1, c]),
+        )
+
     def finish(c, total):
         at = pl.ds(pl.multiple_of(c * 256, 256), 256)
         dkk = dk[at, :]
@@ -215,14 +226,20 @@
         low = whole.astype(bf16)
         own[c] = jnp.where(here[1] == 0, low[0:128], low[128:256])
         other[c] = jnp.where(here[1] == 0, low[128:256], low[0:128])
+        for copy in store(c):
+            copy.start()
         return total
 
     total = lax.fori_loop(0, 4, finish, jnp.zeros((1, 1536), f32))
     grad_gain[...] = total / narrow[64:65, :]
+    for c in range(4):
+        for copy in store(c):
+            copy.wait()
 
 
 def attend_backward(here, gm, q01, q2k, val, lse, cc, ss, starts, normed, w, narrow):
-    vm = pl.BlockSpec(memory_space=pltpu.VMEM)
+    vm, hbm = pl.BlockSpec(memory_space=pltpu.VMEM), pl.BlockSpec(memory_space=pl.ANY)
+    rows = pltpu.VMEM((4, 128, 1536), bf16)
     shape = jax.ShapeDtypeStruct
     half = pltpu.VMEM((1024, 128), bf16)
     full = pltpu.VMEM((1024, 128), f32)
@@ -234,10 +251,12 @@
             shape((4, 128, 1536), bf16),
             shape((1, 1536), f32),
         ),
-        in_specs=[pl.BlockSpec(memory_space=pltpu.SMEM)] + [vm] * 11,
-        out_specs=(vm,) * 4,
+        in_specs=[pl.BlockSpec(memory_space=pltpu.SMEM)] + [vm] * 9 + [hbm, vm],
+        out_specs=(vm, hbm, hbm, vm),
         scratch_shapes=[
             half, half, half, pltpu.VMEM((128, 1024), bf16), half, half, full, full, full, full,
+            pltpu.VMEM((1024, 1536), bf16), rows, rows,
+            pltpu.SemaphoreType.DMA, pltpu.SemaphoreType.DMA((2, 4)),
         ],
         compiler_params=pltpu.CompilerParams(vmem_limit_bytes=56 * MIB),
         cost_estimate=pl.CostEstimate(flops=1_000_000, bytes_accessed=100_000, transcendentals=0),
@@ -450,9 +469,9 @@
 
 def weight_body(normed, grad_qkv, mixed, branch, gain_a, gain_b, router, out):
     first = mm(normed[...].T, grad_qkv[...])
-    cols = jnp.concatenate([branch[b, :, 256:512] for b in range(8)], axis=0)
+    cols = jnp.concatenate([branch[b, :, 192:384] for b in range(8)], axis=0)
     second = mm(mixed[...].T, cols)
-    last = jnp.concatenate([first[:, 256:320], second[:, 0:192]], axis=1)
+    last = jnp.concatenate([first[:, 256:320], second], axis=1)
     zero = jnp.zeros((1, 32), f32)
     for y in range(4):
         rows, lanes = slice(96 * y, 96 * (y + 1)), slice(96 * y, 96 * (y + 1))
@@ -660,11 +679,10 @@
     grad_hidden[...] = gh
     low = (residual_scale * gh).astype(bf16)
     gx[...] = mm_nt(low, w_out[...])
-    zero = jnp.zeros((128, 64), f32)
     low = low.astype(f32)
     for j in range(8):
         cols = slice(192 * j, 192 * (j + 1))
-        heads[j] = jnp.concatenate([gx[:, cols], zero, low[:, cols], zero], axis=1).astype(bf16)
+        heads[j] = jnp.concatenate([gx[:, cols], low[:, cols]], axis=1).astype(bf16)
 
 
 def middle(w_out, sums, grads, hidden, gates, narrow, held):
@@ -674,7 +692,7 @@
         middle_body,
         out_shape=(
             shape((128, 1536), f32),
-            shape((8, 128, 512), bf16),
+            shape((8, 128, 384), bf16),
             shape((1, 1536), f32),
             shape((16, 1536), f32),
         ),
@@ -798,9 +816,9 @@
     )
     far_two = gather_x(sent_two)
     grad_all, back = back_rows(ids, grad_blocks, expert_down)
-    far_two[2], back = tied(far_two[2], back)
-    mixed, *far_two = tied(mixed, *far_two)
-    second_blocks = both_cores(far_two)
+    twins = [swap(block) for block in far_two]
+    mixed, back, *far_two = tied(mixed, back, *far_two)
+    second_blocks = [each for pair in zip(far_two, twins) for each in pair]
     mixed_all = lax.all_gather(mixed, ("x", "core"), axis=0, tiled=True)
 
     grad_w_gate, grad_w_up, grad_w_down, weighted, grad_gate_pre, grad_up_pre, routed = experts(
@@ -819,14 +837,14 @@
         out_all, terms, out_grad, hidden, gates, narrow, own_out
     )
     grad_heads = lax.all_to_all(heads, ("x", "core"), 0, 0, tiled=True)
-    near_out = near_sum(own_out, other_out)
     grad_qkv, own, other, grad_gain_one = attend_backward(
         at, grad_heads, q01, q2k, val, lse, cos, sin, starts, normed, qkv_w, narrow
     )
     table = weight_grads(
         normed, grad_qkv, mixed_all, grad_heads, grad_gain_one, grad_gain_two, grad_router
     )
-    near_out, table = tied(near_out, table)
+    own_out, table = tied(own_out, table)
+    near_out = near_sum(own_out, other_out)
     output = (hidden + residual_scale * total_of(exchange_apart(near_out))).astype(bf16)
     normed_mine = total_of(exchange_apart(near_sum(own, other)))
     inputs = tokens.astype(f32)

time: 330 us -> 325 us (0.985)
  blocking collectives: 0 us -> 17.6 us
  waiting for transfers between devices: 104 us -> 88.7 us
  starting transfers between devices: 58 us -> 53.2 us
    all_to_all x0 -> x1, blocking collectives: none -> 17.6 us  [per_device(): grad_heads = lax.all_to_all(heads, ('x', 'core'), 0, 0, tiled=True)]
    all_to_all x1 -> x0, waiting for transfers between devices: 14.9 us -> none  [per_device(): grad_heads = lax.all_to_all(heads, ('x', 'core'), 0, 0, tiled=True)]
    all_to_all x1 -> x0, starting transfers between devices: 4.64 us -> none  [per_device(): grad_heads = lax.all_to_all(heads, ('x', 'core'), 0, 0, tiled=True)]
    unnamed x75 -> x71, local copies, waits for them, and re-layouts: 8.37 us -> 7.35 us
  transfers between devices with their start and end apart: 45 -> 44, of which waited for: 21 -> 19; matrix products, arithmetic and copies ran while one was open for 5% -> 5% of each run, Pallas kernels for 35% -> 35%
where the time goes in v3:
time: 325 us; the launch traced here: 320 us
  Pallas kernels  123 us (38%)
  waiting for transfers between devices  88.7 us (27%)
  starting transfers between devices  53.2 us (16%)
  blocking collectives  17.6 us (5%)
  other arithmetic  14.7 us (5%)
  between operations  14.4 us (4%)
  local copies, waits for them, and re-layouts  8.99 us (3%)
    ppermute x18, waiting for transfers between devices, shift(): lax.ppermute(value, axis, [((i + amount) % size, i) for i in range(size)])  52.9 us
    pallas_call x1, Pallas kernels, experts(): pl.pallas_call(experts_body, grid=(2, 2), out_shape=(shape((2, 1536, 512)...  26.2 us
    pallas_call x2, Pallas kernels, by_chip(): pl.pallas_call(body, grid_spec=pltpu.PrefetchScalarGridSpec(num_scalar_pr...  20.6 us
    all_to_all x1, blocking collectives, per_device(): grad_heads = lax.all_to_all(heads, ('x', 'core'), 0, 0, tiled=True)  17.6 us
    pallas_call x1, Pallas kernels, attend_backward(): pl.pallas_call(attend_back_body, out_shape=(shape((1024, 384), bf16), sha...  15.7 us
    pallas_call x1, Pallas kernels, attend_forward(): pl.pallas_call(attend_body, out_shape=(shape((1024, 1536), bf16), shape((...  15.5 us
    ppermute x18, starting transfers between devices, shift(): lax.ppermute(value, axis, [((i + amount) % size, i) for i in range(size)])  15.4 us
    ppermute x19, starting transfers between devices, swap(): return lax.ppermute(value, 'core', [(0, 1), (1, 0)])  15.3 us
  transfers between devices with their start and end apart: 44, of which 19 were waited for; matrix products, arithmetic and copies ran while one was open for 5% of the time, Pallas kernels for 35%

profile of v3, /device:TPU:1, one launch (start us, length us, event | category | flops | bytes accessed | tf_op | source)
XLA Modules:
  0.0 320.2 jit_solution(5254587469355226738)
XLA Ops:
  16.4 7.8 %all-to-all-start = ((bf16[16,96,384]{2,1,0:T(8,128)(2,1)}), bf16[16,96,384]{2,1,0:T(8,128)(2,1)S(1)}, u32[]{:S(2)}, u32[]{:S(2)}) async-start(bf16[16,96,384]{2,1,0:T(8,128)(2,1)} %get-tuple-element.81), calls=%async_computation | async-start | bytes 2359296 | tf_op jit(solution)/shard_map/all_to_all | solution.py:790
  25.9 7.8 %collective-permute-done.1.refs_2_ = bf16[128,1664]{1,0:T(8,128)(2,1)S(1)} collective-permute-done((bf16[128,1664]{1,0:T(8,128)(2,1)}, bf16[128,1664]{1,0:T(8,128)(2,1)S(1)}, u32[]{:S(2)}, u32[]{:S(2)}) %collective-permute-start.1) | collective-permute-done | bytes 426016 | tf_op jit(solution)/shard_map/ppermute | solution.py:710
  48.5 15.5 %attend_forward.1 = (bf16[1024,1536]{1,0:T(8,128)(2,1)}, f32[128,1536]{1,0:T(8,128)}, bf16[1024,128]{1,0:T(8,128)(2,1)}, bf16[1024,128]{1,0:T(8,128)(2,1)}, bf16...) custom-call(s32[8]{0:T(128)} %add.160.ids, ...), custom_call_target="tpu_custom_call" | custom-call | flops 14000000000 | bytes 12000000 | tf_op jit(solution)/shard_map/attend_forward/pallas_call | solution.py:130
  64.0 5.1 %all-to-all-start.1 = ((bf16[8,128,256]{2,1,0:T(8,128)(2,1)}), bf16[8,128,256]{2,1,0:T(8,128)(2,1)S(1)}, u32[]{:S(2)}, u32[]{:S(2)}) async-start(bf16[8,128,256]{2,1,0:T(8,128)(2,1)} %get-tuple-element.84), calls=%async_computation.1 | async-start | bytes 1048576 | tf_op jit(solution)/shard_map/all_to_all | solution.py:813
  70.1 8.5 %all-to-all-done.1.mixed = bf16[8,128,256]{2,1,0:T(8,128)(2,1)S(1)} async-done(((bf16[8,128,256]{2,1,0:T(8,128)(2,1)}), bf16[8,128,256]{2,1,0:T(8,128)(2,1)S(1)}, u32[]{:S(2)}, u32[]{:S(2)}) %all-to-all-start.1) | async-done | bytes 524320 | tf_op jit(solution)/shard_map/all_to_all | solution.py:813
  79.4 5.2 %project_out.1 = (bf16[128,1664]{1,0:T(8,128)(2,1)}, f32[128,1536]{1,0:T(8,128)}, f32[128,128]{1,0:T(8,128)}, bf16[128,1536]{1,0:T(8,128)(2,1)}) custom-call(bf16[8,128,256]{2,1,0:T(8,128)(2,1)} %copy-done.8, bf16[1536,1536]{1,0:T(8,128)(2,1)} %all-gather.3.cloned.1.call-done.w_out, bf16[128,1536]{1,0:T(8,128)(2,1)} %tokens.3, ...), custom_call_target="tpu_custom_call" | custom-call | flops 4000000000 | bytes 8000000 | tf_op jit(solution)/shard_map/project_out/pallas_call | solution.py:638
  88.1 7.7 %back_rows.1 = (bf16[1024,1536]{1,0:T(8,128)(2,1)}, bf16[1024,1024]{1,0:T(8,128)(2,1)}) custom-call(s32[8]{0:T(128)} %add.160.ids, bf16[128,1536]{1,0:T(8,128)(2,1)} %grads.1, bf16[128,1536]{1,0:T(8,128)(2,1)} %copy-done.32, bf16[128,1536]{1,0:T(8,128)(2,1)} %collective-permute-done.7.refs_2_, bf16[128,1536]{1,0:T(8,128)(2,1)} %copy-done.33, ...), custom_call_target="tpu_custom_call" | custom-call | flops 8000000000 | bytes 11000000 | tf_op jit(solution)/shard_map/back_rows/pallas_call | solution.py:456
  97.7 10.5 %collective-permute-done.16.refs_6_ = bf16[128,1664]{1,0:T(8,128)(2,1)S(1)} collective-permute-done((bf16[128,1664]{1,0:T(8,128)(2,1)}, bf16[128,1664]{1,0:T(8,128)(2,1)S(1)}, u32[]{:S(2)}, u32[]{:S(2)}) %collective-permute-start.16) | collective-permute-done | bytes 426016 | tf_op jit(solution)/shard_map/ppermute | solution.py:710
  112.8 26.2 %experts.1 = (bf16[2,1536,512]{2,1,0:T(8,128)(2,1)}, bf16[2,1536,512]{2,1,0:T(8,128)(2,1)}, bf16[2,512,1536]{2,1,0:T(8,128)(2,1)}, bf16[1024,1024]{1,0:T(8,128)(...) custom-call(s32[8]{0:T(128)} %add.160.ids, ...), custom_call_target="tpu_custom_call" | custom-call | flops 16000000000 | bytes 34000000 | tf_op jit(solution)/shard_map/experts/pallas_call | solution.py:320
  139.0 12.4 %experts_back.1 = (bf16[4,128,1664]{2,1,0:T(8,128)(2,1)}, bf16[4,128,1664]{2,1,0:T(8,128)(2,1)}) custom-call(s32[3]{0:T(128)} %pad_add_fusion.at.here, bf16[1024,1024]{1,0:T(8,128)(2,1)} %get-tuple-element.99.gg, bf16[1024,1024]{1,0:T(8,128)(2,1)} %get-tuple-element.100.gu, f32[1024,128]{1,0:T(8,128)} %get-tuple-element.101.routed, ...), custom_call_target="tpu_custom_call" | custom-call | flops 1000000 | bytes 100000 | tf_op jit(solution)/shard_map/experts_back/pallas_call | solution.py:357
  151.8 3.4 %collective-permute-done.21 = bf16[4,128,1664]{2,1,0:T(8,128)(2,1)S(1)} collective-permute-done((bf16[4,128,1664]{2,1,0:T(8,128)(2,1)}, bf16[4,128,1664]{2,1,0:T(8,128)(2,1)S(1)}, u32[]{:S(2)}, u32[]{:S(2)}) %collective-permute-start.21) | collective-permute-done | bytes 1703968 | tf_op jit(solution)/shard_map/ppermute | solution.py:714
  158.3 3.6 %all-to-all-start.2 = ((bf16[4,128,1664]{2,1,0:T(8,128)(2,1)}), bf16[4,128,1664]{2,1,0:T(8,128)(2,1)S(1)}, u32[]{:S(2)}, u32[]{:S(2)}) async-start(bf16[4,128,1664]{2,1,0:T(8,128)(2,1)} %add_convert_fusion), calls=%async_computation.2 | async-start | bytes 3407872 | tf_op jit(solution)/shard_map/all_to_all | solution.py:734
  161.9 8.2 %combine.1 = (bf16[4,128,1536]{2,1,0:T(8,128)(2,1)}, bf16[4,128,1536]{2,1,0:T(8,128)(2,1)}) custom-call(s32[3]{0:T(128)} %pad_add_fusion.at.here, bf16[1024,1024]{1,0:T(8,128)(2,1)} %get-tuple-element.105.aw, bf16[2,512,1536]{2,1,0:T(8,128)(2,1)} %down_w.1), custom_call_target="tpu_custom_call" | custom-call | flops 8000000000 | bytes 100000 | tf_op jit(solution)/shard_map/combine/pallas_call | solution.py:357
  170.6 13.2 %all-to-all-done.2.sums = bf16[4,128,1664]{2,1,0:T(8,128)(2,1)S(1)} async-done(((bf16[4,128,1664]{2,1,0:T(8,128)(2,1)}), bf16[4,128,1664]{2,1,0:T(8,128)(2,1)S(1)}, u32[]{:S(2)}, u32[]{:S(2)}) %all-to-all-start.2) | async-done | bytes 1703968 | tf_op jit(solution)/shard_map/all_to_all | solution.py:734
  185.0 7.0 %middle.1 = (f32[128,1536]{1,0:T(8,128)}, bf16[8,128,384]{2,1,0:T(8,128)(2,1)}, f32[1,1536]{1,0:T(1,128)}, f32[16,1536]{1,0:T(8,128)}) custom-call(bf16[1536,1536]{1,0:T(8,128)(2,1)} %all-gather.3.cloned.1.call-done.w_out, bf16[4,128,1664]{2,1,0:T(8,128)(2,1)} %copy-done.1, bf16[128,1536]{1,0:T(8,128)(2,1)} %grads.1, f32[128,1536]{1,0:T(8,128)} %get-tuple-element.109.hidden, ...), custom_call_target="tpu_custom_call" | custom-call | flops 1000000 | bytes 100000 | tf_op jit(solution)/shard_map/middle/pallas_call | solution.py:691
  192.0 17.6 %all_to_all.25.gm.branch = bf16[8,128,384]{2,1,0:T(8,128)(2,1)} all-to-all(bf16[8,128,384]{2,1,0:T(8,128)(2,1)} %get-tuple-element.111), channel_id=1, replica_groups=mesh['z'=4,'y'=4,'x'=4,'core'=2] {'x','core'}, dimensions={0} | all-to-all | bytes 1572864 | tf_op jit(solution)/shard_map/all_to_all | solution.py:839
  209.6 15.7 %attend_backward.1 = (bf16[1024,384]{1,0:T(8,128)(2,1)}, bf16[4,128,1536]{2,1,0:T(8,128)(2,1)}, bf16[4,128,1536]{2,1,0:T(8,128)(2,1)}, f32[1,1536]{1,0:T(1,128)}) custom-call(s32[3]{0:T(128)} %pad_add_fusion.at.here, bf16[1536,384]{1,0:T(8,128)(2,1)} %bitcast.34, bf16[8,128,384]{2,1,0:T(8,128)(2,1)} %all_to_all.25.gm.branch, ...), custom_call_target="tpu_custom_call" | custom-call | flops 1000000 | bytes 100000 | tf_op jit(solution)/shard_map/attend_backward/pallas_call | solution.py:246
  227.3 7.9 %weight_grads.1 = bf16[16,112,512]{2,1,0:T(8,128)(2,1)} custom-call(bf16[1024,1536]{1,0:T(8,128)(2,1)} %get-tuple-element.107.normed_hbm.normed, bf16[1024,384]{1,0:T(8,128)(2,1)} %get-tuple-element.119.grad_qkv, bf16[1024,1536]{1,0:T(8,128)(2,1)} %all-gather.5.cloned.1.call-done.mixed, bf16[8,128,384]{2,1,0:T(8,128)(2,1)} %all_to_all.25.gm.branch, ...), custom_call_target="tpu_custom_call" | custom-call | flops 1000000 | bytes 100000 | tf_op jit(solution)/shard_map/weight_grads/pallas_call | solution.py:494
  235.1 6.0 %all-to-all-start.4 = ((bf16[16,112,512]{2,1,0:T(8,128)(2,1)}), bf16[16,112,512]{2,1,0:T(8,128)(2,1)S(1)}, u32[]{:S(2)}, u32[]{:S(2)}) async-start(bf16[16,112,512]{2,1,0:T(8,128)(2,1)} %weight_grads.1), calls=%async_computation.4 | async-start | bytes 3670016 | tf_op jit(solution)/shard_map/all_to_all | solution.py:859
  249.4 4.2 %collective-permute-done.25 = bf16[128,1536]{1,0:T(8,128)(2,1)S(1)} collective-permute-done((bf16[128,1536]{1,0:T(8,128)(2,1)S(1)}, bf16[128,1536]{1,0:T(8,128)(2,1)S(1)}, u32[]{:S(2)}, u32[]{:S(2)}) %collective-permute-start.25) | collective-permute-done | bytes 393248 | tf_op jit(solution)/shard_map/ppermute | solution.py:710
  254.5 8.8 %collective-permute-done.24 = bf16[128,1536]{1,0:T(8,128)(2,1)S(1)} collective-permute-done((bf16[128,1536]{1,0:T(8,128)(2,1)S(1)}, bf16[128,1536]{1,0:T(8,128)(2,1)S(1)}, u32[]{:S(2)}, u32[]{:S(2)}) %collective-permute-start.24) | collective-permute-done | bytes 393248 | tf_op jit(solution)/shard_map/ppermute | solution.py:710
  264.3 6.3 %collective-permute-done.29 = bf16[128,1536]{1,0:T(8,128)(2,1)S(1)} collective-permute-done((bf16[128,1536]{1,0:T(8,128)(2,1)S(1)}, bf16[128,1536]{1,0:T(8,128)(2,1)S(1)}, u32[]{:S(2)}, u32[]{:S(2)}) %collective-permute-start.29) | collective-permute-done | bytes 393248 | tf_op jit(solution)/shard_map/ppermute | solution.py:710
  270.5 10.1 %collective-permute-done.28 = bf16[128,1536]{1,0:T(8,128)(2,1)S(1)} collective-permute-done((bf16[128,1536]{1,0:T(8,128)(2,1)S(1)}, bf16[128,1536]{1,0:T(8,128)(2,1)S(1)}, u32[]{:S(2)}, u32[]{:S(2)}) %collective-permute-start.28) | collective-permute-done | bytes 393248 | tf_op jit(solution)/shard_map/ppermute | solution.py:710
  304.2 9.1 %widen.1 = (f32[2,1536,512]{2,1,0:T(8,128)}, f32[2,1536,512]{2,1,0:T(8,128)}, f32[2,512,1536]{2,1,0:T(8,128)}) custom-call(bf16[2,1536,512]{2,1,0:T(8,128)(2,1)} %get-tuple-element.148.a, bf16[2,1536,512]{2,1,0:T(8,128)(2,1)} %get-tuple-element.149.b, bf16[2,512,1536]{2,1,0:T(8,128)(2,1)} %get-tuple-element.150.c), custom_call_target="tpu_custom_call" | custom-call | flops 1000000 | bytes 28000000 | tf_op jit(solution)/shard_map/widen/pallas_call | solution.py:428
  (174 shorter events, 78.2 us)
Async XLA Ops:
  7.2 71.4 %all-gather.3.cloned.1.call-start = ((), (), s32[]{:S(2)}) async-start(), calls=%async_computation.5 | async-start | bytes 5013504 | tf_op jit(solution)/shard_map/all_gather | solution.py:789
  11.3 31.0 %collective-permute-start = (bf16[128,1664]{1,0:T(8,128)(2,1)}, bf16[128,1664]{1,0:T(8,128)(2,1)S(1)}, u32[]{:S(2)}, u32[]{:S(2)}) collective-permute-start(bf16[128,1664]{1,0:T(8,128)(2,1)} %get-tuple-element.79.refs_0_), channel_id=1, source_target_pairs={{0,1},{1,0},{2,3},{3,2},{4,5},{5,4},{6,7},{7,6},{8,9},{9,8},{10,11... | collective-permute-start | bytes 1277960 | tf_op jit(solution)/shard_map/ppermute | solution.py:714
  12.7 21.0 %collective-permute-start.1 = (bf16[128,1664]{1,0:T(8,128)(2,1)}, bf16[128,1664]{1,0:T(8,128)(2,1)S(1)}, u32[]{:S(2)}, u32[]{:S(2)}) collective-permute-start(bf16[128,1664]{1,0:T(8,128)(2,1)} %get-tuple-element.79.refs_0_), channel_id=1, source_target_pairs={{2,0},{4,2},{6,4},{0,6},{3,1},{5,3},{7,5},{1,7},{10,8},{12,10},{14... | collective-permute-start | bytes 1277960 | tf_op jit(solution)/shard_map/ppermute | solution.py:710
  15.3 19.5 %collective-permute-start.3 = (bf16[128,1664]{1,0:T(8,128)(2,1)}, bf16[128,1664]{1,0:T(8,128)(2,1)S(1)}, u32[]{:S(2)}, u32[]{:S(2)}) collective-permute-start(bf16[128,1664]{1,0:T(8,128)(2,1)} %get-tuple-element.79.refs_0_), channel_id=1, source_target_pairs={{4,0},{6,2},{0,4},{2,6},{5,1},{7,3},{1,5},{3,7},{12,8},{14,10},{8,... | collective-permute-start | bytes 1277960 | tf_op jit(solution)/shard_map/ppermute | solution.py:710
  15.8 22.2 %collective-permute-start.5 = (bf16[128,1664]{1,0:T(8,128)(2,1)}, bf16[128,1664]{1,0:T(8,128)(2,1)S(1)}, u32[]{:S(2)}, u32[]{:S(2)}) collective-permute-start(bf16[128,1664]{1,0:T(8,128)(2,1)} %get-tuple-element.79.refs_0_), channel_id=1, source_target_pairs={{6,0},{0,2},{2,4},{4,6},{7,1},{1,3},{3,5},{5,7},{14,8},{8,10},{10,... | collective-permute-start | bytes 1277960 | tf_op jit(solution)/shard_map/ppermute | solution.py:710
  16.4 31.0 %all-to-all-start = ((bf16[16,96,384]{2,1,0:T(8,128)(2,1)}), bf16[16,96,384]{2,1,0:T(8,128)(2,1)S(1)}, u32[]{:S(2)}, u32[]{:S(2)}) async-start(bf16[16,96,384]{2,1,0:T(8,128)(2,1)} %get-tuple-element.81), calls=%async_computation | async-start | bytes 2359296 | tf_op jit(solution)/shard_map/all_to_all | solution.py:790
  41.9 22.0 %collective-permute-start.7 = (bf16[128,1536]{1,0:T(8,128)(2,1)S(1)}, bf16[128,1536]{1,0:T(8,128)(2,1)}, u32[]{:S(2)}, u32[]{:S(2)}) collective-permute-start(bf16[128,1536]{1,0:T(8,128)(2,1)S(1)} %copy-done.9), channel_id=1, source_target_pairs={{2,0},{4,2},{6,4},{0,6},{3,1},{5,3},{7,5},{1,7},{10,8},{12,10},{14... | collective-permute-start | bytes 1179656 | tf_op jit(solution)/shard_map/ppermute | solution.py:710
  42.2 21.7 %collective-permute-start.8 = (bf16[128,1536]{1,0:T(8,128)(2,1)S(1)}, bf16[128,1536]{1,0:T(8,128)(2,1)}, u32[]{:S(2)}, u32[]{:S(2)}) collective-permute-start(bf16[128,1536]{1,0:T(8,128)(2,1)S(1)} %copy-done.9), channel_id=1, source_target_pairs={{4,0},{6,2},{0,4},{2,6},{5,1},{7,3},{1,5},{3,7},{12,8},{14,10},{8,... | collective-permute-start | bytes 1179656 | tf_op jit(solution)/shard_map/ppermute | solution.py:710
  42.8 21.2 %collective-permute-start.9 = (bf16[128,1536]{1,0:T(8,128)(2,1)S(1)}, bf16[128,1536]{1,0:T(8,128)(2,1)}, u32[]{:S(2)}, u32[]{:S(2)}) collective-permute-start(bf16[128,1536]{1,0:T(8,128)(2,1)S(1)} %copy-done.9), channel_id=1, source_target_pairs={{6,0},{0,2},{2,4},{4,6},{7,1},{1,3},{3,5},{5,7},{14,8},{8,10},{10,... | collective-permute-start | bytes 1179656 | tf_op jit(solution)/shard_map/ppermute | solution.py:710
  69.1 158.1 %all-gather.5.cloned.1.call-start = ((), (), s32[]{:S(2)}) async-start(), calls=%async_computation.6 | async-start | bytes 3538944 | tf_op jit(solution)/shard_map/all_gather | solution.py:822
  69.2 17.5 %collective-permute-start.11 = (bf16[128,1536]{1,0:T(8,128)(2,1)}, bf16[128,1536]{1,0:T(8,128)(2,1)S(1)}, u32[]{:S(2)}, u32[]{:S(2)}) collective-permute-start(bf16[128,1536]{1,0:T(8,128)(2,1)} %collective-permute-done.7.refs_2_), channel_id=1, source_target_pairs={{0,1},{1,0},{2,3},{3,2},{4,5},{5,4},{6,7},{7,6},{8,9},{9,8},{10,11... | collective-permute-start | bytes 1179656 | tf_op jit(solution)/shard_map/ppermute | solution.py:714
  69.6 17.7 %collective-permute-start.12 = (bf16[128,1536]{1,0:T(8,128)(2,1)}, bf16[128,1536]{1,0:T(8,128)(2,1)S(1)}, u32[]{:S(2)}, u32[]{:S(2)}) collective-permute-start(bf16[128,1536]{1,0:T(8,128)(2,1)} %collective-permute-done.8.refs_4_), channel_id=1, source_target_pairs={{0,1},{1,0},{2,3},{3,2},{4,5},{5,4},{6,7},{7,6},{8,9},{9,8},{10,11... | collective-permute-start | bytes 1179656 | tf_op jit(solution)/shard_map/ppermute | solution.py:714
  69.8 17.6 %collective-permute-start.13 = (bf16[128,1536]{1,0:T(8,128)(2,1)}, bf16[128,1536]{1,0:T(8,128)(2,1)}, u32[]{:S(2)}, u32[]{:S(2)}) collective-permute-start(bf16[128,1536]{1,0:T(8,128)(2,1)} %collective-permute-done.9.refs_6_), channel_id=1, source_target_pairs={{0,1},{1,0},{2,3},{3,2},{4,5},{5,4},{6,7},{7,6},{8,9},{9,8},{10,11... | collective-permute-start | bytes 1179656 | tf_op jit(solution)/shard_map/ppermute | solution.py:714
  86.8 21.4 %collective-permute-start.16 = (bf16[128,1664]{1,0:T(8,128)(2,1)}, bf16[128,1664]{1,0:T(8,128)(2,1)S(1)}, u32[]{:S(2)}, u32[]{:S(2)}) collective-permute-start(bf16[128,1664]{1,0:T(8,128)(2,1)} %get-tuple-element.93.refs_0_), channel_id=1, source_target_pairs={{6,0},{0,2},{2,4},{4,6},{7,1},{1,3},{3,5},{5,7},{14,8},{8,10},{10,... | collective-permute-start | bytes 1277960 | tf_op jit(solution)/shard_map/ppermute | solution.py:710
  108.2 196.0 %all-reduce.3.cloned.1.call-start = ((), (), s32[]{:S(2)}) async-start(), calls=%async_computation.7 | async-start | bytes 18874368 | tf_op jit(solution)/shard_map/psum | solution.py:827
  158.3 25.5 %all-to-all-start.2 = ((bf16[4,128,1664]{2,1,0:T(8,128)(2,1)}), bf16[4,128,1664]{2,1,0:T(8,128)(2,1)S(1)}, u32[]{:S(2)}, u32[]{:S(2)}) async-start(bf16[4,128,1664]{2,1,0:T(8,128)(2,1)} %add_convert_fusion), calls=%async_computation.2 | async-start | bytes 3407872 | tf_op jit(solution)/shard_map/all_to_all | solution.py:734
  170.1 71.0 %collective-permute-start.22 = (bf16[4,128,1536]{2,1,0:T(8,128)(2,1)}, bf16[4,128,1536]{2,1,0:T(8,128)(2,1)}, u32[]{:S(2)}, u32[]{:S(2)}) collective-permute-start(bf16[4,128,1536]{2,1,0:T(8,128)(2,1)} %get-tuple-element.126), channel_id=1, source_target_pairs={{0,1},{1,0},{2,3},{3,2},{4,5},{5,4},{6,7},{7,6},{8,9},{9,8},{10,11... | collective-permute-start | bytes 4718600 | tf_op jit(solution)/shard_map/ppermute | solution.py:714
  225.3 20.0 %collective-permute-start.26 = (bf16[4,128,1536]{2,1,0:T(8,128)(2,1)}, bf16[4,128,1536]{2,1,0:T(8,128)(2,1)}, u32[]{:S(2)}, u32[]{:S(2)}) collective-permute-start(bf16[4,128,1536]{2,1,0:T(8,128)(2,1)} %get-tuple-element.129), channel_id=1, source_target_pairs={{0,1},{1,0},{2,3},{3,2},{4,5},{5,4},{6,7},{7,6},{8,9},{9,8},{10,11... | collective-permute-start | bytes 4718600 | tf_op jit(solution)/shard_map/ppermute | solution.py:714
  235.1 47.3 %all-to-all-start.4 = ((bf16[16,112,512]{2,1,0:T(8,128)(2,1)}), bf16[16,112,512]{2,1,0:T(8,128)(2,1)S(1)}, u32[]{:S(2)}, u32[]{:S(2)}) async-start(bf16[16,112,512]{2,1,0:T(8,128)(2,1)} %weight_grads.1), calls=%async_computation.4 | async-start | bytes 3670016 | tf_op jit(solution)/shard_map/all_to_all | solution.py:859
  244.0 19.3 %collective-permute-start.24 = (bf16[128,1536]{1,0:T(8,128)(2,1)S(1)}, bf16[128,1536]{1,0:T(8,128)(2,1)S(1)}, u32[]{:S(2)}, u32[]{:S(2)}) collective-permute-start(bf16[128,1536]{1,0:T(8,128)(2,1)S(1)} %get-tuple-element.156), channel_id=1, source_target_pairs={{6,0},{0,2},{2,4},{4,6},{7,1},{1,3},{3,5},{5,7},{14,8},{8,10},{10,... | collective-permute-start | bytes 1179656 | tf_op jit(solution)/shard_map/ppermute | solution.py:710
  244.6 18.7 %collective-permute-start.23 = (bf16[128,1536]{1,0:T(8,128)(2,1)S(1)}, bf16[128,1536]{1,0:T(8,128)(2,1)S(1)}, u32[]{:S(2)}, u32[]{:S(2)}) collective-permute-start(bf16[128,1536]{1,0:T(8,128)(2,1)S(1)} %get-tuple-element.154), channel_id=1, source_target_pairs={{4,0},{6,2},{0,4},{2,6},{5,1},{7,3},{1,5},{3,7},{12,8},{14,10},{8,... | collective-permute-start | bytes 1179656 | tf_op jit(solution)/shard_map/ppermute | solution.py:710
  247.2 23.3 %collective-permute-start.29 = (bf16[128,1536]{1,0:T(8,128)(2,1)S(1)}, bf16[128,1536]{1,0:T(8,128)(2,1)S(1)}, u32[]{:S(2)}, u32[]{:S(2)}) collective-permute-start(bf16[128,1536]{1,0:T(8,128)(2,1)S(1)} %get-tuple-element.152), channel_id=1, source_target_pairs={{2,0},{4,2},{6,4},{0,6},{3,1},{5,3},{7,5},{1,7},{10,8},{12,10},{14... | collective-permute-start | bytes 1179656 | tf_op jit(solution)/shard_map/ppermute | solution.py:710
  249.2 31.4 %collective-permute-start.28 = (bf16[128,1536]{1,0:T(8,128)(2,1)S(1)}, bf16[128,1536]{1,0:T(8,128)(2,1)S(1)}, u32[]{:S(2)}, u32[]{:S(2)}) collective-permute-start(bf16[128,1536]{1,0:T(8,128)(2,1)S(1)} %get-tuple-element.153), channel_id=1, source_target_pairs={{6,0},{0,2},{2,4},{4,6},{7,1},{1,3},{3,5},{5,7},{14,8},{8,10},{10,... | collective-permute-start | bytes 1179656 | tf_op jit(solution)/shard_map/ppermute | solution.py:710
  253.6 27.0 %collective-permute-start.27 = (bf16[128,1536]{1,0:T(8,128)(2,1)S(1)}, bf16[128,1536]{1,0:T(8,128)(2,1)S(1)}, u32[]{:S(2)}, u32[]{:S(2)}) collective-permute-start(bf16[128,1536]{1,0:T(8,128)(2,1)S(1)} %get-tuple-element.151), channel_id=1, source_target_pairs={{4,0},{6,2},{0,4},{2,6},{5,1},{7,3},{1,5},{3,7},{12,8},{14,10},{8,... | collective-permute-start | bytes 1179656 | tf_op jit(solution)/shard_map/ppermute | solution.py:710
  (55 other events, 405.5 us)
Sparse Core Ops, SparseCore 0:
  10.2 67.7 all-gather.2
  108.3 26.7 all-gather.4
  139.9 164.2 all-reduce.2

commit v4 on v3

--- a/solution.py
+++ b/solution.py
@@ -59,7 +59,8 @@
 
 def attend_body(ids, *refs):
     blocks = refs[:8]
-    (w, cos_t, sin_t, freq, _, normed, narrow, q01, q2k, val, lse, cos_o, sin_o, starts, mixed, ka, kb, vt) = refs[8:]
+    (w, cos_t, sin_t, freq, _, normed, narrow, gain_row, q01, q2k, val, lse, cos_o, sin_o, starts, mixed,
+     ka, kb, vt) = refs[8:]
     one = jnp.zeros((1, 128), f32)
     two = jnp.zeros((1, 128), f32)
     for b in range(8):
@@ -70,8 +71,10 @@
     begin_rows = jnp.concatenate([one, two, jnp.zeros((6, 128), f32)], axis=0)
     angles = begin_rows * freq[...]
     cos_b, sin_b = jnp.cos(angles), jnp.sin(angles)
-    narrow[...] = w[:, 256:384].astype(f32).T
-    gain = narrow[64:65, :]
+    last = w[:, 256:384].astype(f32).T
+    narrow[...] = last[64:128].astype(bf16)
+    gain = last[64:65]
+    gain_row[...] = gain
     for b in range(8):
         x = blocks[b][:, 0:1536].astype(f32)
         r = lax.rsqrt(jnp.mean(x * x, axis=1, keepdims=True) + eps)
@@ -131,7 +134,8 @@
         attend_body,
         out_shape=(
             shape((1024, 1536), bf16),
-            shape((128, 1536), f32),
+            shape((64, 1536), bf16),
+            shape((1, 1536), f32),
             shape((1024, 128), bf16),
             shape((1024, 128), bf16),
             shape((1024, 128), bf16),
@@ -144,7 +148,7 @@
         in_specs=[pl.BlockSpec(memory_space=pltpu.SMEM)]
         + [vm] * 12
         + [pl.BlockSpec(memory_space=pl.ANY)],
-        out_specs=(vm,) * 10,
+        out_specs=(vm,) * 11,
         scratch_shapes=[
             pltpu.VMEM((1024, 128), bf16),
             pltpu.VMEM((1024, 128), bf16),
@@ -157,7 +161,7 @@
 
 
 def attend_back_body(
-    here, w, gm, q01, q2k, val, lse, cc, ss, starts, normed_hbm, narrow,
+    here, w, gm, q01, q2k, val, lse, cc, ss, starts, normed_hbm, gain,
     dqkv, own_hbm, other_hbm, grad_gain, ka, kb, vb, kt, do01, do2, dk, dv, d01, dq2,
     normed, own, other, got, sent,
 ):
@@ -231,13 +235,13 @@
         return total
 
     total = lax.fori_loop(0, 4, finish, jnp.zeros((1, 1536), f32))
-    grad_gain[...] = total / narrow[64:65, :]
+    grad_gain[...] = total / gain[...]
     for c in range(4):
         for copy in store(c):
             copy.wait()
 
 
-def attend_backward(here, gm, q01, q2k, val, lse, cc, ss, starts, normed, w, narrow):
+def attend_backward(here, gm, q01, q2k, val, lse, cc, ss, starts, normed, w, gain):
     vm, hbm = pl.BlockSpec(memory_space=pltpu.VMEM), pl.BlockSpec(memory_space=pl.ANY)
     rows = pltpu.VMEM((4, 128, 1536), bf16)
     shape = jax.ShapeDtypeStruct
@@ -261,7 +265,7 @@
         compiler_params=pltpu.CompilerParams(vmem_limit_bytes=56 * MIB),
         cost_estimate=pl.CostEstimate(flops=1_000_000, bytes_accessed=100_000, transcendentals=0),
         name="attend_backward",
-    )(here, w, gm, q01, q2k, val, lse, cc, ss, starts, normed, narrow)
+    )(here, w, gm, q01, q2k, val, lse, cc, ss, starts, normed, gain)
 
 
 def experts_body(ids, *refs):
@@ -617,9 +621,11 @@
     value = tokens[...].astype(f32) + residual_scale * mm(mx[...], w_out[...])
     hidden[...] = value
     r = lax.rsqrt(jnp.mean(value * value, axis=1, keepdims=True) + eps)
-    second = (value * r * narrow[65:66, :]).astype(bf16)
+    gain = narrow[0:16, :].astype(f32)[1:2]
+    second = (value * r * gain).astype(bf16)
     sent[:, 0:1536] = second
-    logits = pltpu.roll(mm_nt(second, narrow[...].astype(bf16)), 62, 1)
+    logits = mm_nt(second, narrow[...])
+    logits = pltpu.roll(jnp.concatenate([logits, jnp.zeros_like(logits)], axis=1), 126, 1)
     on = named[...] > 0.5
     logits = jnp.where(on, logits, -1e30)
     top = jnp.max(logits, axis=1, keepdims=True)
@@ -654,7 +660,7 @@
 def middle_body(
     w_out, sums, grads, hidden, gates, narrow, _, grad_hidden, heads, grad_gain, grad_router, gx
 ):
-    gain = narrow[65:66, :]
+    gain = narrow[0:16, :].astype(f32)[1:2]
     total = sums[0].astype(f32)
     for i in range(1, 4):
         total = total + sums[i].astype(f32)
@@ -667,8 +673,8 @@
     table = jnp.where(lane < 16, table + pltpu.roll(table, 112, 1), 0.0)
     logits = (g * (table - jnp.sum(g * table, axis=1, keepdims=True))).astype(bf16)
     grad_router[...] = mm(logits.astype(f32).T.astype(bf16), second)[0:16]
-    router = pltpu.roll(logits.astype(f32), 66, 1).astype(bf16)
-    grad_second = total[:, 0:1536] + mm(router, narrow[...].astype(bf16))
+    router = pltpu.roll(logits.astype(f32), 2, 1)[:, 0:64].astype(bf16)
+    grad_second = total[:, 0:1536] + mm(router, narrow[...])
     grad_gain[...] = jnp.sum(grad_second * value * r, axis=0, keepdims=True)
     scaled = grad_second * gain
     gh = (
@@ -805,7 +811,7 @@
 
     named = jnp.any(routes[:, :, None] == lane[None, None, :], axis=1).astype(f32)
 
-    normed, narrow, q01, q2k, val, lse, cos, sin, starts, mixed_head = attend_forward(
+    normed, narrow, gain_one, q01, q2k, val, lse, cos, sin, starts, mixed_head = attend_forward(
         ids, blocks, qkv_w, jnp.cos(angles), jnp.sin(angles), freq, named
     )
     mixed_head, *grads_far = tied(mixed_head, *grads_far)
@@ -838,7 +844,7 @@
     )
     grad_heads = lax.all_to_all(heads, ("x", "core"), 0, 0, tiled=True)
     grad_qkv, own, other, grad_gain_one = attend_backward(
-        at, grad_heads, q01, q2k, val, lse, cos, sin, starts, normed, qkv_w, narrow
+        at, grad_heads, q01, q2k, val, lse, cos, sin, starts, normed, qkv_w, gain_one
     )
     table = weight_grads(
         normed, grad_qkv, mixed_all, grad_heads, grad_gain_one, grad_gain_two, grad_router
@@ -849,7 +855,7 @@
     normed_mine = total_of(exchange_apart(near_sum(own, other)))
     inputs = tokens.astype(f32)
     scale_one = inverse_rms(inputs)
-    scaled_one = normed_mine * narrow[64:65, :]
+    scaled_one = normed_mine * gain_one
     grad_inputs = (
         grad_hidden
         + scale_one * scaled_one

time: 325 us -> 323 us (level)
    unnamed x71 -> x73, local copies, waits for them, and re-layouts: 7.35 us -> 7.35 us
where the time goes in v4:
time: 323 us; the launch traced here: 319 us
  Pallas kernels  122 us (38%)
  waiting for transfers between devices  88.8 us (27%)
  starting transfers between devices  53.2 us (16%)
  blocking collectives  17.5 us (5%)
  other arithmetic  14.7 us (5%)
  between operations  14.4 us (4%)
  local copies, waits for them, and re-layouts  8.15 us (3%)
    ppermute x18, waiting for transfers between devices, shift(): lax.ppermute(value, axis, [((i + amount) % size, i) for i in range(size)])  52.9 us
    pallas_call x1, Pallas kernels, experts(): pl.pallas_call(experts_body, grid=(2, 2), out_shape=(shape((2, 1536, 512)...  26.2 us
    pallas_call x2, Pallas kernels, by_chip(): pl.pallas_call(body, grid_spec=pltpu.PrefetchScalarGridSpec(num_scalar_pr...  20.5 us
    all_to_all x1, blocking collectives, per_device(): grad_heads = lax.all_to_all(heads, ('x', 'core'), 0, 0, tiled=True)  17.5 us
    pallas_call x1, Pallas kernels, attend_backward(): pl.pallas_call(attend_back_body, out_shape=(shape((1024, 384), bf16), sha...  15.5 us
    pallas_call x1, Pallas kernels, attend_forward(): pl.pallas_call(attend_body, out_shape=(shape((1024, 1536), bf16), shape((...  15.5 us
    ppermute x18, starting transfers between devices, shift(): lax.ppermute(value, axis, [((i + amount) % size, i) for i in range(size)])  15.4 us
    ppermute x19, starting transfers between devices, swap(): return lax.ppermute(value, 'core', [(0, 1), (1, 0)])  15.3 us
  transfers between devices with their start and end apart: 44, of which 19 were waited for; matrix products, arithmetic and copies ran while one was open for 5% of the time, Pallas kernels for 35%

profile of v4, /device:TPU:1, one launch (start us, length us, event | category | flops | bytes accessed | tf_op | source)
XLA Modules:
  0.0 318.7 jit_solution(1797091132731649531)
XLA Ops:
  16.3 7.8 %all-to-all-start = ((bf16[16,96,384]{2,1,0:T(8,128)(2,1)}), bf16[16,96,384]{2,1,0:T(8,128)(2,1)S(1)}, u32[]{:S(2)}, u32[]{:S(2)}) async-start(bf16[16,96,384]{2,1,0:T(8,128)(2,1)} %get-tuple-element.82), calls=%async_computation | async-start | bytes 2359296 | tf_op jit(solution)/shard_map/all_to_all | solution.py:796
  25.8 7.9 %collective-permute-done.1.refs_2_ = bf16[128,1664]{1,0:T(8,128)(2,1)S(1)} collective-permute-done((bf16[128,1664]{1,0:T(8,128)(2,1)}, bf16[128,1664]{1,0:T(8,128)(2,1)S(1)}, u32[]{:S(2)}, u32[]{:S(2)}) %collective-permute-start.1) | collective-permute-done | bytes 426016 | tf_op jit(solution)/shard_map/ppermute | solution.py:716
  48.6 15.5 %attend_forward.1 = (bf16[1024,1536]{1,0:T(8,128)(2,1)}, bf16[64,1536]{1,0:T(8,128)(2,1)}, f32[1,1536]{1,0:T(1,128)}, bf16[1024,128]{1,0:T(8,128)(2,1)}, bf16[10...) custom-call(s32[8]{0:T(128)} %add.160.ids, ...), custom_call_target="tpu_custom_call" | custom-call | flops 14000000000 | bytes 12000000 | tf_op jit(solution)/shard_map/attend_forward/pallas_call | solution.py:133
  64.1 5.1 %all-to-all-start.1 = ((bf16[8,128,256]{2,1,0:T(8,128)(2,1)}), bf16[8,128,256]{2,1,0:T(8,128)(2,1)S(1)}, u32[]{:S(2)}, u32[]{:S(2)}) async-start(bf16[8,128,256]{2,1,0:T(8,128)(2,1)} %get-tuple-element.85), calls=%async_computation.1 | async-start | bytes 1048576 | tf_op jit(solution)/shard_map/all_to_all | solution.py:819
  70.2 8.5 %all-to-all-done.1.mixed = bf16[8,128,256]{2,1,0:T(8,128)(2,1)S(1)} async-done(((bf16[8,128,256]{2,1,0:T(8,128)(2,1)}), bf16[8,128,256]{2,1,0:T(8,128)(2,1)S(1)}, u32[]{:S(2)}, u32[]{:S(2)}) %all-to-all-start.1) | async-done | bytes 524320 | tf_op jit(solution)/shard_map/all_to_all | solution.py:819
  79.4 5.0 %project_out.1 = (bf16[128,1664]{1,0:T(8,128)(2,1)}, f32[128,1536]{1,0:T(8,128)}, f32[128,128]{1,0:T(8,128)}, bf16[128,1536]{1,0:T(8,128)(2,1)}) custom-call(bf16[8,128,256]{2,1,0:T(8,128)(2,1)} %copy-done.8, bf16[1536,1536]{1,0:T(8,128)(2,1)} %all-gather.3.cloned.1.call-done.w_out, bf16[128,1536]{1,0:T(8,128)(2,1)} %tokens.3, ...), custom_call_target="tpu_custom_call" | custom-call | flops 4000000000 | bytes 8000000 | tf_op jit(solution)/shard_map/project_out/pallas_call | solution.py:644
  87.8 7.7 %back_rows.1 = (bf16[1024,1536]{1,0:T(8,128)(2,1)}, bf16[1024,1024]{1,0:T(8,128)(2,1)}) custom-call(s32[8]{0:T(128)} %add.160.ids, bf16[128,1536]{1,0:T(8,128)(2,1)} %grads.1, bf16[128,1536]{1,0:T(8,128)(2,1)} %copy-done.33, bf16[128,1536]{1,0:T(8,128)(2,1)} %collective-permute-done.7.refs_2_, bf16[128,1536]{1,0:T(8,128)(2,1)} %copy-done.34, ...), custom_call_target="tpu_custom_call" | custom-call | flops 8000000000 | bytes 11000000 | tf_op jit(solution)/shard_map/back_rows/pallas_call | solution.py:460
  97.2 10.7 %collective-permute-done.16.refs_6_ = bf16[128,1664]{1,0:T(8,128)(2,1)S(1)} collective-permute-done((bf16[128,1664]{1,0:T(8,128)(2,1)}, bf16[128,1664]{1,0:T(8,128)(2,1)S(1)}, u32[]{:S(2)}, u32[]{:S(2)}) %collective-permute-start.16) | collective-permute-done | bytes 426016 | tf_op jit(solution)/shard_map/ppermute | solution.py:716
  112.6 26.2 %experts.1 = (bf16[2,1536,512]{2,1,0:T(8,128)(2,1)}, bf16[2,1536,512]{2,1,0:T(8,128)(2,1)}, bf16[2,512,1536]{2,1,0:T(8,128)(2,1)}, bf16[1024,1024]{1,0:T(8,128)(...) custom-call(s32[8]{0:T(128)} %add.160.ids, ...), custom_call_target="tpu_custom_call" | custom-call | flops 16000000000 | bytes 34000000 | tf_op jit(solution)/shard_map/experts/pallas_call | solution.py:324
  138.8 12.4 %experts_back.1 = (bf16[4,128,1664]{2,1,0:T(8,128)(2,1)}, bf16[4,128,1664]{2,1,0:T(8,128)(2,1)}) custom-call(s32[3]{0:T(128)} %pad_add_fusion.at.here, bf16[1024,1024]{1,0:T(8,128)(2,1)} %get-tuple-element.100.gg, bf16[1024,1024]{1,0:T(8,128)(2,1)} %get-tuple-element.101.gu, f32[1024,128]{1,0:T(8,128)} %get-tuple-element.102.routed, ...), custom_call_target="tpu_custom_call" | custom-call | flops 1000000 | bytes 100000 | tf_op jit(solution)/shard_map/experts_back/pallas_call | solution.py:361
  151.5 3.4 %collective-permute-done.21 = bf16[4,128,1664]{2,1,0:T(8,128)(2,1)S(1)} collective-permute-done((bf16[4,128,1664]{2,1,0:T(8,128)(2,1)}, bf16[4,128,1664]{2,1,0:T(8,128)(2,1)S(1)}, u32[]{:S(2)}, u32[]{:S(2)}) %collective-permute-start.21) | collective-permute-done | bytes 1703968 | tf_op jit(solution)/shard_map/ppermute | solution.py:720
  158.1 3.6 %all-to-all-start.2 = ((bf16[4,128,1664]{2,1,0:T(8,128)(2,1)}), bf16[4,128,1664]{2,1,0:T(8,128)(2,1)S(1)}, u32[]{:S(2)}, u32[]{:S(2)}) async-start(bf16[4,128,1664]{2,1,0:T(8,128)(2,1)} %add_convert_fusion), calls=%async_computation.2 | async-start | bytes 3407872 | tf_op jit(solution)/shard_map/all_to_all | solution.py:740
  161.7 8.2 %combine.1 = (bf16[4,128,1536]{2,1,0:T(8,128)(2,1)}, bf16[4,128,1536]{2,1,0:T(8,128)(2,1)}) custom-call(s32[3]{0:T(128)} %pad_add_fusion.at.here, bf16[1024,1024]{1,0:T(8,128)(2,1)} %get-tuple-element.106.aw, bf16[2,512,1536]{2,1,0:T(8,128)(2,1)} %down_w.1), custom_call_target="tpu_custom_call" | custom-call | flops 8000000000 | bytes 100000 | tf_op jit(solution)/shard_map/combine/pallas_call | solution.py:361
  170.3 13.3 %all-to-all-done.2.sums = bf16[4,128,1664]{2,1,0:T(8,128)(2,1)S(1)} async-done(((bf16[4,128,1664]{2,1,0:T(8,128)(2,1)}), bf16[4,128,1664]{2,1,0:T(8,128)(2,1)S(1)}, u32[]{:S(2)}, u32[]{:S(2)}) %all-to-all-start.2) | async-done | bytes 1703968 | tf_op jit(solution)/shard_map/all_to_all | solution.py:740
  184.8 6.8 %middle.1 = (f32[128,1536]{1,0:T(8,128)}, bf16[8,128,384]{2,1,0:T(8,128)(2,1)}, f32[1,1536]{1,0:T(1,128)}, f32[16,1536]{1,0:T(8,128)}) custom-call(bf16[1536,1536]{1,0:T(8,128)(2,1)} %all-gather.3.cloned.1.call-done.w_out, bf16[4,128,1664]{2,1,0:T(8,128)(2,1)} %copy-done.1, bf16[128,1536]{1,0:T(8,128)(2,1)} %grads.1, f32[128,1536]{1,0:T(8,128)} %get-tuple-element.110.hidden, ...), custom_call_target="tpu_custom_call" | custom-call | flops 1000000 | bytes 100000 | tf_op jit(solution)/shard_map/middle/pallas_call | solution.py:697
  191.5 17.5 %all_to_all.25.gm.branch = bf16[8,128,384]{2,1,0:T(8,128)(2,1)} all-to-all(bf16[8,128,384]{2,1,0:T(8,128)(2,1)} %get-tuple-element.112), channel_id=1, replica_groups=mesh['z'=4,'y'=4,'x'=4,'core'=2] {'x','core'}, dimensions={0} | all-to-all | bytes 1572864 | tf_op jit(solution)/shard_map/all_to_all | solution.py:845
  209.1 15.5 %attend_backward.1 = (bf16[1024,384]{1,0:T(8,128)(2,1)}, bf16[4,128,1536]{2,1,0:T(8,128)(2,1)}, bf16[4,128,1536]{2,1,0:T(8,128)(2,1)}, f32[1,1536]{1,0:T(1,128)}) custom-call(s32[3]{0:T(128)} %pad_add_fusion.at.here, bf16[1536,384]{1,0:T(8,128)(2,1)} %bitcast.34, bf16[8,128,384]{2,1,0:T(8,128)(2,1)} %all_to_all.25.gm.branch, ...), custom_call_target="tpu_custom_call" | custom-call | flops 1000000 | bytes 100000 | tf_op jit(solution)/shard_map/attend_backward/pallas_call | solution.py:250
  225.8 7.8 %weight_grads.1 = bf16[16,112,512]{2,1,0:T(8,128)(2,1)} custom-call(bf16[1024,1536]{1,0:T(8,128)(2,1)} %get-tuple-element.108.normed_hbm.normed, bf16[1024,384]{1,0:T(8,128)(2,1)} %get-tuple-element.121.grad_qkv, bf16[1024,1536]{1,0:T(8,128)(2,1)} %all-gather.5.cloned.1.call-done.mixed, bf16[8,128,384]{2,1,0:T(8,128)(2,1)} %all_to_all.25.gm.branch, ...), custom_call_target="tpu_custom_call" | custom-call | flops 1000000 | bytes 100000 | tf_op jit(solution)/shard_map/weight_grads/pallas_call | solution.py:498
  233.6 6.0 %all-to-all-start.4 = ((bf16[16,112,512]{2,1,0:T(8,128)(2,1)}), bf16[16,112,512]{2,1,0:T(8,128)(2,1)S(1)}, u32[]{:S(2)}, u32[]{:S(2)}) async-start(bf16[16,112,512]{2,1,0:T(8,128)(2,1)} %weight_grads.1), calls=%async_computation.4 | async-start | bytes 3670016 | tf_op jit(solution)/shard_map/all_to_all | solution.py:865
  248.0 4.1 %collective-permute-done.25 = bf16[128,1536]{1,0:T(8,128)(2,1)S(1)} collective-permute-done((bf16[128,1536]{1,0:T(8,128)(2,1)S(1)}, bf16[128,1536]{1,0:T(8,128)(2,1)S(1)}, u32[]{:S(2)}, u32[]{:S(2)}) %collective-permute-start.25) | collective-permute-done | bytes 393248 | tf_op jit(solution)/shard_map/ppermute | solution.py:716
  253.1 8.7 %collective-permute-done.24 = bf16[128,1536]{1,0:T(8,128)(2,1)S(1)} collective-permute-done((bf16[128,1536]{1,0:T(8,128)(2,1)S(1)}, bf16[128,1536]{1,0:T(8,128)(2,1)S(1)}, u32[]{:S(2)}, u32[]{:S(2)}) %collective-permute-start.24) | collective-permute-done | bytes 393248 | tf_op jit(solution)/shard_map/ppermute | solution.py:716
  262.9 6.1 %collective-permute-done.29 = bf16[128,1536]{1,0:T(8,128)(2,1)S(1)} collective-permute-done((bf16[128,1536]{1,0:T(8,128)(2,1)S(1)}, bf16[128,1536]{1,0:T(8,128)(2,1)S(1)}, u32[]{:S(2)}, u32[]{:S(2)}) %collective-permute-start.29) | collective-permute-done | bytes 393248 | tf_op jit(solution)/shard_map/ppermute | solution.py:716
  269.0 10.3 %collective-permute-done.28 = bf16[128,1536]{1,0:T(8,128)(2,1)S(1)} collective-permute-done((bf16[128,1536]{1,0:T(8,128)(2,1)S(1)}, bf16[128,1536]{1,0:T(8,128)(2,1)S(1)}, u32[]{:S(2)}, u32[]{:S(2)}) %collective-permute-start.28) | collective-permute-done | bytes 393248 | tf_op jit(solution)/shard_map/ppermute | solution.py:716
  302.8 9.1 %widen.1 = (f32[2,1536,512]{2,1,0:T(8,128)}, f32[2,1536,512]{2,1,0:T(8,128)}, f32[2,512,1536]{2,1,0:T(8,128)}) custom-call(bf16[2,1536,512]{2,1,0:T(8,128)(2,1)} %get-tuple-element.150.a, bf16[2,1536,512]{2,1,0:T(8,128)(2,1)} %get-tuple-element.151.b, bf16[2,512,1536]{2,1,0:T(8,128)(2,1)} %get-tuple-element.152.c), custom_call_target="tpu_custom_call" | custom-call | flops 1000000 | bytes 28000000 | tf_op jit(solution)/shard_map/widen/pallas_call | solution.py:432
  (176 shorter events, 77.3 us)
Async XLA Ops:
  7.2 71.4 %all-gather.3.cloned.1.call-start = ((), (), s32[]{:S(2)}) async-start(), calls=%async_computation.5 | async-start | bytes 5013504 | tf_op jit(solution)/shard_map/all_gather | solution.py:795
  11.2 31.0 %collective-permute-start = (bf16[128,1664]{1,0:T(8,128)(2,1)}, bf16[128,1664]{1,0:T(8,128)(2,1)S(1)}, u32[]{:S(2)}, u32[]{:S(2)}) collective-permute-start(bf16[128,1664]{1,0:T(8,128)(2,1)} %get-tuple-element.80.refs_0_), channel_id=1, source_target_pairs={{0,1},{1,0},{2,3},{3,2},{4,5},{5,4},{6,7},{7,6},{8,9},{9,8},{10,11... | collective-permute-start | bytes 1277960 | tf_op jit(solution)/shard_map/ppermute | solution.py:720
  12.6 21.1 %collective-permute-start.1 = (bf16[128,1664]{1,0:T(8,128)(2,1)}, bf16[128,1664]{1,0:T(8,128)(2,1)S(1)}, u32[]{:S(2)}, u32[]{:S(2)}) collective-permute-start(bf16[128,1664]{1,0:T(8,128)(2,1)} %get-tuple-element.80.refs_0_), channel_id=1, source_target_pairs={{2,0},{4,2},{6,4},{0,6},{3,1},{5,3},{7,5},{1,7},{10,8},{12,10},{14... | collective-permute-start | bytes 1277960 | tf_op jit(solution)/shard_map/ppermute | solution.py:716
  15.2 19.5 %collective-permute-start.3 = (bf16[128,1664]{1,0:T(8,128)(2,1)}, bf16[128,1664]{1,0:T(8,128)(2,1)S(1)}, u32[]{:S(2)}, u32[]{:S(2)}) collective-permute-start(bf16[128,1664]{1,0:T(8,128)(2,1)} %get-tuple-element.80.refs_0_), channel_id=1, source_target_pairs={{4,0},{6,2},{0,4},{2,6},{5,1},{7,3},{1,5},{3,7},{12,8},{14,10},{8,... | collective-permute-start | bytes 1277960 | tf_op jit(solution)/shard_map/ppermute | solution.py:716
  15.7 22.2 %collective-permute-start.5 = (bf16[128,1664]{1,0:T(8,128)(2,1)}, bf16[128,1664]{1,0:T(8,128)(2,1)S(1)}, u32[]{:S(2)}, u32[]{:S(2)}) collective-permute-start(bf16[128,1664]{1,0:T(8,128)(2,1)} %get-tuple-element.80.refs_0_), channel_id=1, source_target_pairs={{6,0},{0,2},{2,4},{4,6},{7,1},{1,3},{3,5},{5,7},{14,8},{8,10},{10,... | collective-permute-start | bytes 1277960 | tf_op jit(solution)/shard_map/ppermute | solution.py:716
  16.3 31.2 %all-to-all-start = ((bf16[16,96,384]{2,1,0:T(8,128)(2,1)}), bf16[16,96,384]{2,1,0:T(8,128)(2,1)S(1)}, u32[]{:S(2)}, u32[]{:S(2)}) async-start(bf16[16,96,384]{2,1,0:T(8,128)(2,1)} %get-tuple-element.82), calls=%async_computation | async-start | bytes 2359296 | tf_op jit(solution)/shard_map/all_to_all | solution.py:796
  41.9 22.2 %collective-permute-start.7 = (bf16[128,1536]{1,0:T(8,128)(2,1)S(1)}, bf16[128,1536]{1,0:T(8,128)(2,1)}, u32[]{:S(2)}, u32[]{:S(2)}) collective-permute-start(bf16[128,1536]{1,0:T(8,128)(2,1)S(1)} %copy-done.9), channel_id=1, source_target_pairs={{2,0},{4,2},{6,4},{0,6},{3,1},{5,3},{7,5},{1,7},{10,8},{12,10},{14... | collective-permute-start | bytes 1179656 | tf_op jit(solution)/shard_map/ppermute | solution.py:716
  42.2 21.9 %collective-permute-start.8 = (bf16[128,1536]{1,0:T(8,128)(2,1)S(1)}, bf16[128,1536]{1,0:T(8,128)(2,1)}, u32[]{:S(2)}, u32[]{:S(2)}) collective-permute-start(bf16[128,1536]{1,0:T(8,128)(2,1)S(1)} %copy-done.9), channel_id=1, source_target_pairs={{4,0},{6,2},{0,4},{2,6},{5,1},{7,3},{1,5},{3,7},{12,8},{14,10},{8,... | collective-permute-start | bytes 1179656 | tf_op jit(solution)/shard_map/ppermute | solution.py:716
  42.7 21.4 %collective-permute-start.9 = (bf16[128,1536]{1,0:T(8,128)(2,1)S(1)}, bf16[128,1536]{1,0:T(8,128)(2,1)}, u32[]{:S(2)}, u32[]{:S(2)}) collective-permute-start(bf16[128,1536]{1,0:T(8,128)(2,1)S(1)} %copy-done.9), channel_id=1, source_target_pairs={{6,0},{0,2},{2,4},{4,6},{7,1},{1,3},{3,5},{5,7},{14,8},{8,10},{10,... | collective-permute-start | bytes 1179656 | tf_op jit(solution)/shard_map/ppermute | solution.py:716
  69.1 156.6 %all-gather.5.cloned.1.call-start = ((), (), s32[]{:S(2)}) async-start(), calls=%async_computation.6 | async-start | bytes 3538944 | tf_op jit(solution)/shard_map/all_gather | solution.py:828
  69.3 17.3 %collective-permute-start.11 = (bf16[128,1536]{1,0:T(8,128)(2,1)}, bf16[128,1536]{1,0:T(8,128)(2,1)S(1)}, u32[]{:S(2)}, u32[]{:S(2)}) collective-permute-start(bf16[128,1536]{1,0:T(8,128)(2,1)} %collective-permute-done.7.refs_2_), channel_id=1, source_target_pairs={{0,1},{1,0},{2,3},{3,2},{4,5},{5,4},{6,7},{7,6},{8,9},{9,8},{10,11... | collective-permute-start | bytes 1179656 | tf_op jit(solution)/shard_map/ppermute | solution.py:720
  69.7 17.4 %collective-permute-start.12 = (bf16[128,1536]{1,0:T(8,128)(2,1)}, bf16[128,1536]{1,0:T(8,128)(2,1)S(1)}, u32[]{:S(2)}, u32[]{:S(2)}) collective-permute-start(bf16[128,1536]{1,0:T(8,128)(2,1)} %collective-permute-done.8.refs_4_), channel_id=1, source_target_pairs={{0,1},{1,0},{2,3},{3,2},{4,5},{5,4},{6,7},{7,6},{8,9},{9,8},{10,11... | collective-permute-start | bytes 1179656 | tf_op jit(solution)/shard_map/ppermute | solution.py:720
  69.8 17.3 %collective-permute-start.13 = (bf16[128,1536]{1,0:T(8,128)(2,1)}, bf16[128,1536]{1,0:T(8,128)(2,1)}, u32[]{:S(2)}, u32[]{:S(2)}) collective-permute-start(bf16[128,1536]{1,0:T(8,128)(2,1)} %collective-permute-done.9.refs_6_), channel_id=1, source_target_pairs={{0,1},{1,0},{2,3},{3,2},{4,5},{5,4},{6,7},{7,6},{8,9},{9,8},{10,11... | collective-permute-start | bytes 1179656 | tf_op jit(solution)/shard_map/ppermute | solution.py:720
  86.6 21.3 %collective-permute-start.16 = (bf16[128,1664]{1,0:T(8,128)(2,1)}, bf16[128,1664]{1,0:T(8,128)(2,1)S(1)}, u32[]{:S(2)}, u32[]{:S(2)}) collective-permute-start(bf16[128,1664]{1,0:T(8,128)(2,1)} %get-tuple-element.94.refs_0_), channel_id=1, source_target_pairs={{6,0},{0,2},{2,4},{4,6},{7,1},{1,3},{3,5},{5,7},{14,8},{8,10},{10,... | collective-permute-start | bytes 1277960 | tf_op jit(solution)/shard_map/ppermute | solution.py:716
  107.9 194.9 %all-reduce.3.cloned.1.call-start = ((), (), s32[]{:S(2)}) async-start(), calls=%async_computation.7 | async-start | bytes 18874368 | tf_op jit(solution)/shard_map/psum | solution.py:833
  158.1 25.5 %all-to-all-start.2 = ((bf16[4,128,1664]{2,1,0:T(8,128)(2,1)}), bf16[4,128,1664]{2,1,0:T(8,128)(2,1)S(1)}, u32[]{:S(2)}, u32[]{:S(2)}) async-start(bf16[4,128,1664]{2,1,0:T(8,128)(2,1)} %add_convert_fusion), calls=%async_computation.2 | async-start | bytes 3407872 | tf_op jit(solution)/shard_map/all_to_all | solution.py:740
  169.8 69.8 %collective-permute-start.22 = (bf16[4,128,1536]{2,1,0:T(8,128)(2,1)}, bf16[4,128,1536]{2,1,0:T(8,128)(2,1)}, u32[]{:S(2)}, u32[]{:S(2)}) collective-permute-start(bf16[4,128,1536]{2,1,0:T(8,128)(2,1)} %get-tuple-element.128), channel_id=1, source_target_pairs={{0,1},{1,0},{2,3},{3,2},{4,5},{5,4},{6,7},{7,6},{8,9},{9,8},{10,11... | collective-permute-start | bytes 4718600 | tf_op jit(solution)/shard_map/ppermute | solution.py:720
  224.6 19.3 %collective-permute-start.26 = (bf16[4,128,1536]{2,1,0:T(8,128)(2,1)}, bf16[4,128,1536]{2,1,0:T(8,128)(2,1)}, u32[]{:S(2)}, u32[]{:S(2)}) collective-permute-start(bf16[4,128,1536]{2,1,0:T(8,128)(2,1)} %get-tuple-element.131), channel_id=1, source_target_pairs={{0,1},{1,0},{2,3},{3,2},{4,5},{5,4},{6,7},{7,6},{8,9},{9,8},{10,11... | collective-permute-start | bytes 4718600 | tf_op jit(solution)/shard_map/ppermute | solution.py:720
  233.6 47.5 %all-to-all-start.4 = ((bf16[16,112,512]{2,1,0:T(8,128)(2,1)}), bf16[16,112,512]{2,1,0:T(8,128)(2,1)S(1)}, u32[]{:S(2)}, u32[]{:S(2)}) async-start(bf16[16,112,512]{2,1,0:T(8,128)(2,1)} %weight_grads.1), calls=%async_computation.4 | async-start | bytes 3670016 | tf_op jit(solution)/shard_map/all_to_all | solution.py:865
  242.6 19.2 %collective-permute-start.24 = (bf16[128,1536]{1,0:T(8,128)(2,1)S(1)}, bf16[128,1536]{1,0:T(8,128)(2,1)S(1)}, u32[]{:S(2)}, u32[]{:S(2)}) collective-permute-start(bf16[128,1536]{1,0:T(8,128)(2,1)S(1)} %get-tuple-element.158), channel_id=1, source_target_pairs={{6,0},{0,2},{2,4},{4,6},{7,1},{1,3},{3,5},{5,7},{14,8},{8,10},{10,... | collective-permute-start | bytes 1179656 | tf_op jit(solution)/shard_map/ppermute | solution.py:716
  243.1 18.8 %collective-permute-start.23 = (bf16[128,1536]{1,0:T(8,128)(2,1)S(1)}, bf16[128,1536]{1,0:T(8,128)(2,1)S(1)}, u32[]{:S(2)}, u32[]{:S(2)}) collective-permute-start(bf16[128,1536]{1,0:T(8,128)(2,1)S(1)} %get-tuple-element.156), channel_id=1, source_target_pairs={{4,0},{6,2},{0,4},{2,6},{5,1},{7,3},{1,5},{3,7},{12,8},{14,10},{8,... | collective-permute-start | bytes 1179656 | tf_op jit(solution)/shard_map/ppermute | solution.py:716
  245.8 23.1 %collective-permute-start.29 = (bf16[128,1536]{1,0:T(8,128)(2,1)S(1)}, bf16[128,1536]{1,0:T(8,128)(2,1)S(1)}, u32[]{:S(2)}, u32[]{:S(2)}) collective-permute-start(bf16[128,1536]{1,0:T(8,128)(2,1)S(1)} %get-tuple-element.154), channel_id=1, source_target_pairs={{2,0},{4,2},{6,4},{0,6},{3,1},{5,3},{7,5},{1,7},{10,8},{12,10},{14... | collective-permute-start | bytes 1179656 | tf_op jit(solution)/shard_map/ppermute | solution.py:716
  247.8 31.4 %collective-permute-start.28 = (bf16[128,1536]{1,0:T(8,128)(2,1)S(1)}, bf16[128,1536]{1,0:T(8,128)(2,1)S(1)}, u32[]{:S(2)}, u32[]{:S(2)}) collective-permute-start(bf16[128,1536]{1,0:T(8,128)(2,1)S(1)} %get-tuple-element.155), channel_id=1, source_target_pairs={{6,0},{0,2},{2,4},{4,6},{7,1},{1,3},{3,5},{5,7},{14,8},{8,10},{10,... | collective-permute-start | bytes 1179656 | tf_op jit(solution)/shard_map/ppermute | solution.py:716
  252.1 27.2 %collective-permute-start.27 = (bf16[128,1536]{1,0:T(8,128)(2,1)S(1)}, bf16[128,1536]{1,0:T(8,128)(2,1)S(1)}, u32[]{:S(2)}, u32[]{:S(2)}) collective-permute-start(bf16[128,1536]{1,0:T(8,128)(2,1)S(1)} %get-tuple-element.153), channel_id=1, source_target_pairs={{4,0},{6,2},{0,4},{2,6},{5,1},{7,3},{1,5},{3,7},{12,8},{14,10},{8,... | collective-permute-start | bytes 1179656 | tf_op jit(solution)/shard_map/ppermute | solution.py:716
  (56 other events, 422.6 us)
Sparse Core Ops, SparseCore 0:
  10.2 67.6 all-gather.2
  108.0 26.8 all-gather.4
  139.7 163.0 all-reduce.2

commit v5 on v4

--- a/solution.py
+++ b/solution.py
@@ -162,11 +162,13 @@
 
 def attend_back_body(
     here, w, gm, q01, q2k, val, lse, cc, ss, starts, normed_hbm, gain,
-    dqkv, own_hbm, other_hbm, grad_gain, ka, kb, vb, kt, do01, do2, dk, dv, d01, dq2,
-    normed, own, other, got, sent,
+    mixed_hbm, gain_b, router, own_hbm, other_hbm, table,
+    ka, kb, vb, kt, do01, do2, dk, dv, d01, dq2, normed, own, other, got, sent, dqkv, mixed,
 ):
-    load = pltpu.make_async_copy(normed_hbm, normed, got)
+    load = pltpu.make_async_copy(normed_hbm, normed, got.at[0])
+    load_mixed = pltpu.make_async_copy(mixed_hbm, mixed, got.at[1])
     load.start()
+    load_mixed.start()
     k = high_half(q2k[...].astype(f32)) * score_scale
     kb[...] = k.astype(bf16)
     k_low = pltpu.roll(k, 64, 1)
@@ -235,37 +237,58 @@
         return total
 
     total = lax.fori_loop(0, 4, finish, jnp.zeros((1, 1536), f32))
-    grad_gain[...] = total / gain[...]
+    gain_a = total / gain[...]
+    load_mixed.wait()
+    branch = jnp.concatenate([gm[b, :, 192:384] for b in range(8)], axis=0)
+    row = lax.broadcasted_iota(jnp.int32, (16, 256), 0)
+    for z in range(4):
+        cols = slice(384 * z, 384 * (z + 1))
+        first = mm(normed[:, cols].T, dqkv[...])
+        second = mm(mixed[:, cols].T, branch)
+        last = jnp.concatenate([first[:, 256:320], second], axis=1)
+        for y in range(4):
+            here_rows = slice(96 * y, 96 * (y + 1))
+            lanes = slice(384 * z + 96 * y, 384 * z + 96 * (y + 1))
+            zero = jnp.zeros((1, 32), f32)
+            gains = jnp.concatenate([gain_a[:, lanes], zero, gain_b[:, lanes], zero], axis=1)
+            small = jnp.concatenate([router[:, lanes], jnp.zeros((16, 160), f32)], axis=1)
+            extra = jnp.where(row == 0, jnp.broadcast_to(gains, (16, 256)), 0.0)
+            chunk = table.at[4 * z + y]
+            chunk[0:96, 0:256] = first[here_rows, 0:256].astype(bf16)
+            chunk[96:112, 0:256] = small.astype(bf16)
+            chunk[0:96, 256:512] = last[here_rows].astype(bf16)
+            chunk[96:112, 256:512] = extra.astype(bf16)
     for c in range(4):
         for copy in store(c):
             copy.wait()
 
 
-def attend_backward(here, gm, q01, q2k, val, lse, cc, ss, starts, normed, w, gain):
+def attend_backward(
+    here, gm, q01, q2k, val, lse, cc, ss, starts, normed, w, gain, mixed, gain_b, router
+):
     vm, hbm = pl.BlockSpec(memory_space=pltpu.VMEM), pl.BlockSpec(memory_space=pl.ANY)
     rows = pltpu.VMEM((4, 128, 1536), bf16)
+    whole = pltpu.VMEM((1024, 1536), bf16)
     shape = jax.ShapeDtypeStruct
     half = pltpu.VMEM((1024, 128), bf16)
     full = pltpu.VMEM((1024, 128), f32)
     return pl.pallas_call(
         attend_back_body,
         out_shape=(
-            shape((1024, 384), bf16),
             shape((4, 128, 1536), bf16),
             shape((4, 128, 1536), bf16),
-            shape((1, 1536), f32),
+            shape((16, 112, 512), bf16),
         ),
-        in_specs=[pl.BlockSpec(memory_space=pltpu.SMEM)] + [vm] * 9 + [hbm, vm],
-        out_specs=(vm, hbm, hbm, vm),
-        scratch_shapes=[
-            half, half, half, pltpu.VMEM((128, 1024), bf16), half, half, full, full, full, full,
-            pltpu.VMEM((1024, 1536), bf16), rows, rows,
-            pltpu.SemaphoreType.DMA, pltpu.SemaphoreType.DMA((2, 4)),
-        ],
+        in_specs=[pl.BlockSpec(memory_space=pltpu.SMEM)] + [vm] * 9 + [hbm, vm, hbm, vm, vm],
+        out_specs=(hbm, hbm, vm),
+        scratch_shapes=[half, half, half, pltpu.VMEM((128, 1024), bf16), half, half]
+        + [full, full, full, full, whole, rows, rows]
+        + [pltpu.SemaphoreType.DMA((2,)), pltpu.SemaphoreType.DMA((2, 4))]
+        + [pltpu.VMEM((1024, 384), bf16), whole],
         compiler_params=pltpu.CompilerParams(vmem_limit_bytes=56 * MIB),
         cost_estimate=pl.CostEstimate(flops=1_000_000, bytes_accessed=100_000, transcendentals=0),
         name="attend_backward",
-    )(here, w, gm, q01, q2k, val, lse, cc, ss, starts, normed, gain)
+    )(here, w, gm, q01, q2k, val, lse, cc, ss, starts, normed, gain, mixed, gain_b, router)
 
 
 def experts_body(ids, *refs):
@@ -469,42 +492,6 @@
         cost_estimate=pl.CostEstimate(flops=8_000_000_000, bytes_accessed=11_000_000, transcendentals=0),
         name="back_rows",
     )(ids, *blocks, down_w)
-
-
-def weight_body(normed, grad_qkv, mixed, branch, gain_a, gain_b, router, out):
-    first = mm(normed[...].T, grad_qkv[...])
-    cols = jnp.concatenate([branch[b, :, 192:384] for b in range(8)], axis=0)
-    second = mm(mixed[...].T, cols)
-    last = jnp.concatenate([first[:, 256:320], second], axis=1)
-    zero = jnp.zeros((1, 32), f32)
-    for y in range(4):
-        rows, lanes = slice(96 * y, 96 * (y + 1)), slice(96 * y, 96 * (y + 1))
-        gains = jnp.concatenate(
-            [gain_a[:, lanes], zero, gain_b[:, lanes], zero], axis=1
-        )
-        small = jnp.concatenate([router[:, lanes], jnp.zeros((16, 160), f32)], axis=1)
-        row = lax.broadcasted_iota(jnp.int32, (16, 256), 0)
-        extra = jnp.where(row == 0, jnp.broadcast_to(gains, (16, 256)), 0.0)
-        out[y, 0:96, 0:256] = first[rows, 0:256].astype(bf16)
-        out[y, 96:112, 0:256] = small.astype(bf16)
-        out[y, 0:96, 256:512] = last[rows].astype(bf16)
-        out[y, 96:112, 256:512] = extra.astype(bf16)
-
-
-def weight_grads(normed, grad_qkv, mixed, branch, gain_a, gain_b, router):
-    vm = pl.BlockSpec(memory_space=pltpu.VMEM)
-    slab = pl.BlockSpec((1024, 384), lambda i: (0, i))
-    flat = pl.BlockSpec((1, 384), lambda i: (0, i))
-    return pl.pallas_call(
-        weight_body,
-        grid=(4,),
-        out_shape=jax.ShapeDtypeStruct((16, 112, 512), bf16),
-        in_specs=[slab, vm, slab, vm, flat, flat, pl.BlockSpec((16, 384), lambda i: (0, i))],
-        out_specs=pl.BlockSpec((4, 112, 512), lambda i: (i, 0, 0)),
-        compiler_params=pltpu.CompilerParams(vmem_limit_bytes=56 * MIB),
-        cost_estimate=pl.CostEstimate(flops=1_000_000, bytes_accessed=100_000, transcendentals=0),
-        name="weight_grads",
-    )(normed, grad_qkv, mixed, branch, gain_a, gain_b, router)
 
 
 def sum_body(pieces, out):
@@ -843,11 +830,22 @@
         out_all, terms, out_grad, hidden, gates, narrow, own_out
     )
     grad_heads = lax.all_to_all(heads, ("x", "core"), 0, 0, tiled=True)
-    grad_qkv, own, other, grad_gain_one = attend_backward(
-        at, grad_heads, q01, q2k, val, lse, cos, sin, starts, normed, qkv_w, gain_one
-    )
-    table = weight_grads(
-        normed, grad_qkv, mixed_all, grad_heads, grad_gain_one, grad_gain_two, grad_router
+    own, other, table = attend_backward(
+        at,
+        grad_heads,
+        q01,
+        q2k,
+        val,
+        lse,
+        cos,
+        sin,
+        starts,
+        normed,
+        qkv_w,
+        gain_one,
+        mixed_all,
+        grad_gain_two,
+        grad_router,
     )
     own_out, table = tied(own_out, table)
     near_out = near_sum(own_out, other_out)

time: 323 us -> 322 us (level)
  Pallas kernels: 122 us -> 116 us
  waiting for transfers between devices: 88.8 us -> 93.6 us
    pallas_call x2 -> x1, Pallas kernels: 23.3 us -> 17.7 us  [attend_backward(): pl.pallas_call(attend_back_body, out_shape=(shape((4, 128, 1536), bf16),...]
    psum x1, waiting for transfers between devices: 3.39 us -> 7.83 us  [per_device(): sums = lax.psum((grad_w_gate, grad_w_up, grad_w_down), ('z', 'y'))]
  transfers between devices with their start and end apart: 44 -> 44, of which waited for: 19 -> 19; matrix products, arithmetic and copies ran while one was open for 5% -> 5% of each run, Pallas kernels for 35% -> 34%
where the time goes in v5:
time: 322 us; the launch traced here: 318 us
  Pallas kernels  116 us (36%)
  waiting for transfers between devices  93.6 us (29%)
  starting transfers between devices  52.9 us (16%)
  blocking collectives  17.8 us (6%)
  other arithmetic  14.7 us (5%)
  between operations  14.6 us (5%)
  local copies, waits for them, and re-layouts  8.15 us (3%)
    ppermute x18, waiting for transfers between devices, shift(): lax.ppermute(value, axis, [((i + amount) % size, i) for i in range(size)])  53.3 us
    pallas_call x1, Pallas kernels, experts(): pl.pallas_call(experts_body, grid=(2, 2), out_shape=(shape((2, 1536, 512)...  26.2 us
    pallas_call x2, Pallas kernels, by_chip(): pl.pallas_call(body, grid_spec=pltpu.PrefetchScalarGridSpec(num_scalar_pr...  20.5 us
    all_to_all x1, blocking collectives, per_device(): grad_heads = lax.all_to_all(heads, ('x', 'core'), 0, 0, tiled=True)  17.8 us
    pallas_call x1, Pallas kernels, attend_backward(): pl.pallas_call(attend_back_body, out_shape=(shape((4, 128, 1536), bf16),...  17.7 us
    pallas_call x1, Pallas kernels, attend_forward(): pl.pallas_call(attend_body, out_shape=(shape((1024, 1536), bf16), shape((...  15.5 us
    ppermute x18, starting transfers between devices, shift(): lax.ppermute(value, axis, [((i + amount) % size, i) for i in range(size)])  15.2 us
    ppermute x19, starting transfers between devices, swap(): return lax.ppermute(value, 'core', [(0, 1), (1, 0)])  15.2 us
  transfers between devices with their start and end apart: 44, of which 19 were waited for; matrix products, arithmetic and copies ran while one was open for 5% of the time, Pallas kernels for 34%

profile of v5, /device:TPU:1, one launch (start us, length us, event | category | flops | bytes accessed | tf_op | source)
XLA Modules:
  0.0 317.8 jit_solution(10051058559201048233)
XLA Ops:
  16.3 7.8 %all-to-all-start = ((bf16[16,96,384]{2,1,0:T(8,128)(2,1)}), bf16[16,96,384]{2,1,0:T(8,128)(2,1)S(1)}, u32[]{:S(2)}, u32[]{:S(2)}) async-start(bf16[16,96,384]{2,1,0:T(8,128)(2,1)} %get-tuple-element.81), calls=%async_computation | async-start | bytes 2359296 | tf_op jit(solution)/shard_map/all_to_all | solution.py:783
  25.8 7.9 %collective-permute-done.1.refs_2_ = bf16[128,1664]{1,0:T(8,128)(2,1)S(1)} collective-permute-done((bf16[128,1664]{1,0:T(8,128)(2,1)}, bf16[128,1664]{1,0:T(8,128)(2,1)S(1)}, u32[]{:S(2)}, u32[]{:S(2)}) %collective-permute-start.1) | collective-permute-done | bytes 426016 | tf_op jit(solution)/shard_map/ppermute | solution.py:703
  48.6 15.5 %attend_forward.1 = (bf16[1024,1536]{1,0:T(8,128)(2,1)}, bf16[64,1536]{1,0:T(8,128)(2,1)}, f32[1,1536]{1,0:T(1,128)}, bf16[1024,128]{1,0:T(8,128)(2,1)}, bf16[10...) custom-call(s32[8]{0:T(128)} %add.160.ids, ...), custom_call_target="tpu_custom_call" | custom-call | flops 14000000000 | bytes 12000000 | tf_op jit(solution)/shard_map/attend_forward/pallas_call | solution.py:133
  64.1 5.1 %all-to-all-start.1 = ((bf16[8,128,256]{2,1,0:T(8,128)(2,1)}), bf16[8,128,256]{2,1,0:T(8,128)(2,1)S(1)}, u32[]{:S(2)}, u32[]{:S(2)}) async-start(bf16[8,128,256]{2,1,0:T(8,128)(2,1)} %get-tuple-element.84), calls=%async_computation.1 | async-start | bytes 1048576 | tf_op jit(solution)/shard_map/all_to_all | solution.py:806
  70.2 8.5 %all-to-all-done.1.mixed = bf16[8,128,256]{2,1,0:T(8,128)(2,1)S(1)} async-done(((bf16[8,128,256]{2,1,0:T(8,128)(2,1)}), bf16[8,128,256]{2,1,0:T(8,128)(2,1)S(1)}, u32[]{:S(2)}, u32[]{:S(2)}) %all-to-all-start.1) | async-done | bytes 524320 | tf_op jit(solution)/shard_map/all_to_all | solution.py:806
  79.4 5.0 %project_out.1 = (bf16[128,1664]{1,0:T(8,128)(2,1)}, f32[128,1536]{1,0:T(8,128)}, f32[128,128]{1,0:T(8,128)}, bf16[128,1536]{1,0:T(8,128)(2,1)}) custom-call(bf16[8,128,256]{2,1,0:T(8,128)(2,1)} %copy-done.8, bf16[1536,1536]{1,0:T(8,128)(2,1)} %all-gather.3.cloned.1.call-done.w_out, bf16[128,1536]{1,0:T(8,128)(2,1)} %tokens.3, ...), custom_call_target="tpu_custom_call" | custom-call | flops 4000000000 | bytes 8000000 | tf_op jit(solution)/shard_map/project_out/pallas_call | solution.py:631
  87.5 7.7 %back_rows.1 = (bf16[1024,1536]{1,0:T(8,128)(2,1)}, bf16[1024,1024]{1,0:T(8,128)(2,1)}) custom-call(s32[8]{0:T(128)} %add.160.ids, bf16[128,1536]{1,0:T(8,128)(2,1)} %grads.1, bf16[128,1536]{1,0:T(8,128)(2,1)} %copy-done.33, bf16[128,1536]{1,0:T(8,128)(2,1)} %collective-permute-done.7.refs_2_, bf16[128,1536]{1,0:T(8,128)(2,1)} %copy-done.34, ...), custom_call_target="tpu_custom_call" | custom-call | flops 8000000000 | bytes 11000000 | tf_op jit(solution)/shard_map/back_rows/pallas_call | solution.py:483
  97.2 10.7 %collective-permute-done.16.refs_6_ = bf16[128,1664]{1,0:T(8,128)(2,1)S(1)} collective-permute-done((bf16[128,1664]{1,0:T(8,128)(2,1)}, bf16[128,1664]{1,0:T(8,128)(2,1)S(1)}, u32[]{:S(2)}, u32[]{:S(2)}) %collective-permute-start.16) | collective-permute-done | bytes 426016 | tf_op jit(solution)/shard_map/ppermute | solution.py:703
  112.6 26.2 %experts.1 = (bf16[2,1536,512]{2,1,0:T(8,128)(2,1)}, bf16[2,1536,512]{2,1,0:T(8,128)(2,1)}, bf16[2,512,1536]{2,1,0:T(8,128)(2,1)}, bf16[1024,1024]{1,0:T(8,128)(...) custom-call(s32[8]{0:T(128)} %add.160.ids, ...), custom_call_target="tpu_custom_call" | custom-call | flops 16000000000 | bytes 34000000 | tf_op jit(solution)/shard_map/experts/pallas_call | solution.py:347
  138.8 12.4 %experts_back.1 = (bf16[4,128,1664]{2,1,0:T(8,128)(2,1)}, bf16[4,128,1664]{2,1,0:T(8,128)(2,1)}) custom-call(s32[3]{0:T(128)} %pad_add_fusion.at.here, bf16[1024,1024]{1,0:T(8,128)(2,1)} %get-tuple-element.99.gg, bf16[1024,1024]{1,0:T(8,128)(2,1)} %get-tuple-element.100.gu, f32[1024,128]{1,0:T(8,128)} %get-tuple-element.101.routed, ...), custom_call_target="tpu_custom_call" | custom-call | flops 1000000 | bytes 100000 | tf_op jit(solution)/shard_map/experts_back/pallas_call | solution.py:384
  151.5 3.4 %collective-permute-done.21 = bf16[4,128,1664]{2,1,0:T(8,128)(2,1)S(1)} collective-permute-done((bf16[4,128,1664]{2,1,0:T(8,128)(2,1)}, bf16[4,128,1664]{2,1,0:T(8,128)(2,1)S(1)}, u32[]{:S(2)}, u32[]{:S(2)}) %collective-permute-start.21) | collective-permute-done | bytes 1703968 | tf_op jit(solution)/shard_map/ppermute | solution.py:707
  158.1 3.6 %all-to-all-start.2 = ((bf16[4,128,1664]{2,1,0:T(8,128)(2,1)}), bf16[4,128,1664]{2,1,0:T(8,128)(2,1)S(1)}, u32[]{:S(2)}, u32[]{:S(2)}) async-start(bf16[4,128,1664]{2,1,0:T(8,128)(2,1)} %add_convert_fusion), calls=%async_computation.2 | async-start | bytes 3407872 | tf_op jit(solution)/shard_map/all_to_all | solution.py:727
  161.7 8.1 %combine.1 = (bf16[4,128,1536]{2,1,0:T(8,128)(2,1)}, bf16[4,128,1536]{2,1,0:T(8,128)(2,1)}) custom-call(s32[3]{0:T(128)} %pad_add_fusion.at.here, bf16[1024,1024]{1,0:T(8,128)(2,1)} %get-tuple-element.105.aw, bf16[2,512,1536]{2,1,0:T(8,128)(2,1)} %down_w.1), custom_call_target="tpu_custom_call" | custom-call | flops 8000000000 | bytes 100000 | tf_op jit(solution)/shard_map/combine/pallas_call | solution.py:384
  170.1 13.4 %all-to-all-done.2.sums = bf16[4,128,1664]{2,1,0:T(8,128)(2,1)S(1)} async-done(((bf16[4,128,1664]{2,1,0:T(8,128)(2,1)}), bf16[4,128,1664]{2,1,0:T(8,128)(2,1)S(1)}, u32[]{:S(2)}, u32[]{:S(2)}) %all-to-all-start.2) | async-done | bytes 1703968 | tf_op jit(solution)/shard_map/all_to_all | solution.py:727
  184.8 6.8 %middle.1 = (f32[128,1536]{1,0:T(8,128)}, bf16[8,128,384]{2,1,0:T(8,128)(2,1)}, f32[1,1536]{1,0:T(1,128)}, f32[16,1536]{1,0:T(8,128)}) custom-call(bf16[1536,1536]{1,0:T(8,128)(2,1)} %all-gather.3.cloned.1.call-done.w_out, bf16[4,128,1664]{2,1,0:T(8,128)(2,1)} %copy-done.1, bf16[128,1536]{1,0:T(8,128)(2,1)} %grads.1, f32[128,1536]{1,0:T(8,128)} %get-tuple-element.108.hidden, ...), custom_call_target="tpu_custom_call" | custom-call | flops 1000000 | bytes 100000 | tf_op jit(solution)/shard_map/middle/pallas_call | solution.py:684
  191.5 17.8 %all_to_all.25.gm = bf16[8,128,384]{2,1,0:T(8,128)(2,1)} all-to-all(bf16[8,128,384]{2,1,0:T(8,128)(2,1)} %get-tuple-element.110), channel_id=1, replica_groups=mesh['z'=4,'y'=4,'x'=4,'core'=2] {'x','core'}, dimensions={0} | all-to-all | bytes 1572864 | tf_op jit(solution)/shard_map/all_to_all | solution.py:832
  209.3 17.7 %attend_backward.1 = (bf16[4,128,1536]{2,1,0:T(8,128)(2,1)}, bf16[4,128,1536]{2,1,0:T(8,128)(2,1)}, bf16[16,112,512]{2,1,0:T(8,128)(2,1)}) custom-call(s32[3]{0:T(128)} %pad_add_fusion.at.here, bf16[1536,384]{1,0:T(8,128)(2,1)} %bitcast.34, bf16[8,128,384]{2,1,0:T(8,128)(2,1)} %all_to_all.25.gm, bf16[1024,128]{1,0:T(8,128)(2,1)} %get-tuple-element.111.q01, ...), custom_call_target="tpu_custom_call" | custom-call | flops 1000000 | bytes 100000 | tf_op jit(solution)/shard_map/attend_backward/pallas_call | solution.py:275
  228.1 5.9 %all-to-all-start.4 = ((bf16[16,112,512]{2,1,0:T(8,128)(2,1)}), bf16[16,112,512]{2,1,0:T(8,128)(2,1)S(1)}, u32[]{:S(2)}, u32[]{:S(2)}) async-start(bf16[16,112,512]{2,1,0:T(8,128)(2,1)} %get-tuple-element.124), calls=%async_computation.4 | async-start | bytes 3670016 | tf_op jit(solution)/shard_map/all_to_all | solution.py:863
  242.5 4.2 %collective-permute-done.25 = bf16[128,1536]{1,0:T(8,128)(2,1)S(1)} collective-permute-done((bf16[128,1536]{1,0:T(8,128)(2,1)S(1)}, bf16[128,1536]{1,0:T(8,128)(2,1)S(1)}, u32[]{:S(2)}, u32[]{:S(2)}) %collective-permute-start.25) | collective-permute-done | bytes 393248 | tf_op jit(solution)/shard_map/ppermute | solution.py:703
  247.6 8.8 %collective-permute-done.24 = bf16[128,1536]{1,0:T(8,128)(2,1)S(1)} collective-permute-done((bf16[128,1536]{1,0:T(8,128)(2,1)S(1)}, bf16[128,1536]{1,0:T(8,128)(2,1)S(1)}, u32[]{:S(2)}, u32[]{:S(2)}) %collective-permute-start.24) | collective-permute-done | bytes 393248 | tf_op jit(solution)/shard_map/ppermute | solution.py:703
  257.4 6.3 %collective-permute-done.29 = bf16[128,1536]{1,0:T(8,128)(2,1)S(1)} collective-permute-done((bf16[128,1536]{1,0:T(8,128)(2,1)S(1)}, bf16[128,1536]{1,0:T(8,128)(2,1)S(1)}, u32[]{:S(2)}, u32[]{:S(2)}) %collective-permute-start.29) | collective-permute-done | bytes 393248 | tf_op jit(solution)/shard_map/ppermute | solution.py:703
  263.7 10.1 %collective-permute-done.28 = bf16[128,1536]{1,0:T(8,128)(2,1)S(1)} collective-permute-done((bf16[128,1536]{1,0:T(8,128)(2,1)S(1)}, bf16[128,1536]{1,0:T(8,128)(2,1)S(1)}, u32[]{:S(2)}, u32[]{:S(2)}) %collective-permute-start.28) | collective-permute-done | bytes 393248 | tf_op jit(solution)/shard_map/ppermute | solution.py:703
  293.8 7.8 %all-reduce.3.cloned.1.call-done = (bf16[2,1536,512]{2,1,0:T(8,128)(2,1)}, bf16[2,1536,512]{2,1,0:T(8,128)(2,1)}, bf16[2,512,1536]{2,1,0:T(8,128)(2,1)}) async-done(((bf16[2,1536,512]{2,1,0:T(8,128)(2,1)}, bf16[2,1536,512]{2,1,0:T(8,128)(2,1)}, bf16[2,512,1536]{2,1,0:T(8,128)(2,1)}), (bf16[2,1536,512]{2,1,0:T(8,128)(2,1)}, bf16[2,1536,512]{2,1,0:T(8,128)(2,1)}, ...) | async-done | bytes 9437200 | tf_op jit(solution)/shard_map/psum | solution.py:820
  301.7 9.1 %widen.1 = (f32[2,1536,512]{2,1,0:T(8,128)}, f32[2,1536,512]{2,1,0:T(8,128)}, f32[2,512,1536]{2,1,0:T(8,128)}) custom-call(bf16[2,1536,512]{2,1,0:T(8,128)(2,1)} %get-tuple-element.148.a, bf16[2,1536,512]{2,1,0:T(8,128)(2,1)} %get-tuple-element.149.b, bf16[2,512,1536]{2,1,0:T(8,128)(2,1)} %get-tuple-element.150.c), custom_call_target="tpu_custom_call" | custom-call | flops 1000000 | bytes 28000000 | tf_op jit(solution)/shard_map/widen/pallas_call | solution.py:455
  (175 shorter events, 73.6 us)
Async XLA Ops:
  7.2 71.4 %all-gather.3.cloned.1.call-start = ((), (), s32[]{:S(2)}) async-start(), calls=%async_computation.5 | async-start | bytes 5013504 | tf_op jit(solution)/shard_map/all_gather | solution.py:782
  11.2 31.0 %collective-permute-start = (bf16[128,1664]{1,0:T(8,128)(2,1)}, bf16[128,1664]{1,0:T(8,128)(2,1)S(1)}, u32[]{:S(2)}, u32[]{:S(2)}) collective-permute-start(bf16[128,1664]{1,0:T(8,128)(2,1)} %get-tuple-element.79.refs_0_), channel_id=1, source_target_pairs={{0,1},{1,0},{2,3},{3,2},{4,5},{5,4},{6,7},{7,6},{8,9},{9,8},{10,11... | collective-permute-start | bytes 1277960 | tf_op jit(solution)/shard_map/ppermute | solution.py:707
  12.6 21.1 %collective-permute-start.1 = (bf16[128,1664]{1,0:T(8,128)(2,1)}, bf16[128,1664]{1,0:T(8,128)(2,1)S(1)}, u32[]{:S(2)}, u32[]{:S(2)}) collective-permute-start(bf16[128,1664]{1,0:T(8,128)(2,1)} %get-tuple-element.79.refs_0_), channel_id=1, source_target_pairs={{2,0},{4,2},{6,4},{0,6},{3,1},{5,3},{7,5},{1,7},{10,8},{12,10},{14... | collective-permute-start | bytes 1277960 | tf_op jit(solution)/shard_map/ppermute | solution.py:703
  15.2 19.5 %collective-permute-start.3 = (bf16[128,1664]{1,0:T(8,128)(2,1)}, bf16[128,1664]{1,0:T(8,128)(2,1)S(1)}, u32[]{:S(2)}, u32[]{:S(2)}) collective-permute-start(bf16[128,1664]{1,0:T(8,128)(2,1)} %get-tuple-element.79.refs_0_), channel_id=1, source_target_pairs={{4,0},{6,2},{0,4},{2,6},{5,1},{7,3},{1,5},{3,7},{12,8},{14,10},{8,... | collective-permute-start | bytes 1277960 | tf_op jit(solution)/shard_map/ppermute | solution.py:703
  15.7 22.2 %collective-permute-start.5 = (bf16[128,1664]{1,0:T(8,128)(2,1)}, bf16[128,1664]{1,0:T(8,128)(2,1)S(1)}, u32[]{:S(2)}, u32[]{:S(2)}) collective-permute-start(bf16[128,1664]{1,0:T(8,128)(2,1)} %get-tuple-element.79.refs_0_), channel_id=1, source_target_pairs={{6,0},{0,2},{2,4},{4,6},{7,1},{1,3},{3,5},{5,7},{14,8},{8,10},{10,... | collective-permute-start | bytes 1277960 | tf_op jit(solution)/shard_map/ppermute | solution.py:703
  16.3 31.2 %all-to-all-start = ((bf16[16,96,384]{2,1,0:T(8,128)(2,1)}), bf16[16,96,384]{2,1,0:T(8,128)(2,1)S(1)}, u32[]{:S(2)}, u32[]{:S(2)}) async-start(bf16[16,96,384]{2,1,0:T(8,128)(2,1)} %get-tuple-element.81), calls=%async_computation | async-start | bytes 2359296 | tf_op jit(solution)/shard_map/all_to_all | solution.py:783
  41.9 22.2 %collective-permute-start.7 = (bf16[128,1536]{1,0:T(8,128)(2,1)S(1)}, bf16[128,1536]{1,0:T(8,128)(2,1)}, u32[]{:S(2)}, u32[]{:S(2)}) collective-permute-start(bf16[128,1536]{1,0:T(8,128)(2,1)S(1)} %copy-done.9), channel_id=1, source_target_pairs={{2,0},{4,2},{6,4},{0,6},{3,1},{5,3},{7,5},{1,7},{10,8},{12,10},{14... | collective-permute-start | bytes 1179656 | tf_op jit(solution)/shard_map/ppermute | solution.py:703
  42.2 21.9 %collective-permute-start.8 = (bf16[128,1536]{1,0:T(8,128)(2,1)S(1)}, bf16[128,1536]{1,0:T(8,128)(2,1)}, u32[]{:S(2)}, u32[]{:S(2)}) collective-permute-start(bf16[128,1536]{1,0:T(8,128)(2,1)S(1)} %copy-done.9), channel_id=1, source_target_pairs={{4,0},{6,2},{0,4},{2,6},{5,1},{7,3},{1,5},{3,7},{12,8},{14,10},{8,... | collective-permute-start | bytes 1179656 | tf_op jit(solution)/shard_map/ppermute | solution.py:703
  42.7 21.4 %collective-permute-start.9 = (bf16[128,1536]{1,0:T(8,128)(2,1)S(1)}, bf16[128,1536]{1,0:T(8,128)(2,1)}, u32[]{:S(2)}, u32[]{:S(2)}) collective-permute-start(bf16[128,1536]{1,0:T(8,128)(2,1)S(1)} %copy-done.9), channel_id=1, source_target_pairs={{6,0},{0,2},{2,4},{4,6},{7,1},{1,3},{3,5},{5,7},{14,8},{8,10},{10,... | collective-permute-start | bytes 1179656 | tf_op jit(solution)/shard_map/ppermute | solution.py:703
  69.1 140.2 %all-gather.5.cloned.1.call-start = ((), (), s32[]{:S(2)}) async-start(), calls=%async_computation.6 | async-start | bytes 3538944 | tf_op jit(solution)/shard_map/all_gather | solution.py:815
  69.1 16.2 %collective-permute-start.10 = (bf16[128,1536]{1,0:T(8,128)(2,1)S(1)}, bf16[128,1536]{1,0:T(8,128)(2,1)S(1)}, u32[]{:S(2)}, u32[]{:S(2)}) collective-permute-start(bf16[128,1536]{1,0:T(8,128)(2,1)S(1)} %copy-done.9), channel_id=1, source_target_pairs={{0,1},{1,0},{2,3},{3,2},{4,5},{5,4},{6,7},{7,6},{8,9},{9,8},{10,11... | collective-permute-start | bytes 1179656 | tf_op jit(solution)/shard_map/ppermute | solution.py:707
  69.3 17.3 %collective-permute-start.11 = (bf16[128,1536]{1,0:T(8,128)(2,1)}, bf16[128,1536]{1,0:T(8,128)(2,1)S(1)}, u32[]{:S(2)}, u32[]{:S(2)}) collective-permute-start(bf16[128,1536]{1,0:T(8,128)(2,1)} %collective-permute-done.7.refs_2_), channel_id=1, source_target_pairs={{0,1},{1,0},{2,3},{3,2},{4,5},{5,4},{6,7},{7,6},{8,9},{9,8},{10,11... | collective-permute-start | bytes 1179656 | tf_op jit(solution)/shard_map/ppermute | solution.py:707
  69.7 17.1 %collective-permute-start.12 = (bf16[128,1536]{1,0:T(8,128)(2,1)}, bf16[128,1536]{1,0:T(8,128)(2,1)S(1)}, u32[]{:S(2)}, u32[]{:S(2)}) collective-permute-start(bf16[128,1536]{1,0:T(8,128)(2,1)} %collective-permute-done.8.refs_4_), channel_id=1, source_target_pairs={{0,1},{1,0},{2,3},{3,2},{4,5},{5,4},{6,7},{7,6},{8,9},{9,8},{10,11... | collective-permute-start | bytes 1179656 | tf_op jit(solution)/shard_map/ppermute | solution.py:707
  69.8 17.0 %collective-permute-start.13 = (bf16[128,1536]{1,0:T(8,128)(2,1)}, bf16[128,1536]{1,0:T(8,128)(2,1)}, u32[]{:S(2)}, u32[]{:S(2)}) collective-permute-start(bf16[128,1536]{1,0:T(8,128)(2,1)} %collective-permute-done.9.refs_6_), channel_id=1, source_target_pairs={{0,1},{1,0},{2,3},{3,2},{4,5},{5,4},{6,7},{7,6},{8,9},{9,8},{10,11... | collective-permute-start | bytes 1179656 | tf_op jit(solution)/shard_map/ppermute | solution.py:707
  86.6 21.3 %collective-permute-start.16 = (bf16[128,1664]{1,0:T(8,128)(2,1)}, bf16[128,1664]{1,0:T(8,128)(2,1)S(1)}, u32[]{:S(2)}, u32[]{:S(2)}) collective-permute-start(bf16[128,1664]{1,0:T(8,128)(2,1)} %get-tuple-element.93.refs_0_), channel_id=1, source_target_pairs={{6,0},{0,2},{2,4},{4,6},{7,1},{1,3},{3,5},{5,7},{14,8},{8,10},{10,... | collective-permute-start | bytes 1277960 | tf_op jit(solution)/shard_map/ppermute | solution.py:703
  107.9 193.8 %all-reduce.3.cloned.1.call-start = ((), (), s32[]{:S(2)}) async-start(), calls=%async_computation.7 | async-start | bytes 18874368 | tf_op jit(solution)/shard_map/psum | solution.py:820
  158.1 25.5 %all-to-all-start.2 = ((bf16[4,128,1664]{2,1,0:T(8,128)(2,1)}), bf16[4,128,1664]{2,1,0:T(8,128)(2,1)S(1)}, u32[]{:S(2)}, u32[]{:S(2)}) async-start(bf16[4,128,1664]{2,1,0:T(8,128)(2,1)} %add_convert_fusion), calls=%async_computation.2 | async-start | bytes 3407872 | tf_op jit(solution)/shard_map/all_to_all | solution.py:727
  169.8 64.3 %collective-permute-start.22 = (bf16[4,128,1536]{2,1,0:T(8,128)(2,1)}, bf16[4,128,1536]{2,1,0:T(8,128)(2,1)}, u32[]{:S(2)}, u32[]{:S(2)}) collective-permute-start(bf16[4,128,1536]{2,1,0:T(8,128)(2,1)} %get-tuple-element.126), channel_id=1, source_target_pairs={{0,1},{1,0},{2,3},{3,2},{4,5},{5,4},{6,7},{7,6},{8,9},{9,8},{10,11... | collective-permute-start | bytes 4718600 | tf_op jit(solution)/shard_map/ppermute | solution.py:707
  228.1 47.4 %all-to-all-start.4 = ((bf16[16,112,512]{2,1,0:T(8,128)(2,1)}), bf16[16,112,512]{2,1,0:T(8,128)(2,1)S(1)}, u32[]{:S(2)}, u32[]{:S(2)}) async-start(bf16[16,112,512]{2,1,0:T(8,128)(2,1)} %get-tuple-element.124), calls=%async_computation.4 | async-start | bytes 3670016 | tf_op jit(solution)/shard_map/all_to_all | solution.py:863
  237.2 19.2 %collective-permute-start.24 = (bf16[128,1536]{1,0:T(8,128)(2,1)S(1)}, bf16[128,1536]{1,0:T(8,128)(2,1)S(1)}, u32[]{:S(2)}, u32[]{:S(2)}) collective-permute-start(bf16[128,1536]{1,0:T(8,128)(2,1)S(1)} %get-tuple-element.156), channel_id=1, source_target_pairs={{6,0},{0,2},{2,4},{4,6},{7,1},{1,3},{3,5},{5,7},{14,8},{8,10},{10,... | collective-permute-start | bytes 1179656 | tf_op jit(solution)/shard_map/ppermute | solution.py:703
  237.8 18.6 %collective-permute-start.23 = (bf16[128,1536]{1,0:T(8,128)(2,1)S(1)}, bf16[128,1536]{1,0:T(8,128)(2,1)S(1)}, u32[]{:S(2)}, u32[]{:S(2)}) collective-permute-start(bf16[128,1536]{1,0:T(8,128)(2,1)S(1)} %get-tuple-element.154), channel_id=1, source_target_pairs={{4,0},{6,2},{0,4},{2,6},{5,1},{7,3},{1,5},{3,7},{12,8},{14,10},{8,... | collective-permute-start | bytes 1179656 | tf_op jit(solution)/shard_map/ppermute | solution.py:703
  240.4 23.3 %collective-permute-start.29 = (bf16[128,1536]{1,0:T(8,128)(2,1)S(1)}, bf16[128,1536]{1,0:T(8,128)(2,1)S(1)}, u32[]{:S(2)}, u32[]{:S(2)}) collective-permute-start(bf16[128,1536]{1,0:T(8,128)(2,1)S(1)} %get-tuple-element.152), channel_id=1, source_target_pairs={{2,0},{4,2},{6,4},{0,6},{3,1},{5,3},{7,5},{1,7},{10,8},{12,10},{14... | collective-permute-start | bytes 1179656 | tf_op jit(solution)/shard_map/ppermute | solution.py:703
  242.4 31.4 %collective-permute-start.28 = (bf16[128,1536]{1,0:T(8,128)(2,1)S(1)}, bf16[128,1536]{1,0:T(8,128)(2,1)S(1)}, u32[]{:S(2)}, u32[]{:S(2)}) collective-permute-start(bf16[128,1536]{1,0:T(8,128)(2,1)S(1)} %get-tuple-element.153), channel_id=1, source_target_pairs={{6,0},{0,2},{2,4},{4,6},{7,1},{1,3},{3,5},{5,7},{14,8},{8,10},{10,... | collective-permute-start | bytes 1179656 | tf_op jit(solution)/shard_map/ppermute | solution.py:703
  246.7 27.1 %collective-permute-start.27 = (bf16[128,1536]{1,0:T(8,128)(2,1)S(1)}, bf16[128,1536]{1,0:T(8,128)(2,1)S(1)}, u32[]{:S(2)}, u32[]{:S(2)}) collective-permute-start(bf16[128,1536]{1,0:T(8,128)(2,1)S(1)} %get-tuple-element.151), channel_id=1, source_target_pairs={{4,0},{6,2},{0,4},{2,6},{5,1},{7,3},{1,5},{3,7},{12,8},{14,10},{8,... | collective-permute-start | bytes 1179656 | tf_op jit(solution)/shard_map/ppermute | solution.py:703
  (56 other events, 420.0 us)
Sparse Core Ops, SparseCore 0:
  10.2 67.6 all-gather.2
  108.0 26.8 all-gather.4
  139.8 161.8 all-reduce.2

commit v6 on v5

--- a/solution.py
+++ b/solution.py
@@ -645,12 +645,13 @@
 
 
 def middle_body(
-    w_out, sums, grads, hidden, gates, narrow, _, grad_hidden, heads, grad_gain, grad_router, gx
+    w_out, sum_a, sum_b, sum_c, sum_d, grads, hidden, gates, narrow, _,
+    grad_hidden, heads, grad_gain, grad_router, gx,
 ):
     gain = narrow[0:16, :].astype(f32)[1:2]
-    total = sums[0].astype(f32)
-    for i in range(1, 4):
-        total = total + sums[i].astype(f32)
+    total = sum_a[...].astype(f32)
+    for term in (sum_b, sum_c, sum_d):
+        total = total + term[...].astype(f32)
     value = hidden[...]
     r = lax.rsqrt(jnp.mean(value * value, axis=1, keepdims=True) + eps)
     second = (value * r * gain).astype(bf16)
@@ -689,13 +690,13 @@
             shape((1, 1536), f32),
             shape((16, 1536), f32),
         ),
-        in_specs=[vm] * 6 + [pl.BlockSpec(memory_space=pl.ANY)],
+        in_specs=[vm] * 9 + [pl.BlockSpec(memory_space=pl.ANY)],
         out_specs=(vm,) * 4,
         scratch_shapes=[pltpu.VMEM((128, 1536), f32)],
         compiler_params=pltpu.CompilerParams(vmem_limit_bytes=56 * MIB),
         cost_estimate=pl.CostEstimate(flops=1_000_000, bytes_accessed=100_000, transcendentals=0),
         name="middle",
-    )(w_out, sums, grads, hidden, gates, narrow, held)
+    )(w_out, *sums, grads, hidden, gates, narrow, held)
 
 
 def shift(value, axis, amount):
@@ -823,7 +824,7 @@
     )
     near = near_sum(own, other)
     near, weighted = tied(near, weighted)
-    terms = exchange(near)
+    terms = exchange_apart(near)
     own_out, other_out = combine(at, weighted, expert_down)
 
     grad_hidden, heads, grad_gain_two, grad_router = middle(
@@ -847,10 +848,10 @@
         grad_gain_two,
         grad_router,
     )
-    own_out, table = tied(own_out, table)
-    near_out = near_sum(own_out, other_out)
+    near_out, near_normed = near_sum(own_out, other_out), near_sum(own, other)
+    near_out, near_normed, table = tied(near_out, near_normed, table)
     output = (hidden + residual_scale * total_of(exchange_apart(near_out))).astype(bf16)
-    normed_mine = total_of(exchange_apart(near_sum(own, other)))
+    normed_mine = total_of(exchange_apart(near_normed))
     inputs = tokens.astype(f32)
     scale_one = inverse_rms(inputs)
     scaled_one = normed_mine * gain_one

time: 322 us -> 320 us (level)
  blocking collectives: 17.8 us -> 0 us
  starting transfers between devices: 52.9 us -> 61.8 us
  local copies, waits for them, and re-layouts: 8.15 us -> 12 us
    all_to_all x1 -> x0, blocking collectives: 17.8 us -> none  [per_device(): grad_heads = lax.all_to_all(heads, ('x', 'core'), 0, 0, tiled=True)]
    ppermute x19, starting transfers between devices: 15.2 us -> 19.8 us  [swap(): return lax.ppermute(value, 'core', [(0, 1), (1, 0)])]
    ppermute x18 -> x21, starting transfers between devices: 15.2 us -> 19.5 us  [shift(): lax.ppermute(value, axis, [((i + amount) % size, i) for i in range(size)])]
    ppermute x18 -> x21, waiting for transfers between devices: 53.3 us -> 56.8 us  [shift(): lax.ppermute(value, axis, [((i + amount) % size, i) for i in range(size)])]
    unnamed x73 -> x79, local copies, waits for them, and re-layouts: 7.35 us -> 7.97 us
  transfers between devices with their start and end apart: 44 -> 47, of which waited for: 19 -> 20; matrix products, arithmetic and copies ran while one was open for 5% -> 6% of each run, Pallas kernels for 34% -> 34%
where the time goes in v6:
time: 320 us; the launch traced here: 316 us
  Pallas kernels  116 us (36%)
  waiting for transfers between devices  95.8 us (30%)
  starting transfers between devices  61.8 us (19%)
  other arithmetic  15.3 us (5%)
  between operations  14.4 us (4%)
  local copies, waits for them, and re-layouts  12 us (4%)
    ppermute x21, waiting for transfers between devices, shift(): lax.ppermute(value, axis, [((i + amount) % size, i) for i in range(size)])  56.8 us
    pallas_call x1, Pallas kernels, experts(): pl.pallas_call(experts_body, grid=(2, 2), out_shape=(shape((2, 1536, 512)...  26.2 us
    pallas_call x2, Pallas kernels, by_chip(): pl.pallas_call(body, grid_spec=pltpu.PrefetchScalarGridSpec(num_scalar_pr...  20.5 us
    ppermute x19, starting transfers between devices, swap(): return lax.ppermute(value, 'core', [(0, 1), (1, 0)])  19.8 us
    ppermute x21, starting transfers between devices, shift(): lax.ppermute(value, axis, [((i + amount) % size, i) for i in range(size)])  19.5 us
    pallas_call x1, Pallas kernels, attend_backward(): pl.pallas_call(attend_back_body, out_shape=(shape((4, 128, 1536), bf16),...  17.8 us
    pallas_call x1, Pallas kernels, attend_forward(): pl.pallas_call(attend_body, out_shape=(shape((1024, 1536), bf16), shape((...  15.5 us
    all_to_all x1, waiting for transfers between devices, per_device(): grad_heads = lax.all_to_all(heads, ('x', 'core'), 0, 0, tiled=True)  12 us
  transfers between devices with their start and end apart: 47, of which 20 were waited for; matrix products, arithmetic and copies ran while one was open for 6% of the time, Pallas kernels for 34%

profile of v6, /device:TPU:1, one launch (start us, length us, event | category | flops | bytes accessed | tf_op | source)
XLA Modules:
  0.0 315.5 jit_solution(4292802716741097349)
XLA Ops:
  16.3 7.8 %all-to-all-start = ((bf16[16,96,384]{2,1,0:T(8,128)(2,1)}), bf16[16,96,384]{2,1,0:T(8,128)(2,1)S(1)}, u32[]{:S(2)}, u32[]{:S(2)}) async-start(bf16[16,96,384]{2,1,0:T(8,128)(2,1)} %get-tuple-element.82), calls=%async_computation | async-start | bytes 2359296 | tf_op jit(solution)/shard_map/all_to_all | solution.py:784
  25.9 7.8 %collective-permute-done.1.refs_2_ = bf16[128,1664]{1,0:T(8,128)(2,1)S(1)} collective-permute-done((bf16[128,1664]{1,0:T(8,128)(2,1)}, bf16[128,1664]{1,0:T(8,128)(2,1)S(1)}, u32[]{:S(2)}, u32[]{:S(2)}) %collective-permute-start.1) | collective-permute-done | bytes 426016 | tf_op jit(solution)/shard_map/ppermute | solution.py:704
  48.6 15.5 %attend_forward.1 = (bf16[1024,1536]{1,0:T(8,128)(2,1)}, bf16[64,1536]{1,0:T(8,128)(2,1)}, f32[1,1536]{1,0:T(1,128)}, bf16[1024,128]{1,0:T(8,128)(2,1)}, bf16[10...) custom-call(s32[8]{0:T(128)} %add.172.ids, ...), custom_call_target="tpu_custom_call" | custom-call | flops 14000000000 | bytes 12000000 | tf_op jit(solution)/shard_map/attend_forward/pallas_call | solution.py:133
  64.1 5.1 %all-to-all-start.1 = ((bf16[8,128,256]{2,1,0:T(8,128)(2,1)}), bf16[8,128,256]{2,1,0:T(8,128)(2,1)S(1)}, u32[]{:S(2)}, u32[]{:S(2)}) async-start(bf16[8,128,256]{2,1,0:T(8,128)(2,1)} %get-tuple-element.85), calls=%async_computation.1 | async-start | bytes 1048576 | tf_op jit(solution)/shard_map/all_to_all | solution.py:807
  70.2 8.5 %all-to-all-done.1.mixed = bf16[8,128,256]{2,1,0:T(8,128)(2,1)S(1)} async-done(((bf16[8,128,256]{2,1,0:T(8,128)(2,1)}), bf16[8,128,256]{2,1,0:T(8,128)(2,1)S(1)}, u32[]{:S(2)}, u32[]{:S(2)}) %all-to-all-start.1) | async-done | bytes 524320 | tf_op jit(solution)/shard_map/all_to_all | solution.py:807
  79.4 5.0 %project_out.1 = (bf16[128,1664]{1,0:T(8,128)(2,1)}, f32[128,1536]{1,0:T(8,128)}, f32[128,128]{1,0:T(8,128)}, bf16[128,1536]{1,0:T(8,128)(2,1)}) custom-call(bf16[8,128,256]{2,1,0:T(8,128)(2,1)} %copy-done.8, bf16[1536,1536]{1,0:T(8,128)(2,1)} %all-gather.3.cloned.1.call-done.w_out, bf16[128,1536]{1,0:T(8,128)(2,1)} %tokens.3, ...), custom_call_target="tpu_custom_call" | custom-call | flops 4000000000 | bytes 8000000 | tf_op jit(solution)/shard_map/project_out/pallas_call | solution.py:631
  87.7 7.7 %back_rows.1 = (bf16[1024,1536]{1,0:T(8,128)(2,1)}, bf16[1024,1024]{1,0:T(8,128)(2,1)}) custom-call(s32[8]{0:T(128)} %add.172.ids, bf16[128,1536]{1,0:T(8,128)(2,1)} %grads.1, bf16[128,1536]{1,0:T(8,128)(2,1)} %copy-done.36, bf16[128,1536]{1,0:T(8,128)(2,1)} %collective-permute-done.7.refs_2_, bf16[128,1536]{1,0:T(8,128)(2,1)} %copy-done.37, ...), custom_call_target="tpu_custom_call" | custom-call | flops 8000000000 | bytes 11000000 | tf_op jit(solution)/shard_map/back_rows/pallas_call | solution.py:483
  97.2 10.7 %collective-permute-done.16.refs_6_ = bf16[128,1664]{1,0:T(8,128)(2,1)S(1)} collective-permute-done((bf16[128,1664]{1,0:T(8,128)(2,1)}, bf16[128,1664]{1,0:T(8,128)(2,1)S(1)}, u32[]{:S(2)}, u32[]{:S(2)}) %collective-permute-start.16) | collective-permute-done | bytes 426016 | tf_op jit(solution)/shard_map/ppermute | solution.py:704
  112.6 26.2 %experts.1 = (bf16[2,1536,512]{2,1,0:T(8,128)(2,1)}, bf16[2,1536,512]{2,1,0:T(8,128)(2,1)}, bf16[2,512,1536]{2,1,0:T(8,128)(2,1)}, bf16[1024,1024]{1,0:T(8,128)(...) custom-call(s32[8]{0:T(128)} %add.172.ids, ...), custom_call_target="tpu_custom_call" | custom-call | flops 16000000000 | bytes 34000000 | tf_op jit(solution)/shard_map/experts/pallas_call | solution.py:347
  138.8 12.4 %experts_back.1 = (bf16[4,128,1664]{2,1,0:T(8,128)(2,1)}, bf16[4,128,1664]{2,1,0:T(8,128)(2,1)}) custom-call(s32[3]{0:T(128)} %pad_add_fusion.at.here, bf16[1024,1024]{1,0:T(8,128)(2,1)} %get-tuple-element.100.gg, bf16[1024,1024]{1,0:T(8,128)(2,1)} %get-tuple-element.101.gu, f32[1024,128]{1,0:T(8,128)} %get-tuple-element.102.routed, ...), custom_call_target="tpu_custom_call" | custom-call | flops 1000000 | bytes 100000 | tf_op jit(solution)/shard_map/experts_back/pallas_call | solution.py:384
  151.6 3.5 %collective-permute-done.21 = bf16[4,128,1664]{2,1,0:T(8,128)(2,1)S(1)} collective-permute-done((bf16[4,128,1664]{2,1,0:T(8,128)(2,1)}, bf16[4,128,1664]{2,1,0:T(8,128)(2,1)S(1)}, u32[]{:S(2)}, u32[]{:S(2)}) %collective-permute-start.21) | collective-permute-done | bytes 1703968 | tf_op jit(solution)/shard_map/ppermute | solution.py:708
  161.6 8.1 %combine.1 = (bf16[4,128,1536]{2,1,0:T(8,128)(2,1)}, bf16[4,128,1536]{2,1,0:T(8,128)(2,1)}) custom-call(s32[3]{0:T(128)} %pad_add_fusion.at.here, bf16[1024,1024]{1,0:T(8,128)(2,1)} %get-tuple-element.106.aw, bf16[2,512,1536]{2,1,0:T(8,128)(2,1)} %down_w.1), custom_call_target="tpu_custom_call" | custom-call | flops 8000000000 | bytes 100000 | tf_op jit(solution)/shard_map/combine/pallas_call | solution.py:384
  170.5 9.9 %collective-permute-done.24.sum_c = bf16[128,1664]{1,0:T(8,128)(2,1)S(1)} collective-permute-done((bf16[128,1664]{1,0:T(8,128)(2,1)S(1)}, bf16[128,1664]{1,0:T(8,128)(2,1)S(1)}, u32[]{:S(2)}, u32[]{:S(2)}) %collective-permute-start.24) | collective-permute-done | bytes 426016 | tf_op jit(solution)/shard_map/ppermute | solution.py:704
  181.2 6.7 %middle.1 = (f32[128,1536]{1,0:T(8,128)}, bf16[8,128,384]{2,1,0:T(8,128)(2,1)}, f32[1,1536]{1,0:T(1,128)}, f32[16,1536]{1,0:T(8,128)}) custom-call(bf16[1536,1536]{1,0:T(8,128)(2,1)} %all-gather.3.cloned.1.call-done.w_out, bf16[128,1664]{1,0:T(8,128)(2,1)} %get-tuple-element.156.sum_a, bf16[128,1664]{1,0:T(8,128)(2,1)} %copy-done.9, ...), custom_call_target="tpu_custom_call" | custom-call | flops 1000000 | bytes 100000 | tf_op jit(solution)/shard_map/middle/pallas_call | solution.py:685
  187.9 3.9 %all-to-all-start.2 = ((bf16[8,128,384]{2,1,0:T(8,128)(2,1)}), bf16[8,128,384]{2,1,0:T(8,128)(2,1)S(1)}, u32[]{:S(2)}, u32[]{:S(2)}) async-start(bf16[8,128,384]{2,1,0:T(8,128)(2,1)} %get-tuple-element.112), calls=%async_computation.2 | async-start | bytes 1572864 | tf_op jit(solution)/shard_map/all_to_all | solution.py:833
  192.2 12.0 %all-to-all-done.2.gm = bf16[8,128,384]{2,1,0:T(8,128)(2,1)S(1)} async-done(((bf16[8,128,384]{2,1,0:T(8,128)(2,1)}), bf16[8,128,384]{2,1,0:T(8,128)(2,1)S(1)}, u32[]{:S(2)}, u32[]{:S(2)}) %all-to-all-start.2) | async-done | bytes 786464 | tf_op jit(solution)/shard_map/all_to_all | solution.py:833
  205.0 17.8 %attend_backward.1 = (bf16[4,128,1536]{2,1,0:T(8,128)(2,1)}, bf16[4,128,1536]{2,1,0:T(8,128)(2,1)}, bf16[16,112,512]{2,1,0:T(8,128)(2,1)}) custom-call(s32[3]{0:T(128)} %pad_add_fusion.at.here, bf16[1536,384]{1,0:T(8,128)(2,1)} %bitcast.42, bf16[8,128,384]{2,1,0:T(8,128)(2,1)} %copy-done.4, bf16[1024,128]{1,0:T(8,128)(2,1)} %get-tuple-element.113.q01, ...), custom_call_target="tpu_custom_call" | custom-call | flops 1000000 | bytes 100000 | tf_op jit(solution)/shard_map/attend_backward/pallas_call | solution.py:275
  230.9 5.6 %all-to-all-start.3 = ((bf16[16,112,512]{2,1,0:T(8,128)(2,1)}), bf16[16,112,512]{2,1,0:T(8,128)(2,1)S(1)}, u32[]{:S(2)}, u32[]{:S(2)}) async-start(bf16[16,112,512]{2,1,0:T(8,128)(2,1)} %get-tuple-element.128), calls=%async_computation.3 | async-start | bytes 3670016 | tf_op jit(solution)/shard_map/all_to_all | solution.py:864
  241.8 7.2 %collective-permute-done.31 = bf16[128,1536]{1,0:T(8,128)(2,1)} collective-permute-done((bf16[128,1536]{1,0:T(8,128)(2,1)}, bf16[128,1536]{1,0:T(8,128)(2,1)}, u32[]{:S(2)}, u32[]{:S(2)}) %collective-permute-start.31) | collective-permute-done | bytes 393248 | tf_op jit(solution)/shard_map/ppermute | solution.py:704
  250.9 5.4 %collective-permute-done.29 = bf16[128,1536]{1,0:T(8,128)(2,1)S(1)} collective-permute-done((bf16[128,1536]{1,0:T(8,128)(2,1)S(1)}, bf16[128,1536]{1,0:T(8,128)(2,1)S(1)}, u32[]{:S(2)}, u32[]{:S(2)}) %collective-permute-start.29) | collective-permute-done | bytes 393248 | tf_op jit(solution)/shard_map/ppermute | solution.py:704
  256.2 10.2 %collective-permute-done.28 = bf16[128,1536]{1,0:T(8,128)(2,1)S(1)} collective-permute-done((bf16[128,1536]{1,0:T(8,128)(2,1)S(1)}, bf16[128,1536]{1,0:T(8,128)(2,1)S(1)}, u32[]{:S(2)}, u32[]{:S(2)}) %collective-permute-start.28) | collective-permute-done | bytes 393248 | tf_op jit(solution)/shard_map/ppermute | solution.py:704
  276.3 6.7 %collective-permute-start.33 = (bf16[112,512]{1,0:T(8,128)(2,1)}, bf16[112,512]{1,0:T(8,128)(2,1)S(1)}, u32[]{:S(2)}, u32[]{:S(2)}) collective-permute-start(bf16[112,512]{1,0:T(8,128)(2,1)} %sum_pieces.1.refs_0_), channel_id=1, source_target_pairs={{0,1},{1,0},{2,3},{3,2},{4,5},{5,4},{6,7},{7,6},{8,9},{9,8},{10,11... | collective-permute-start | bytes 344072 | tf_op jit(solution)/shard_map/ppermute | solution.py:708
  293.6 6.0 %all-reduce.3.cloned.1.call-done = (bf16[2,1536,512]{2,1,0:T(8,128)(2,1)}, bf16[2,1536,512]{2,1,0:T(8,128)(2,1)}, bf16[2,512,1536]{2,1,0:T(8,128)(2,1)}) async-done(((bf16[2,1536,512]{2,1,0:T(8,128)(2,1)}, bf16[2,1536,512]{2,1,0:T(8,128)(2,1)}, bf16[2,512,1536]{2,1,0:T(8,128)(2,1)}), (bf16[2,1536,512]{2,1,0:T(8,128)(2,1)}, bf16[2,1536,512]{2,1,0:T(8,128)(2,1)}, ...) | async-done | bytes 9437200 | tf_op jit(solution)/shard_map/psum | solution.py:821
  299.6 9.1 %widen.1 = (f32[2,1536,512]{2,1,0:T(8,128)}, f32[2,1536,512]{2,1,0:T(8,128)}, f32[2,512,1536]{2,1,0:T(8,128)}) custom-call(bf16[2,1536,512]{2,1,0:T(8,128)(2,1)} %get-tuple-element.150.a, bf16[2,1536,512]{2,1,0:T(8,128)(2,1)} %get-tuple-element.151.b, bf16[2,512,1536]{2,1,0:T(8,128)(2,1)} %get-tuple-element.152.c), custom_call_target="tpu_custom_call" | custom-call | flops 1000000 | bytes 28000000 | tf_op jit(solution)/shard_map/widen/pallas_call | solution.py:455
  (187 shorter events, 82.6 us)
Async XLA Ops:
  7.2 71.4 %all-gather.3.cloned.1.call-start = ((), (), s32[]{:S(2)}) async-start(), calls=%async_computation.4 | async-start | bytes 5013504 | tf_op jit(solution)/shard_map/all_gather | solution.py:783
  11.2 31.0 %collective-permute-start = (bf16[128,1664]{1,0:T(8,128)(2,1)}, bf16[128,1664]{1,0:T(8,128)(2,1)S(1)}, u32[]{:S(2)}, u32[]{:S(2)}) collective-permute-start(bf16[128,1664]{1,0:T(8,128)(2,1)} %get-tuple-element.80.refs_0_), channel_id=1, source_target_pairs={{0,1},{1,0},{2,3},{3,2},{4,5},{5,4},{6,7},{7,6},{8,9},{9,8},{10,11... | collective-permute-start | bytes 1277960 | tf_op jit(solution)/shard_map/ppermute | solution.py:708
  12.6 21.1 %collective-permute-start.1 = (bf16[128,1664]{1,0:T(8,128)(2,1)}, bf16[128,1664]{1,0:T(8,128)(2,1)S(1)}, u32[]{:S(2)}, u32[]{:S(2)}) collective-permute-start(bf16[128,1664]{1,0:T(8,128)(2,1)} %get-tuple-element.80.refs_0_), channel_id=1, source_target_pairs={{2,0},{4,2},{6,4},{0,6},{3,1},{5,3},{7,5},{1,7},{10,8},{12,10},{14... | collective-permute-start | bytes 1277960 | tf_op jit(solution)/shard_map/ppermute | solution.py:704
  15.2 19.5 %collective-permute-start.3 = (bf16[128,1664]{1,0:T(8,128)(2,1)}, bf16[128,1664]{1,0:T(8,128)(2,1)S(1)}, u32[]{:S(2)}, u32[]{:S(2)}) collective-permute-start(bf16[128,1664]{1,0:T(8,128)(2,1)} %get-tuple-element.80.refs_0_), channel_id=1, source_target_pairs={{4,0},{6,2},{0,4},{2,6},{5,1},{7,3},{1,5},{3,7},{12,8},{14,10},{8,... | collective-permute-start | bytes 1277960 | tf_op jit(solution)/shard_map/ppermute | solution.py:704
  15.7 22.2 %collective-permute-start.5 = (bf16[128,1664]{1,0:T(8,128)(2,1)}, bf16[128,1664]{1,0:T(8,128)(2,1)S(1)}, u32[]{:S(2)}, u32[]{:S(2)}) collective-permute-start(bf16[128,1664]{1,0:T(8,128)(2,1)} %get-tuple-element.80.refs_0_), channel_id=1, source_target_pairs={{6,0},{0,2},{2,4},{4,6},{7,1},{1,3},{3,5},{5,7},{14,8},{8,10},{10,... | collective-permute-start | bytes 1277960 | tf_op jit(solution)/shard_map/ppermute | solution.py:704
  16.3 31.2 %all-to-all-start = ((bf16[16,96,384]{2,1,0:T(8,128)(2,1)}), bf16[16,96,384]{2,1,0:T(8,128)(2,1)S(1)}, u32[]{:S(2)}, u32[]{:S(2)}) async-start(bf16[16,96,384]{2,1,0:T(8,128)(2,1)} %get-tuple-element.82), calls=%async_computation | async-start | bytes 2359296 | tf_op jit(solution)/shard_map/all_to_all | solution.py:784
  41.9 22.2 %collective-permute-start.7 = (bf16[128,1536]{1,0:T(8,128)(2,1)S(1)}, bf16[128,1536]{1,0:T(8,128)(2,1)}, u32[]{:S(2)}, u32[]{:S(2)}) collective-permute-start(bf16[128,1536]{1,0:T(8,128)(2,1)S(1)} %copy-done.12), channel_id=1, source_target_pairs={{2,0},{4,2},{6,4},{0,6},{3,1},{5,3},{7,5},{1,7},{10,8},{12,10},{14... | collective-permute-start | bytes 1179656 | tf_op jit(solution)/shard_map/ppermute | solution.py:704
  42.2 21.9 %collective-permute-start.8 = (bf16[128,1536]{1,0:T(8,128)(2,1)S(1)}, bf16[128,1536]{1,0:T(8,128)(2,1)}, u32[]{:S(2)}, u32[]{:S(2)}) collective-permute-start(bf16[128,1536]{1,0:T(8,128)(2,1)S(1)} %copy-done.12), channel_id=1, source_target_pairs={{4,0},{6,2},{0,4},{2,6},{5,1},{7,3},{1,5},{3,7},{12,8},{14,10},{8,... | collective-permute-start | bytes 1179656 | tf_op jit(solution)/shard_map/ppermute | solution.py:704
  42.7 21.4 %collective-permute-start.9 = (bf16[128,1536]{1,0:T(8,128)(2,1)S(1)}, bf16[128,1536]{1,0:T(8,128)(2,1)}, u32[]{:S(2)}, u32[]{:S(2)}) collective-permute-start(bf16[128,1536]{1,0:T(8,128)(2,1)S(1)} %copy-done.12), channel_id=1, source_target_pairs={{6,0},{0,2},{2,4},{4,6},{7,1},{1,3},{3,5},{5,7},{14,8},{8,10},{10,... | collective-permute-start | bytes 1179656 | tf_op jit(solution)/shard_map/ppermute | solution.py:704
  69.1 135.0 %all-gather.5.cloned.1.call-start = ((), (), s32[]{:S(2)}) async-start(), calls=%async_computation.5 | async-start | bytes 3538944 | tf_op jit(solution)/shard_map/all_gather | solution.py:816
  69.3 17.3 %collective-permute-start.11 = (bf16[128,1536]{1,0:T(8,128)(2,1)}, bf16[128,1536]{1,0:T(8,128)(2,1)S(1)}, u32[]{:S(2)}, u32[]{:S(2)}) collective-permute-start(bf16[128,1536]{1,0:T(8,128)(2,1)} %collective-permute-done.7.refs_2_), channel_id=1, source_target_pairs={{0,1},{1,0},{2,3},{3,2},{4,5},{5,4},{6,7},{7,6},{8,9},{9,8},{10,11... | collective-permute-start | bytes 1179656 | tf_op jit(solution)/shard_map/ppermute | solution.py:708
  69.7 17.3 %collective-permute-start.12 = (bf16[128,1536]{1,0:T(8,128)(2,1)}, bf16[128,1536]{1,0:T(8,128)(2,1)S(1)}, u32[]{:S(2)}, u32[]{:S(2)}) collective-permute-start(bf16[128,1536]{1,0:T(8,128)(2,1)} %collective-permute-done.8.refs_4_), channel_id=1, source_target_pairs={{0,1},{1,0},{2,3},{3,2},{4,5},{5,4},{6,7},{7,6},{8,9},{9,8},{10,11... | collective-permute-start | bytes 1179656 | tf_op jit(solution)/shard_map/ppermute | solution.py:708
  69.8 17.2 %collective-permute-start.13 = (bf16[128,1536]{1,0:T(8,128)(2,1)}, bf16[128,1536]{1,0:T(8,128)(2,1)}, u32[]{:S(2)}, u32[]{:S(2)}) collective-permute-start(bf16[128,1536]{1,0:T(8,128)(2,1)} %collective-permute-done.9.refs_6_), channel_id=1, source_target_pairs={{0,1},{1,0},{2,3},{3,2},{4,5},{5,4},{6,7},{7,6},{8,9},{9,8},{10,11... | collective-permute-start | bytes 1179656 | tf_op jit(solution)/shard_map/ppermute | solution.py:708
  86.6 21.3 %collective-permute-start.16 = (bf16[128,1664]{1,0:T(8,128)(2,1)}, bf16[128,1664]{1,0:T(8,128)(2,1)S(1)}, u32[]{:S(2)}, u32[]{:S(2)}) collective-permute-start(bf16[128,1664]{1,0:T(8,128)(2,1)} %get-tuple-element.94.refs_0_), channel_id=1, source_target_pairs={{6,0},{0,2},{2,4},{4,6},{7,1},{1,3},{3,5},{5,7},{14,8},{8,10},{10,... | collective-permute-start | bytes 1277960 | tf_op jit(solution)/shard_map/ppermute | solution.py:704
  107.9 191.7 %all-reduce.3.cloned.1.call-start = ((), (), s32[]{:S(2)}) async-start(), calls=%async_computation.6 | async-start | bytes 18874368 | tf_op jit(solution)/shard_map/psum | solution.py:821
  159.0 21.4 %collective-permute-start.24 = (bf16[128,1664]{1,0:T(8,128)(2,1)S(1)}, bf16[128,1664]{1,0:T(8,128)(2,1)S(1)}, u32[]{:S(2)}, u32[]{:S(2)}) collective-permute-start(bf16[128,1664]{1,0:T(8,128)(2,1)S(1)} %get-tuple-element.154), channel_id=1, source_target_pairs={{6,0},{0,2},{2,4},{4,6},{7,1},{1,3},{3,5},{5,7},{14,8},{8,10},{10,... | collective-permute-start | bytes 1277960 | tf_op jit(solution)/shard_map/ppermute | solution.py:704
  159.0 21.4 %collective-permute-start.25 = (bf16[128,1664]{1,0:T(8,128)(2,1)S(1)}, bf16[128,1664]{1,0:T(8,128)(2,1)S(1)}, u32[]{:S(2)}, u32[]{:S(2)}) collective-permute-start(bf16[128,1664]{1,0:T(8,128)(2,1)S(1)} %get-tuple-element.153), channel_id=1, source_target_pairs={{2,0},{4,2},{6,4},{0,6},{3,1},{5,3},{7,5},{1,7},{10,8},{12,10},{14... | collective-permute-start | bytes 1277960 | tf_op jit(solution)/shard_map/ppermute | solution.py:704
  191.8 32.2 %collective-permute-start.22 = (bf16[4,128,1536]{2,1,0:T(8,128)(2,1)}, bf16[4,128,1536]{2,1,0:T(8,128)(2,1)S(1)}, u32[]{:S(2)}, u32[]{:S(2)}) collective-permute-start(bf16[4,128,1536]{2,1,0:T(8,128)(2,1)} %get-tuple-element.108), channel_id=1, source_target_pairs={{0,1},{1,0},{2,3},{3,2},{4,5},{5,4},{6,7},{7,6},{8,9},{9,8},{10,11... | collective-permute-start | bytes 4718600 | tf_op jit(solution)/shard_map/ppermute | solution.py:708
  229.6 19.4 %collective-permute-start.31 = (bf16[128,1536]{1,0:T(8,128)(2,1)}, bf16[128,1536]{1,0:T(8,128)(2,1)}, u32[]{:S(2)}, u32[]{:S(2)}) collective-permute-start(bf16[128,1536]{1,0:T(8,128)(2,1)} %get-tuple-element.159), channel_id=1, source_target_pairs={{6,0},{0,2},{2,4},{4,6},{7,1},{1,3},{3,5},{5,7},{14,8},{8,10},{10,... | collective-permute-start | bytes 1179656 | tf_op jit(solution)/shard_map/ppermute | solution.py:704
  230.2 18.9 %collective-permute-start.30 = (bf16[128,1536]{1,0:T(8,128)(2,1)}, bf16[128,1536]{1,0:T(8,128)(2,1)}, u32[]{:S(2)}, u32[]{:S(2)}) collective-permute-start(bf16[128,1536]{1,0:T(8,128)(2,1)} %get-tuple-element.157), channel_id=1, source_target_pairs={{4,0},{6,2},{0,4},{2,6},{5,1},{7,3},{1,5},{3,7},{12,8},{14,10},{8,... | collective-permute-start | bytes 1179656 | tf_op jit(solution)/shard_map/ppermute | solution.py:704
  230.9 40.1 %all-to-all-start.3 = ((bf16[16,112,512]{2,1,0:T(8,128)(2,1)}), bf16[16,112,512]{2,1,0:T(8,128)(2,1)S(1)}, u32[]{:S(2)}, u32[]{:S(2)}) async-start(bf16[16,112,512]{2,1,0:T(8,128)(2,1)} %get-tuple-element.128), calls=%async_computation.3 | async-start | bytes 3670016 | tf_op jit(solution)/shard_map/all_to_all | solution.py:864
  237.9 18.4 %collective-permute-start.29 = (bf16[128,1536]{1,0:T(8,128)(2,1)S(1)}, bf16[128,1536]{1,0:T(8,128)(2,1)S(1)}, u32[]{:S(2)}, u32[]{:S(2)}) collective-permute-start(bf16[128,1536]{1,0:T(8,128)(2,1)S(1)} %get-tuple-element.161), channel_id=1, source_target_pairs={{2,0},{4,2},{6,4},{0,6},{3,1},{5,3},{7,5},{1,7},{10,8},{12,10},{14... | collective-permute-start | bytes 1179656 | tf_op jit(solution)/shard_map/ppermute | solution.py:704
  240.0 26.4 %collective-permute-start.28 = (bf16[128,1536]{1,0:T(8,128)(2,1)S(1)}, bf16[128,1536]{1,0:T(8,128)(2,1)S(1)}, u32[]{:S(2)}, u32[]{:S(2)}) collective-permute-start(bf16[128,1536]{1,0:T(8,128)(2,1)S(1)} %get-tuple-element.162), channel_id=1, source_target_pairs={{6,0},{0,2},{2,4},{4,6},{7,1},{1,3},{3,5},{5,7},{14,8},{8,10},{10,... | collective-permute-start | bytes 1179656 | tf_op jit(solution)/shard_map/ppermute | solution.py:704
  240.1 26.3 %collective-permute-start.27 = (bf16[128,1536]{1,0:T(8,128)(2,1)S(1)}, bf16[128,1536]{1,0:T(8,128)(2,1)S(1)}, u32[]{:S(2)}, u32[]{:S(2)}) collective-permute-start(bf16[128,1536]{1,0:T(8,128)(2,1)S(1)} %get-tuple-element.160), channel_id=1, source_target_pairs={{4,0},{6,2},{0,4},{2,6},{5,1},{7,3},{1,5},{3,7},{12,8},{14,10},{8,... | collective-permute-start | bytes 1179656 | tf_op jit(solution)/shard_map/ppermute | solution.py:704
  (62 other events, 473.2 us)
Sparse Core Ops, SparseCore 0:
  10.2 67.6 all-gather.2
  108.0 26.8 all-gather.4
  139.7 159.8 all-reduce.2
